TPU v7x, 32 devices: a whole 2x2x4 slice. The times are simulated.
32 devices in a mesh: row: 4 (over z), col: 8 (over y, x, core).
Axes of the slice: x: 2, y: 2, z: 4, core: 2. Of those that a mesh axis runs over, the one named last changes fastest.
Arguments:
- modal_velocity: bfloat16 [2048, 128], P('row'), may hold values from -6 to 6
- mode_shapes: bfloat16 [1536, 2048], P('col', 'row'), may hold values from -0.125 to 0.125
- coords: float32 [3, 1536], replicated, may hold values from 0 to 1
- panel_order: int32 [1536], replicated, may hold values from 0 to 1535, each once
- areas: float32 [1536], replicated, may hold values from 0.5 to 2
- weights: float32 [1536], replicated, may hold values from 0.25 to 4
Outputs:
- pressure: float32 [1536, 128], P(('row', 'col'))
- gradient: float32 [2048, 128], P(('row', 'col'))
Inputs may be any that keep to these rules, and one draw needn't show every extreme that they name: `panel_order`: each panel index appears exactly once.
All inputs are finite; a program needn't handle non-finite values.
Results may differ from a plain program's by a relative error of at most 0.004.
Values may be sent and summed in bfloat16 or wider, within the bound.
No kernel may reach another device: no remote copies, remote signals or barrier semaphores. Data moves between devices by JAX's collectives and lax.ppermute only.
A program may use at most 64 MiB of HBM per device.

v0:
```python
import math

import jax
import jax.numpy as jnp
from jax import lax
from jax.sharding import PartitionSpec as P

wavenumber = 20.0
smoothing = 0.02


def green_rows(target, source, source_area, norm_const):
    offset = target[0][:, None] - source[0][None, :]
    square = offset * offset
    offset = target[1][:, None] - source[1][None, :]
    square = square + offset * offset
    offset = target[2][:, None] - source[2][None, :]
    square = square + offset * offset
    distance = jnp.sqrt(square + smoothing * smoothing)
    factor = source_area[None, :] / (distance * norm_const)
    angle_value = wavenumber * distance
    return jnp.stack([factor * jnp.cos(angle_value), factor * jnp.sin(angle_value)]).astype(
        jnp.bfloat16
    )


def make_tile(target, source, source_area, norm_const):
    row_count = target.shape[1]
    if row_count <= 1024 or row_count % 512 != 0:
        return green_rows(target, source, source_area, norm_const)
    buffer = jnp.zeros((2, row_count, source.shape[1]), jnp.bfloat16)

    def fill(block_index, current):
        first_row = block_index * 512
        target_part = lax.dynamic_slice_in_dim(target, first_row, 512, 1)
        return lax.dynamic_update_slice_in_dim(
            current, green_rows(target_part, source, source_area, norm_const), first_row, 1
        )

    return lax.fori_loop(0, row_count // 512, fill, buffer)


def forward_parts(products, load_count):
    real_part = products[0, :, :load_count] - products[1, :, load_count:]
    imag_part = products[0, :, load_count:] + products[1, :, :load_count]
    return jnp.concatenate([real_part, imag_part], axis=1)


def adjoint_parts(products, load_count):
    real_part = products[0, :, :load_count] + products[1, :, load_count:]
    imag_part = products[0, :, load_count:] - products[1, :, :load_count]
    return jnp.concatenate([real_part, imag_part], axis=1)


def row_total(partial_value):
    return lax.psum(partial_value, "row").astype(jnp.bfloat16)


def local(modal_velocity, mode_shapes, coords, panel_order, areas, weights):
    row_index = lax.axis_index("row")
    col_index = lax.axis_index("col")
    src_rows = mode_shapes.shape[0]
    panels_each = src_rows // lax.axis_size("row")
    tgt_rows = panels_each * lax.axis_size("col")
    panel_total = panel_order.shape[0]
    norm_const = math.sqrt(4.0 * math.pi * panel_total)
    load_count = modal_velocity.shape[1] // 2
    target_ids = lax.dynamic_slice_in_dim(panel_order, row_index * tgt_rows, tgt_rows)
    source_ids = lax.dynamic_slice_in_dim(panel_order, col_index * src_rows, src_rows)
    target_xyz = jnp.take(coords, target_ids, axis=1)
    source_xyz = jnp.take(coords, source_ids, axis=1)
    source_area = jnp.take(areas, source_ids)
    target_weight = jnp.take(weights, target_ids)
    stored = make_tile(target_xyz, source_xyz, source_area, norm_const)

    def tile_rows():
        return stored

    surface = row_total(jnp.dot(mode_shapes, modal_velocity, preferred_element_type=jnp.float32))
    products = jnp.einsum("krm,mc->krc", tile_rows(), surface, preferred_element_type=jnp.float32)
    pressure = lax.psum_scatter(
        forward_parts(products, load_count), "col", scatter_dimension=0, tiled=True
    )
    own_weight = lax.dynamic_slice_in_dim(target_weight, col_index * panels_each, panels_each)
    source_terms = (pressure * own_weight[:, None]).astype(jnp.bfloat16)
    products = jnp.einsum(
        "krm,rc->kmc",
        tile_rows(),
        lax.all_gather(source_terms, "col", axis=0, tiled=True),
        preferred_element_type=jnp.float32,
    )
    sensitivity = adjoint_parts(products, load_count)
    summed = row_total(sensitivity)
    modal_terms = lax.dot_general(
        mode_shapes, summed, (((0,), (0,)), ((), ())), preferred_element_type=jnp.float32
    )
    gradient = lax.psum_scatter(modal_terms, "col", scatter_dimension=0, tiled=True)
    return (pressure, gradient)


def solution(mesh):
    in_specs = (P("row", None), P("col", "row"), P(), P(), P(), P())
    out_specs = (P(("row", "col"), None), P(("row", "col"), None))
    return jax.shard_map(local, mesh=mesh, in_specs=in_specs, out_specs=out_specs, check_vma=False)
```

profile of v0, /device:TPU:0, one launch (start us, length us, event | category | flops | bytes accessed | tf_op | source)
XLA Modules:
  0.0 142.7 jit_solution(8680176960087413540)
XLA Ops:
  7.2 0.0 reduce-scatter.7.cloned.1.call-start
  7.2 1.1 copy.23
  8.3 0.1 compare_select_fusion.1
  8.4 0.7 gather_fusion.2
  9.1 1.4 %gather_fusion = f32[192]{0:T(256)S(1)} fusion(f32[1536]{0:T(1024)S(1)} %copy-done.2, s32[1024]{0:T(1024)S(1)} %pad_clamp_fusion.1), kind=kCustom, calls=%fused_computation | custom fusion | bytes 2304 | tf_op jit(solution)/shard_map/jit(_take)/gather | solution.py:72
  10.6 0.1 broadcast_select_fusion.1
  10.7 0.1 select_bitcast_fusion.1
  10.8 0.3 slice_reduce_fusion.5
  11.0 0.1 compare_select_fusion
  11.1 1.1 gather_fusion.1
  12.2 2.5 %gather_fusion.3 = f32[384]{0:T(512)S(1)} fusion(f32[1536]{0:T(1024)S(1)} %copy-done.1, s32[1024]{0:T(1024)S(1)} %pad_clamp_fusion), kind=kCustom, calls=%fused_computation.3 | custom fusion | bytes 4608 | tf_op jit(solution)/shard_map/jit(_take)/gather | solution.py:73
  14.8 0.1 broadcast_select_fusion
  14.9 0.1 select_bitcast_fusion
  15.0 0.4 slice_reduce_fusion.2
  15.4 0.5 copy-done.3
  15.9 0.2 fusion.12
  16.1 22.2 %psum.14 = bf16[192,128]{1,0:T(8,128)(2,1)S(1)} all-reduce(f32[192,128]{1,0:T(8,128)S(1)} %fusion.12), channel_id=1, replica_groups=mesh['row'=4,'col'=8] {'row'}, use_global_device_ids=true, to_apply=%region_0.1 | all-reduce | flops 24576 | bytes 147456 | tf_op jit(solution)/shard_map/psum | solution.py:56
  38.4 1.5 %multiply_convert_fusion.1 = (bf16[1,384,192]{1,2,0:T(8,128)(2,1)S(1)}, bf16[1,384,192]{1,2,0:T(8,128)(2,1)S(1)}) fusion(f32[192]{0:T(256)S(1)} %get-tuple-element.14, f32[384]{0:T(512)S(1)} %get-tuple-element.11, f32[192]{0:T(256)S(1)} %get-tuple-element.15, f32[384]{0:T(512)S(1)} %get-tuple-element.12, f32[192]{0:T(256)S(1)} %get-tuple-element.13, ...), kind=kLoop, calls=%fused_computation.7 | loop fusion | flops 1179648 | bytes 302592 | tf_op jit(solution)/shard_map/convert
  39.9 0.2 fusion.1
  40.2 0.8 copy.28
  41.0 0.0 reduce-scatter.9.cloned.1.call-start
  41.1 0.1 dynamic_slice.11
  41.2 31.9 %reduce-scatter.7.cloned.1.call-done = f32[48,128]{1,0:T(8,128)} async-done(((f32[384,128]{1,0:T(8,128)}), f32[48,128]{1,0:T(8,128)}) %reduce-scatter.7.cloned.1.call-update) | async-done | bytes 24592
  73.1 0.8 multiply_convert_fusion.2
  73.9 9.2 %all_gather.3 = bf16[384,128]{1,0:T(8,128)(2,1)S(1)} all-gather(bf16[48,128]{1,0:T(8,128)(2,1)S(1)} %multiply_convert_fusion.2), channel_id=1, replica_groups=mesh['row'=4,'col'=8] {'col'}, dimensions={0}, use_global_device_ids=true | all-gather | bytes 110592 | tf_op jit(solution)/shard_map/all_gather | solution.py:89
  83.1 0.2 fusion
  83.3 0.1 fusion.3
  83.4 0.1 pad_maximum_fusion.4
  83.5 20.2 %psum.15 = bf16[192,128]{1,0:T(8,128)(2,1)S(1)} all-reduce(f32[192,128]{1,0:T(8,128)S(1)} %pad_maximum_fusion.4), channel_id=1, replica_groups=mesh['row'=4,'col'=8] {'row'}, use_global_device_ids=true, to_apply=%region_2.3 | all-reduce | flops 24576 | bytes 147456 | tf_op jit(solution)/shard_map/psum | solution.py:56
  103.7 0.2 convolution_bitcast_fusion
  103.9 0.8 copy.30
  104.8 31.1 %reduce-scatter.9.cloned.1.call-done = f32[64,128]{1,0:T(8,128)} async-done(((f32[512,128]{1,0:T(8,128)}), f32[64,128]{1,0:T(8,128)}) %reduce-scatter.9.cloned.1.call-update) | async-done | bytes 32784
  (15 shorter events, 0.1 us)
Async XLA Ops:
  7.2 8.2 %copy-start = (bf16[192,512]{1,0:T(8,128)(2,1)S(1)}, bf16[192,512]{1,0:T(8,128)(2,1)}, u32[]{:S(2)}) copy-start(bf16[192,512]{1,0:T(8,128)(2,1)} %param.7) | copy-start | bytes 589828
  7.2 65.9 %reduce-scatter.7.cloned.1.call-start = ((), (), s32[]{:S(2)}) async-start(), calls=%async_computation.2 | async-start | bytes 221184
  7.2 1.1 copy-start.4
  8.4 0.7 copy-start.2
  11.1 1.1 copy-start.1
  15.0 0.9 copy-start.3
  41.0 94.8 %reduce-scatter.9.cloned.1.call-start = ((), (), s32[]{:S(2)}) async-start(), calls=%async_computation.3 | async-start | bytes 294912
Sparse Core Ops, SparseCore 0:
  41.1 31.8 reduce-scatter.6
  104.9 30.9 reduce-scatter.8
where the time goes:
time: 143 us
  waiting for transfers between devices  63.1 us (44%)
  blocking collectives  51.6 us (36%)
  between operations  14.2 us (10%)
  local copies, waits for them, and re-layouts  9.73 us (7%)
  other arithmetic  3.15 us (2%)
    unnamed x4, waiting for transfers between devices  63.1 us
    psum x2, blocking collectives, row_total(): return lax.psum(partial_value, 'row').astype(jnp.bfloat16)  42.4 us
    all_gather x1, blocking collectives, local(): lax.all_gather(source_terms, 'col', axis=0, tiled=True)  9.17 us
    unnamed x13, local copies, waits for them, and re-layouts  3.24 us
  transfers between devices with their start and end apart: 2, of which 2 were waited for; matrix products, arithmetic and copies ran while one was open for 0% of the time, Pallas kernels for 0%

commit v1 on v0

--- a/solution.py
+++ b/solution.py
@@ -56,7 +56,7 @@
     return lax.psum(partial_value, "row").astype(jnp.bfloat16)
 
 
-def local(modal_velocity, mode_shapes, coords, panel_order, areas, weights):
+def local_general(modal_velocity, mode_shapes, coords, panel_order, areas, weights):
     row_index = lax.axis_index("row")
     col_index = lax.axis_index("col")
     src_rows = mode_shapes.shape[0]
@@ -98,7 +98,75 @@
     return (pressure, gradient)
 
 
+def swap(value, axis, mask):
+    return lax.ppermute(value, axis, [(i, i ^ mask) for i in range(lax.axis_size(axis))])
+
+
+def row_sum(value, wire):
+    sent = value.astype(wire)
+    parts = [swap(sent, "row", mask) for mask in (1, 2, 3)]
+    return value + sum(part.astype(jnp.float32) for part in parts)
+
+
+def col_sum(value):
+    core = lax.axis_index("col") % 2
+    half = value.shape[0] // 2
+    chip_value = value + swap(value, "col", 1)
+    sent = chip_value.astype(jnp.bfloat16)
+    near = lax.ppermute(sent, "col", [(i, i ^ (2 if i % 2 == 0 else 4)) for i in range(8)])
+    far = swap(lax.dynamic_slice_in_dim(sent, core * half, half), "col", 6)
+    zero = jnp.zeros_like(far)
+    far = jnp.concatenate([jnp.where(core == 0, far, zero), jnp.where(core == 0, zero, far)], 0)
+    others = near.astype(jnp.float32) + far.astype(jnp.float32)
+    return chip_value + others + swap(others, "col", 1)
+
+
+def col_scatter(value):
+    col = lax.axis_index("col")
+    core, chip = col % 2, col // 2
+    blocks = value.reshape(4, 2, value.shape[0] // 8, value.shape[1])
+    kept = lax.dynamic_index_in_dim(blocks, core, 1, False)
+    kept = kept + swap(lax.dynamic_index_in_dim(blocks, 1 - core, 1, False), "col", 1)
+    total = lax.dynamic_index_in_dim(kept, chip, 0, False)
+    for mask in (1, 2, 3):
+        total = total + swap(lax.dynamic_index_in_dim(kept, chip ^ mask, 0, False), "col", 2 * mask)
+    return total
+
+
+def local(modal_velocity, mode_shapes, coords, panel_order, areas, weights):
+    row_index = lax.axis_index("row")
+    col_index = lax.axis_index("col")
+    src_rows = mode_shapes.shape[0]
+    panels_each = src_rows // lax.axis_size("row")
+    tgt_rows = panels_each * lax.axis_size("col")
+    panel_total = panel_order.shape[0]
+    norm_const = math.sqrt(4.0 * math.pi * panel_total)
+    load_count = modal_velocity.shape[1] // 2
+    target_ids = lax.dynamic_slice_in_dim(panel_order, row_index * tgt_rows, tgt_rows)
+    source_ids = lax.dynamic_slice_in_dim(panel_order, col_index * src_rows, src_rows)
+    target_xyz = jnp.take(coords, target_ids, axis=1)
+    source_xyz = jnp.take(coords, source_ids, axis=1)
+    source_area = jnp.take(areas, source_ids)
+    target_weight = jnp.take(weights, target_ids)
+    tile = green_rows(target_xyz, source_xyz, source_area, norm_const)
+    surface = jnp.dot(mode_shapes, modal_velocity, preferred_element_type=jnp.float32)
+    surface = row_sum(surface, jnp.bfloat16).astype(jnp.bfloat16)
+    products = jnp.einsum("krm,mc->krc", tile, surface, preferred_element_type=jnp.float32)
+    pressure = col_sum(forward_parts(products, load_count))
+    source_terms = (pressure * target_weight[:, None]).astype(jnp.bfloat16)
+    products = jnp.einsum("krm,rc->kmc", tile, source_terms, preferred_element_type=jnp.float32)
+    sensitivity = adjoint_parts(products, load_count)
+    sensitivity = row_sum(sensitivity, jnp.bfloat16).astype(jnp.bfloat16)
+    modal_terms = lax.dot_general(
+        mode_shapes, sensitivity, (((0,), (0,)), ((), ())), preferred_element_type=jnp.float32
+    )
+    own = lax.dynamic_slice_in_dim(pressure, col_index * panels_each, panels_each)
+    return (own, col_scatter(modal_terms))
+
+
 def solution(mesh):
     in_specs = (P("row", None), P("col", "row"), P(), P(), P(), P())
     out_specs = (P(("row", "col"), None), P(("row", "col"), None))
-    return jax.shard_map(local, mesh=mesh, in_specs=in_specs, out_specs=out_specs, check_vma=False)
+    small = mesh.shape["row"] == 4 and mesh.shape["col"] == 8
+    body = local if small else local_general
+    return jax.shard_map(body, mesh=mesh, in_specs=in_specs, out_specs=out_specs, check_vma=False)

time: 143 us -> 48.4 us (0.34)
  blocking collectives: 51.6 us -> 0 us
  waiting for transfers between devices: 63.1 us -> 15.6 us
  starting transfers between devices: 0.08 us -> 17.2 us
  between operations: 14.2 us -> 0.94 us
    unnamed x4 -> x0, waiting for transfers between devices: 63.1 us -> none
    psum x2 -> x0, blocking collectives: 42.4 us -> none  [row_total(): return lax.psum(partial_value, 'row').astype(jnp.bfloat16)]
    ppermute x0 -> x14, starting transfers between devices: none -> 17.2 us  [the longest x13 16.6 us: swap(): lax.ppermute(value, axis, [(i, i ^ mask) for i in range(lax.axis_size(axi...]
    ppermute x0 -> x14, waiting for transfers between devices: none -> 15.6 us  [the longest x13 13.5 us: swap(): lax.ppermute(value, axis, [(i, i ^ mask) for i in range(lax.axis_size(axi...]
    all_gather x1 -> x0, blocking collectives: 9.17 us -> none  [local(): lax.all_gather(source_terms, 'col', axis=0, tiled=True)]
    unnamed x13 -> x12, local copies, waits for them, and re-layouts: 3.24 us -> 2.61 us
  transfers between devices with their start and end apart: 2 -> 14, of which waited for: 2 -> 9; matrix products, arithmetic and copies ran while one was open for 0% -> 20% of each run, Pallas kernels for 0% -> 0%
where the time goes in v1:
time: 48.4 us; the launch traced here: 48.1 us
  starting transfers between devices  17.2 us (36%)
  waiting for transfers between devices  15.6 us (32%)
  local copies, waits for them, and re-layouts  9.37 us (19%)
  other arithmetic  3.13 us (6%)
  matrix products  1.9 us (4%)
  between operations  0.94 us (2%)
    ppermute x13, starting transfers between devices, swap(): lax.ppermute(value, axis, [(i, i ^ mask) for i in range(lax.axis_size(axi...  16.6 us
    ppermute x13, waiting for transfers between devices, swap(): lax.ppermute(value, axis, [(i, i ^ mask) for i in range(lax.axis_size(axi...  13.5 us
    unnamed x12, local copies, waits for them, and re-layouts  2.61 us
    gather x1, local copies, waits for them, and re-layouts, local(): target_weight = jnp.take(weights, target_ids)  2.54 us
    ppermute x1, waiting for transfers between devices, col_sum(): lax.ppermute(sent, 'col', [(i, i ^ (2 if i % 2 == 0 else 4)) for i in ran...  2.11 us
    another operation x1, other arithmetic  1.52 us
    gather x1, local copies, waits for them, and re-layouts, local(): source_area = jnp.take(areas, source_ids)  1.44 us
    gather x1, local copies, waits for them, and re-layouts, local(): target_xyz = jnp.take(coords, target_ids, axis=1)  1.12 us
  transfers between devices with their start and end apart: 14, of which 9 were waited for; matrix products, arithmetic and copies ran while one was open for 20% of the time, Pallas kernels for 0%

profile of v1, /device:TPU:0, one launch (start us, length us, event | category | flops | bytes accessed | tf_op | source)
XLA Modules:
  0.0 48.1 jit_solution(15291955656174947783)
XLA Ops:
  0.6 0.9 %copy-done = bf16[192,512]{1,0:T(8,128)(2,1)S(1)} copy-done((bf16[192,512]{1,0:T(8,128)(2,1)S(1)}, bf16[192,512]{1,0:T(8,128)(2,1)}, u32[]{:S(2)}) %copy-start) | copy-done | bytes 196632
  1.6 1.1 %fusion.19 = (bf16[192,128]{1,0:T(8,128)(2,1)S(1)}, f32[192,128]{1,0:T(8,128)S(1)}) fusion(bf16[192,512]{1,0:T(8,128)(2,1)S(1)} %copy-done, bf16[512,128]{1,0:T(8,128)(2,1)} %param.6), kind=kOutput, calls=%fused_computation.64 | convolution fusion | flops 25190400 | bytes 475136 | tf_op jit(solution)/shard_map/dot_general | solution.py:152
  2.7 3.1 %collective-permute-start = (bf16[192,128]{1,0:T(8,128)(2,1)S(1)}, bf16[192,128]{1,0:T(8,128)(2,1)S(1)}, u32[]{:S(2)}, u32[]{:S(2)}) collective-permute-start(bf16[192,128]{1,0:T(8,128)(2,1)S(1)} %get-tuple-element.27), channel_id=1, source_target_pairs={{0,8},{8,0},{16,24},{24,16},{1,9},{9,1},{17,25},{25,17},{2,10},{10... | collective-permute-start | bytes 147464 | tf_op jit(solution)/shard_map/ppermute | solution.py:102
  5.8 2.6 %collective-permute-start.1 = (bf16[192,128]{1,0:T(8,128)(2,1)S(1)}, bf16[192,128]{1,0:T(8,128)(2,1)S(1)}, u32[]{:S(2)}, u32[]{:S(2)}) collective-permute-start(bf16[192,128]{1,0:T(8,128)(2,1)S(1)} %get-tuple-element.27), channel_id=1, source_target_pairs={{0,16},{8,24},{16,0},{24,8},{1,17},{9,25},{17,1},{25,9},{2,18},{10... | collective-permute-start | bytes 147464 | tf_op jit(solution)/shard_map/ppermute | solution.py:102
  8.4 0.7 %copy-done.4 = s32[1536]{0:T(1024)S(1)} copy-done((s32[1536]{0:T(1024)S(1)}, s32[1536]{0:T(1024)}, u32[]{:S(2)}) %copy-start.4) | copy-done | bytes 6168
  9.1 1.4 %gather_fusion = f32[192]{0:T(256)S(1)} fusion(f32[1536]{0:T(1024)S(1)} %copy-done.2, s32[1024]{0:T(1024)S(1)} %pad_clamp_fusion.1), kind=kCustom, calls=%fused_computation | custom fusion | bytes 2304 | tf_op jit(solution)/shard_map/jit(_take)/gather | solution.py:149
  10.7 0.3 copy.12
  11.0 0.7 %gather_fusion.2 = f32[192,3]{1,0:T(8,128)S(1)} fusion(f32[3,1536]{0,1:T(8,128)S(1)} %copy.12, s32[1024]{0:T(1024)S(1)} %pad_clamp_fusion.1), kind=kCustom, calls=%fused_computation.2 | custom fusion | bytes 5376 | tf_op jit(solution)/shard_map/jit(_take)/gather | solution.py:148
  12.1 1.1 %gather_fusion.1 = f32[384,3]{1,0:T(8,128)S(1)} fusion(f32[3,1536]{0,1:T(8,128)S(1)} %copy.12, s32[1024]{0:T(1024)S(1)} %pad_clamp_fusion), kind=kCustom, calls=%fused_computation.1 | custom fusion | bytes 10752 | tf_op jit(solution)/shard_map/jit(_take)/gather | solution.py:147
  13.3 2.5 %gather_fusion.3 = f32[384]{0:T(512)S(1)} fusion(f32[1536]{0:T(1024)S(1)} %copy-done.1, s32[1024]{0:T(1024)S(1)} %pad_clamp_fusion), kind=kCustom, calls=%fused_computation.3 | custom fusion | bytes 4608 | tf_op jit(solution)/shard_map/jit(_take)/gather | solution.py:150
  16.0 0.4 slice_reduce_fusion.2
  16.4 1.5 %multiply_convert_fusion.1 = (bf16[1,384,192]{1,2,0:T(8,128)(2,1)S(1)}, bf16[1,384,192]{1,2,0:T(8,128)(2,1)S(1)}) fusion(f32[192]{0:T(256)S(1)} %get-tuple-element.10, f32[384]{0:T(512)S(1)} %get-tuple-element.7, f32[192]{0:T(256)S(1)} %get-tuple-element.11, f32[384]{0:T(512)S(1)} %get-tuple-element.8, f32[192]{0:T(256)S(1)} %get-tuple-element.9, ...), kind=kLoop, calls=%fused_computation.7 | loop fusion | flops 1179648 | bytes 302592 | tf_op jit(solution)/shard_map/convert
  18.4 1.4 %collective-permute-done.3 = f32[384,128]{0,1:T(8,128)S(1)} collective-permute-done((f32[384,128]{0,1:T(8,128)S(1)}, f32[384,128]{0,1:T(8,128)S(1)}, u32[]{:S(2)}, u32[]{:S(2)}) %collective-permute-start.3) | collective-permute-done | bytes 196640 | tf_op jit(solution)/shard_map/ppermute | solution.py:102
  19.9 2.7 %collective-permute-start.5 = (bf16[192,128]{0,1:T(8,128)(2,1)S(1)}, bf16[192,128]{0,1:T(8,128)(2,1)S(1)}, u32[]{:S(2)}, u32[]{:S(2)}) collective-permute-start(bf16[192,128]{0,1:T(8,128)(2,1)S(1)} %constant_dynamic-slice_fusion.1), channel_id=1, source_target_pairs={{0,6},{1,7},{2,4},{3,5},{4,2},{5,3},{6,0},{7,1},{8,14},{9,15},{10,... | collective-permute-start | bytes 147464 | tf_op jit(solution)/shard_map/ppermute | solution.py:102
  22.6 0.5 %collective-permute-start.4 = (bf16[384,128]{0,1:T(8,128)(2,1)S(1)}, bf16[384,128]{0,1:T(8,128)(2,1)S(1)}, u32[]{:S(2)}, u32[]{:S(2)}) collective-permute-start(bf16[384,128]{0,1:T(8,128)(2,1)S(1)} %fusion.18), channel_id=1, source_target_pairs={{0,2},{1,5},{2,0},{3,7},{4,6},{5,1},{6,4},{7,3},{8,10},{9,13},{10,... | collective-permute-start | bytes 294920 | tf_op jit(solution)/shard_map/ppermute | solution.py:116
  23.2 2.0 %collective-permute-done.5 = bf16[192,128]{0,1:T(8,128)(2,1)S(1)} collective-permute-done((bf16[192,128]{0,1:T(8,128)(2,1)S(1)}, bf16[192,128]{0,1:T(8,128)(2,1)S(1)}, u32[]{:S(2)}, u32[]{:S(2)}) %collective-permute-start.5) | collective-permute-done | bytes 49184 | tf_op jit(solution)/shard_map/ppermute | solution.py:102
  25.1 2.1 %collective-permute-done.4 = bf16[384,128]{0,1:T(8,128)(2,1)S(1)} collective-permute-done((bf16[384,128]{0,1:T(8,128)(2,1)S(1)}, bf16[384,128]{0,1:T(8,128)(2,1)S(1)}, u32[]{:S(2)}, u32[]{:S(2)}) %collective-permute-start.4) | collective-permute-done | bytes 98336 | tf_op jit(solution)/shard_map/ppermute | solution.py:116
  27.4 1.4 %collective-permute-done.6 = f32[384,128]{0,1:T(8,128)S(1)} collective-permute-done((f32[384,128]{0,1:T(8,128)S(1)}, f32[384,128]{0,1:T(8,128)S(1)}, u32[]{:S(2)}, u32[]{:S(2)}) %collective-permute-start.6) | collective-permute-done | bytes 196640 | tf_op jit(solution)/shard_map/ppermute | solution.py:102
  28.9 0.3 fusion
  29.4 0.7 %collective-permute-start.7 = (bf16[192,128]{1,0:T(8,128)(2,1)S(1)}, bf16[192,128]{1,0:T(8,128)(2,1)S(1)}, u32[]{:S(2)}, u32[]{:S(2)}) collective-permute-start(bf16[192,128]{1,0:T(8,128)(2,1)S(1)} %fusion.13), channel_id=1, source_target_pairs={{0,8},{8,0},{16,24},{24,16},{1,9},{9,1},{17,25},{25,17},{2,10},{10... | collective-permute-start | bytes 147464 | tf_op jit(solution)/shard_map/ppermute | solution.py:102
  30.1 3.5 %collective-permute-start.8 = (bf16[192,128]{1,0:T(8,128)(2,1)S(1)}, bf16[192,128]{1,0:T(8,128)(2,1)S(1)}, u32[]{:S(2)}, u32[]{:S(2)}) collective-permute-start(bf16[192,128]{1,0:T(8,128)(2,1)S(1)} %fusion.13), channel_id=1, source_target_pairs={{0,16},{8,24},{16,0},{24,8},{1,17},{9,25},{17,1},{25,9},{2,18},{10... | collective-permute-start | bytes 147464 | tf_op jit(solution)/shard_map/ppermute | solution.py:102
  33.8 2.9 %collective-permute-done.8 = bf16[192,128]{1,0:T(8,128)(2,1)S(1)} collective-permute-done((bf16[192,128]{1,0:T(8,128)(2,1)S(1)}, bf16[192,128]{1,0:T(8,128)(2,1)S(1)}, u32[]{:S(2)}, u32[]{:S(2)}) %collective-permute-start.8) | collective-permute-done | bytes 49184 | tf_op jit(solution)/shard_map/ppermute | solution.py:102
  36.8 2.7 %collective-permute-done.9 = bf16[192,128]{1,0:T(8,128)(2,1)S(1)} collective-permute-done((bf16[192,128]{1,0:T(8,128)(2,1)S(1)}, bf16[192,128]{1,0:T(8,128)(2,1)S(1)}, u32[]{:S(2)}, u32[]{:S(2)}) %collective-permute-start.9) | collective-permute-done | bytes 49184 | tf_op jit(solution)/shard_map/ppermute | solution.py:102
  39.5 0.3 convolution_bitcast_fusion
  40.1 1.3 %collective-permute-done.10 = f32[4,64,128]{2,1,0:T(8,128)S(1)} collective-permute-done((f32[4,64,128]{2,1,0:T(8,128)S(1)}, f32[4,64,128]{2,1,0:T(8,128)S(1)}, u32[]{:S(2)}, u32[]{:S(2)}) %collective-permute-start.10) | collective-permute-done | bytes 131104 | tf_op jit(solution)/shard_map/ppermute | solution.py:102
  41.4 0.8 %collective-permute-start.11 = (f32[64,128]{1,0:T(8,128)S(1)}, f32[64,128]{1,0:T(8,128)S(1)}, u32[]{:S(2)}, u32[]{:S(2)}) collective-permute-start(f32[64,128]{1,0:T(8,128)S(1)} %get-tuple-element.20), channel_id=1, source_target_pairs={{0,2},{1,3},{2,0},{3,1},{4,6},{5,7},{6,4},{7,5},{8,10},{9,11},{10,... | collective-permute-start | bytes 98312 | tf_op jit(solution)/shard_map/ppermute | solution.py:102
  42.2 0.5 %collective-permute-start.12 = (f32[64,128]{1,0:T(8,128)S(1)}, f32[64,128]{1,0:T(8,128)S(1)}, u32[]{:S(2)}, u32[]{:S(2)}) collective-permute-start(f32[64,128]{1,0:T(8,128)S(1)} %get-tuple-element.22), channel_id=1, source_target_pairs={{0,4},{1,5},{2,6},{3,7},{4,0},{5,1},{6,2},{7,3},{8,12},{9,13},{10,... | collective-permute-start | bytes 98312 | tf_op jit(solution)/shard_map/ppermute | solution.py:102
  42.7 2.3 %collective-permute-start.13 = (f32[64,128]{1,0:T(8,128)S(1)}, f32[64,128]{1,0:T(8,128)S(1)}, u32[]{:S(2)}, u32[]{:S(2)}) collective-permute-start(f32[64,128]{1,0:T(8,128)S(1)} %get-tuple-element.21), channel_id=1, source_target_pairs={{0,6},{1,7},{2,4},{3,5},{4,2},{5,3},{6,0},{7,1},{8,14},{9,15},{10,... | collective-permute-start | bytes 98312 | tf_op jit(solution)/shard_map/ppermute | solution.py:102
  45.1 0.7 %copy.16 = f32[48,128]{1,0:T(8,128)} copy(f32[48,128]{0,1:T(8,128)S(1)} %constant_dynamic-slice_fusion) | data formatting | bytes 49152
  45.8 0.7 %collective-permute-done.12 = f32[64,128]{1,0:T(8,128)S(1)} collective-permute-done((f32[64,128]{1,0:T(8,128)S(1)}, f32[64,128]{1,0:T(8,128)S(1)}, u32[]{:S(2)}, u32[]{:S(2)}) %collective-permute-start.12) | collective-permute-done | bytes 32800 | tf_op jit(solution)/shard_map/ppermute | solution.py:102
  46.4 1.0 %collective-permute-done.13 = f32[64,128]{1,0:T(8,128)S(1)} collective-permute-done((f32[64,128]{1,0:T(8,128)S(1)}, f32[64,128]{1,0:T(8,128)S(1)}, u32[]{:S(2)}, u32[]{:S(2)}) %collective-permute-start.13) | collective-permute-done | bytes 32800 | tf_op jit(solution)/shard_map/ppermute | solution.py:102
  47.5 0.6 %fusion.12 = f32[64,128]{1,0:T(8,128)} fusion(f32[64,128]{1,0:T(8,128)S(1)} %collective-permute-done.13, f32[64,128]{1,0:T(8,128)S(1)} %collective-permute-done.12, f32[64,128]{1,0:T(8,128)S(1)} %collective-permute-done.11, f32[4,64,128]{2,1,0:T(8,128)S(1)} %bitcast_add_fusion, s32[]{:T(128)S(6)} %select_n.108), kind=kLoop, calls=%fused_computation.44 | loop fusion | flops 24576 | bytes 163844 | tf_op jit(solution)/shard_map/add | solution.py:132
  (42 shorter events, 2.3 us)
Async XLA Ops:
  0.6 0.9 %copy-start = (bf16[192,512]{1,0:T(8,128)(2,1)S(1)}, bf16[192,512]{1,0:T(8,128)(2,1)}, u32[]{:S(2)}) copy-start(bf16[192,512]{1,0:T(8,128)(2,1)} %param.7) | copy-start | bytes 589828
  2.7 15.3 %collective-permute-start = (bf16[192,128]{1,0:T(8,128)(2,1)S(1)}, bf16[192,128]{1,0:T(8,128)(2,1)S(1)}, u32[]{:S(2)}, u32[]{:S(2)}) collective-permute-start(bf16[192,128]{1,0:T(8,128)(2,1)S(1)} %get-tuple-element.27), channel_id=1, source_target_pairs={{0,8},{8,0},{16,24},{24,16},{1,9},{9,1},{17,25},{25,17},{2,10},{10... | collective-permute-start | bytes 147464 | tf_op jit(solution)/shard_map/ppermute | solution.py:102
  5.8 12.2 %collective-permute-start.1 = (bf16[192,128]{1,0:T(8,128)(2,1)S(1)}, bf16[192,128]{1,0:T(8,128)(2,1)S(1)}, u32[]{:S(2)}, u32[]{:S(2)}) collective-permute-start(bf16[192,128]{1,0:T(8,128)(2,1)S(1)} %get-tuple-element.27), channel_id=1, source_target_pairs={{0,16},{8,24},{16,0},{24,8},{1,17},{9,25},{17,1},{25,9},{2,18},{10... | collective-permute-start | bytes 147464 | tf_op jit(solution)/shard_map/ppermute | solution.py:102
  8.3 9.6 %collective-permute-start.2 = (bf16[192,128]{1,0:T(8,128)(2,1)S(1)}, bf16[192,128]{1,0:T(8,128)(2,1)S(1)}, u32[]{:S(2)}, u32[]{:S(2)}) collective-permute-start(bf16[192,128]{1,0:T(8,128)(2,1)S(1)} %get-tuple-element.27), channel_id=1, source_target_pairs={{0,24},{8,16},{16,8},{24,0},{1,25},{9,17},{17,9},{25,1},{2,26},{10... | collective-permute-start | bytes 147464 | tf_op jit(solution)/shard_map/ppermute | solution.py:102
  8.3 0.7 %copy-start.4 = (s32[1536]{0:T(1024)S(1)}, s32[1536]{0:T(1024)}, u32[]{:S(2)}) copy-start(s32[1536]{0:T(1024)} %param.9) | copy-start | bytes 18436
  8.3 0.8 %copy-start.2 = (f32[1536]{0:T(1024)S(1)}, f32[1536]{0:T(1024)}, u32[]{:S(2)}) copy-start(f32[1536]{0:T(1024)} %param.10) | copy-start | bytes 18436
  9.1 1.5 %copy-start.3 = (f32[3,1536]{1,0:T(4,128)S(1)}, f32[3,1536]{1,0:T(4,128)}, u32[]{:S(2)}) copy-start(f32[3,1536]{1,0:T(4,128)} %param.8) | copy-start | bytes 55300
  12.1 1.1 %copy-start.1 = (f32[1536]{0:T(1024)S(1)}, f32[1536]{0:T(1024)}, u32[]{:S(2)}) copy-start(f32[1536]{0:T(1024)} %param.11) | copy-start | bytes 18436
  18.3 1.5 %collective-permute-start.3 = (f32[384,128]{0,1:T(8,128)S(1)}, f32[384,128]{0,1:T(8,128)S(1)}, u32[]{:S(2)}, u32[]{:S(2)}) collective-permute-start(f32[384,128]{0,1:T(8,128)S(1)} %pad_maximum_fusion.1), channel_id=1, source_target_pairs={{0,1},{1,0},{2,3},{3,2},{4,5},{5,4},{6,7},{7,6},{8,9},{9,8},{10,11... | collective-permute-start | bytes 589832 | tf_op jit(solution)/shard_map/ppermute | solution.py:102
  19.9 5.2 %collective-permute-start.5 = (bf16[192,128]{0,1:T(8,128)(2,1)S(1)}, bf16[192,128]{0,1:T(8,128)(2,1)S(1)}, u32[]{:S(2)}, u32[]{:S(2)}) collective-permute-start(bf16[192,128]{0,1:T(8,128)(2,1)S(1)} %constant_dynamic-slice_fusion.1), channel_id=1, source_target_pairs={{0,6},{1,7},{2,4},{3,5},{4,2},{5,3},{6,0},{7,1},{8,14},{9,15},{10,... | collective-permute-start | bytes 147464 | tf_op jit(solution)/shard_map/ppermute | solution.py:102
  22.6 4.6 %collective-permute-start.4 = (bf16[384,128]{0,1:T(8,128)(2,1)S(1)}, bf16[384,128]{0,1:T(8,128)(2,1)S(1)}, u32[]{:S(2)}, u32[]{:S(2)}) collective-permute-start(bf16[384,128]{0,1:T(8,128)(2,1)S(1)} %fusion.18), channel_id=1, source_target_pairs={{0,2},{1,5},{2,0},{3,7},{4,6},{5,1},{6,4},{7,3},{8,10},{9,13},{10,... | collective-permute-start | bytes 294920 | tf_op jit(solution)/shard_map/ppermute | solution.py:116
  27.3 1.5 %collective-permute-start.6 = (f32[384,128]{0,1:T(8,128)S(1)}, f32[384,128]{0,1:T(8,128)S(1)}, u32[]{:S(2)}, u32[]{:S(2)}) collective-permute-start(f32[384,128]{0,1:T(8,128)S(1)} %convert_add_fusion), channel_id=1, source_target_pairs={{0,1},{1,0},{2,3},{3,2},{4,5},{5,4},{6,7},{7,6},{8,9},{9,8},{10,11... | collective-permute-start | bytes 589832 | tf_op jit(solution)/shard_map/ppermute | solution.py:102
  29.4 4.5 %collective-permute-start.7 = (bf16[192,128]{1,0:T(8,128)(2,1)S(1)}, bf16[192,128]{1,0:T(8,128)(2,1)S(1)}, u32[]{:S(2)}, u32[]{:S(2)}) collective-permute-start(bf16[192,128]{1,0:T(8,128)(2,1)S(1)} %fusion.13), channel_id=1, source_target_pairs={{0,8},{8,0},{16,24},{24,16},{1,9},{9,1},{17,25},{25,17},{2,10},{10... | collective-permute-start | bytes 147464 | tf_op jit(solution)/shard_map/ppermute | solution.py:102
  30.1 6.6 %collective-permute-start.8 = (bf16[192,128]{1,0:T(8,128)(2,1)S(1)}, bf16[192,128]{1,0:T(8,128)(2,1)S(1)}, u32[]{:S(2)}, u32[]{:S(2)}) collective-permute-start(bf16[192,128]{1,0:T(8,128)(2,1)S(1)} %fusion.13), channel_id=1, source_target_pairs={{0,16},{8,24},{16,0},{24,8},{1,17},{9,25},{17,1},{25,9},{2,18},{10... | collective-permute-start | bytes 147464 | tf_op jit(solution)/shard_map/ppermute | solution.py:102
  33.6 5.9 %collective-permute-start.9 = (bf16[192,128]{1,0:T(8,128)(2,1)S(1)}, bf16[192,128]{1,0:T(8,128)(2,1)S(1)}, u32[]{:S(2)}, u32[]{:S(2)}) collective-permute-start(bf16[192,128]{1,0:T(8,128)(2,1)S(1)} %fusion.13), channel_id=1, source_target_pairs={{0,24},{8,16},{16,8},{24,0},{1,25},{9,17},{17,9},{25,1},{2,26},{10... | collective-permute-start | bytes 147464 | tf_op jit(solution)/shard_map/ppermute | solution.py:102
  40.0 1.4 %collective-permute-start.10 = (f32[4,64,128]{2,1,0:T(8,128)S(1)}, f32[4,64,128]{2,1,0:T(8,128)S(1)}, u32[]{:S(2)}, u32[]{:S(2)}) collective-permute-start(f32[4,64,128]{2,1,0:T(8,128)S(1)} %dynamic-slice_bitcast_fusion), channel_id=1, source_target_pairs={{0,1},{1,0},{2,3},{3,2},{4,5},{5,4},{6,7},{7,6},{8,9},{9,8},{10,11... | collective-permute-start | bytes 393224 | tf_op jit(solution)/shard_map/ppermute | solution.py:102
  41.4 4.3 %collective-permute-start.11 = (f32[64,128]{1,0:T(8,128)S(1)}, f32[64,128]{1,0:T(8,128)S(1)}, u32[]{:S(2)}, u32[]{:S(2)}) collective-permute-start(f32[64,128]{1,0:T(8,128)S(1)} %get-tuple-element.20), channel_id=1, source_target_pairs={{0,2},{1,3},{2,0},{3,1},{4,6},{5,7},{6,4},{7,5},{8,10},{9,11},{10,... | collective-permute-start | bytes 98312 | tf_op jit(solution)/shard_map/ppermute | solution.py:102
  42.2 4.3 %collective-permute-start.12 = (f32[64,128]{1,0:T(8,128)S(1)}, f32[64,128]{1,0:T(8,128)S(1)}, u32[]{:S(2)}, u32[]{:S(2)}) collective-permute-start(f32[64,128]{1,0:T(8,128)S(1)} %get-tuple-element.22), channel_id=1, source_target_pairs={{0,4},{1,5},{2,6},{3,7},{4,0},{5,1},{6,2},{7,3},{8,12},{9,13},{10,... | collective-permute-start | bytes 98312 | tf_op jit(solution)/shard_map/ppermute | solution.py:102
  42.7 4.8 %collective-permute-start.13 = (f32[64,128]{1,0:T(8,128)S(1)}, f32[64,128]{1,0:T(8,128)S(1)}, u32[]{:S(2)}, u32[]{:S(2)}) collective-permute-start(f32[64,128]{1,0:T(8,128)S(1)} %get-tuple-element.21), channel_id=1, source_target_pairs={{0,6},{1,7},{2,4},{3,5},{4,2},{5,3},{6,0},{7,1},{8,14},{9,15},{10,... | collective-permute-start | bytes 98312 | tf_op jit(solution)/shard_map/ppermute | solution.py:102

commit v2 on v0

--- a/solution.py
+++ b/solution.py
@@ -1,8 +1,11 @@
+import functools
 import math
 
 import jax
 import jax.numpy as jnp
 from jax import lax
+from jax.experimental import pallas as pl
+from jax.experimental.pallas import tpu as pltpu
 from jax.sharding import PartitionSpec as P
 
 wavenumber = 20.0
@@ -56,7 +59,7 @@
     return lax.psum(partial_value, "row").astype(jnp.bfloat16)
 
 
-def local(modal_velocity, mode_shapes, coords, panel_order, areas, weights):
+def local_general(modal_velocity, mode_shapes, coords, panel_order, areas, weights):
     row_index = lax.axis_index("row")
     col_index = lax.axis_index("col")
     src_rows = mode_shapes.shape[0]
@@ -98,7 +101,305 @@
     return (pressure, gradient)
 
 
+sine_terms = (4.442879676818848, -7.307816505432129, 3.5977742671966553, -0.7911993861198425)
+cosine_terms = (
+    -1.4142135381698608,
+    6.978850841522217,
+    -5.739460468292236,
+    1.883557915687561,
+    -0.3106880187988281,
+)
+lanes = 128
+piece = 64
+step_rows = 64
+whole = pl.BlockSpec(memory_space=pltpu.VMEM)
+
+
+def call(kernel, outs, scratch, *args, cost=None):
+    shapes = tuple(jax.ShapeDtypeStruct(shape, dtype) for shape, dtype in outs)
+    return pl.pallas_call(
+        kernel,
+        out_shape=shapes,
+        in_specs=[whole] * len(args),
+        out_specs=(whole,) * len(shapes),
+        scratch_shapes=[pltpu.VMEM(shape, dtype) for shape, dtype in scratch],
+        compiler_params=pltpu.CompilerParams(vmem_limit_bytes=16 * 2**20),
+        cost_estimate=cost,
+    )(*args)
+
+
+def horner(terms, value):
+    total = jnp.float32(terms[-1])
+    for term in terms[-2::-1]:
+        total = jnp.float32(term) + value * total
+    return total
+
+
+def place_panels(order_ref, coords_ref, areas_ref, weights_ref, ids, along, down):
+    col = lax.axis_index("col")
+    chip, core = col // 2, col % 2
+    ids[...] = jnp.zeros(ids.shape, jnp.int32)
+    count = order_ref.shape[0]
+    for at in range(count):
+        side, slot, part = at // (count // 2), at % (count // 2) // 3, at % 3
+        panel_block = 2 * (chip ^ slot) + (core if side == 0 else 1 - core)
+        first = at % 2 * piece
+        ids[at // 2 : at // 2 + 1, first : first + piece] = order_ref[pl.ds(3 * panel_block + part, 1), :]
+    for group in range(ids.shape[0] // 8):
+        index = ids[8 * group : 8 * group + 8, :]
+        high, low = index // lanes, index % lanes
+        values = [jnp.zeros(index.shape, jnp.float32) for _ in range(5)]
+        for part in range(areas_ref.shape[0]):
+            chosen = high == part
+            rows = [coords_ref[axis : axis + 1, part * lanes : (part + 1) * lanes] for axis in range(3)]
+            rows += [areas_ref[part : part + 1, :], weights_ref[part : part + 1, :]]
+            for which, row in enumerate(rows):
+                found = jnp.take_along_axis(
+                    jnp.broadcast_to(row, index.shape), low, axis=1, mode="promise_in_bounds"
+                )
+                values[which] = jnp.where(chosen, found, values[which])
+        for which, value in enumerate(values):
+            along[which, 8 * group : 8 * group + 8, :] = value
+            down[which, :, 8 * group : 8 * group + 8] = jnp.transpose(value)
+
+
+def spread_rows(down_ref, rows_ref, first):
+    for which in range(4):
+        for block in range(rows_ref.shape[1] // lanes):
+            at = first + block
+            rows_ref[which, block * lanes : (block + 1) * lanes, :] = jnp.broadcast_to(
+                down_ref[which, :, at : at + 1], (lanes, lanes)
+            )
+
+
+def fill_green(rows_ref, columns_ref, norm_const, forward_ref, first_row, row_count, adjoint_ref=None):
+    def fill(step, carry):
+        rows = pl.ds(pl.multiple_of(first_row + step * step_rows, step_rows), step_rows)
+        row_x, row_y, row_z, row_area = [rows_ref[which, rows, :] for which in range(4)]
+        row_area = row_area * jnp.float32(1.0 / norm_const)
+        for part in range(columns_ref.shape[2] // lanes):
+            columns = slice(part * lanes, (part + 1) * lanes)
+            col_x, col_y, col_z, col_area = [
+                jnp.concatenate([columns_ref[which, :, columns]] * (step_rows // 8), 0) for which in range(4)
+            ]
+            offset_x, offset_y, offset_z = row_x - col_x, row_y - col_y, row_z - col_z
+            square = offset_x * offset_x + offset_y * offset_y
+            square = square + (offset_z * offset_z + jnp.float32(smoothing * smoothing))
+            inverse = lax.rsqrt(square)
+            turns = (square * jnp.float32(wavenumber / (2.0 * math.pi))) * inverse
+            half_turn = turns - jnp.floor(turns) - jnp.float32(0.5)
+            power = half_turn * half_turn
+            sine = half_turn * horner(sine_terms, power)
+            real_part = sine * sine - jnp.float32(1.0)
+            imag_part = sine * horner(cosine_terms, power)
+            factor = inverse * col_area
+            forward_ref[0, rows, columns] = (real_part * factor).astype(jnp.bfloat16)
+            forward_ref[1, rows, columns] = (imag_part * factor).astype(jnp.bfloat16)
+            if adjoint_ref is not None:
+                factor = inverse * row_area
+                adjoint_ref[0, rows, columns] = (real_part * factor).astype(jnp.bfloat16)
+                adjoint_ref[1, rows, columns] = (imag_part * factor).astype(jnp.bfloat16)
+        return carry
+
+    lax.fori_loop(0, row_count // step_rows, fill, 0)
+
+
+def first_tile_kernel(
+    norm_const,
+    order_ref,
+    coords_ref,
+    areas_ref,
+    weights_ref,
+    forward_ref,
+    adjoint_ref,
+    columns_ref,
+    down_ref,
+    ids,
+    along,
+    rows_ref,
+):
+    place_panels(order_ref, coords_ref, areas_ref, weights_ref, ids, along, down_ref)
+    for which in range(4):
+        scale = jnp.float32(1.0 / norm_const if which == 3 else 1.0)
+        for block in range(columns_ref.shape[2] // lanes):
+            columns_ref[which, :, block * lanes : (block + 1) * lanes] = jnp.broadcast_to(
+                along[which, block : block + 1, :] * scale, (8, lanes)
+            )
+    spread_rows(down_ref, rows_ref, 0)
+    own = adjoint_ref.shape[1]
+    fill_green(rows_ref, columns_ref, norm_const, forward_ref, 0, own, adjoint_ref)
+    fill_green(rows_ref, columns_ref, norm_const, forward_ref, own, forward_ref.shape[1] - own)
+
+
+def next_tile_kernel(norm_const, first, columns_ref, down_ref, forward_ref, rows_ref):
+    spread_rows(down_ref, rows_ref, first // lanes)
+    fill_green(rows_ref, columns_ref, norm_const, forward_ref, 0, forward_ref.shape[1])
+
+
+def first_tile(coords, panel_order, areas, weights, norm_const, row_count, own_rows):
+    panels = panel_order.shape[0]
+    blocks = -(-panels // (8 * lanes)) * 8
+    wide = (panels // lanes, lanes)
+    return call(
+        functools.partial(first_tile_kernel, norm_const),
+        (
+            ((2, row_count, panels), jnp.bfloat16),
+            ((2, own_rows, panels), jnp.bfloat16),
+            ((4, 8, panels), jnp.float32),
+            ((5, lanes, blocks), jnp.float32),
+        ),
+        (
+            ((blocks, lanes), jnp.int32),
+            ((5, blocks, lanes), jnp.float32),
+            ((4, row_count, lanes), jnp.float32),
+        ),
+        panel_order.reshape(panels // piece, piece),
+        coords,
+        areas.reshape(wide),
+        weights.reshape(wide),
+        cost=pl.CostEstimate(flops=10**9, bytes_accessed=2**22, transcendentals=10**6),
+    )
+
+
+def next_tile(columns, down, norm_const, first, row_count):
+    panels = columns.shape[2]
+    return call(
+        functools.partial(next_tile_kernel, norm_const, first),
+        (((2, row_count, panels), jnp.bfloat16),),
+        (((4, row_count, lanes), jnp.float32),),
+        columns,
+        down,
+        cost=pl.CostEstimate(flops=10**9, bytes_accessed=2**22, transcendentals=10**6),
+    )[0]
+
+
+def turned(value, sign):
+    load_count = value.shape[1] // 2
+    first, last = value[:, :load_count], value[:, load_count:]
+    if sign > 0:
+        return jnp.concatenate([-last, first], 1)
+    return jnp.concatenate([last, -first], 1)
+
+
+def tile_dot(tile_ref, columns, value, sign):
+    return jnp.dot(
+        tile_ref[0, :, columns], value, preferred_element_type=jnp.float32
+    ) + jnp.dot(tile_ref[1, :, columns], turned(value, sign), preferred_element_type=jnp.float32)
+
+
+def pressure_kernel(side, *refs):
+    tile_refs, value_ref, out_ref = refs[:2], refs[2], refs[-1]
+    half = value_ref.shape[0]
+    columns = slice(side * half, (side + 1) * half)
+    first = 0
+    for tile_ref in tile_refs:
+        rows = slice(first, first + tile_ref.shape[1])
+        term = tile_dot(tile_ref, columns, value_ref[...], 1)
+        out_ref[rows, :] = term if side == 0 else refs[3][rows, :] + term
+        first = rows.stop
+
+
+def sources(pressure_ref, down_ref, side):
+    count = pressure_ref.shape[0] // lanes
+    parts = []
+    for block in range(count):
+        at = side * count + block
+        weight = down_ref[4, :, at : at + 1]
+        parts.append((pressure_ref[block * lanes : (block + 1) * lanes, :] * weight).astype(jnp.bfloat16))
+    return jnp.concatenate(parts, 0)
+
+
+def own_adjoint_kernel(tile_ref, pressure_ref, down_ref, out_ref):
+    half = pressure_ref.shape[0]
+    out_ref[...] = tile_dot(tile_ref, slice(0, half), sources(pressure_ref, down_ref, 0), -1)
+
+
+def modal_kernel(tile_ref, own_ref, other_ref, down_ref, term_ref, modes_ref, modal_ref, pressure_ref):
+    row = lax.axis_index("row")
+    col = lax.axis_index("col")
+    chip, core = col // 2, col % 2
+    half = own_ref.shape[0]
+    sensitivity = term_ref[...] + tile_dot(
+        tile_ref, slice(half, 2 * half), sources(other_ref, down_ref, 1), -1
+    )
+    modal_ref[...] = lax.dot_general(
+        modes_ref[...],
+        sensitivity.astype(jnp.bfloat16),
+        (((0,), (0,)), ((), ())),
+        preferred_element_type=jnp.float32,
+    )
+    each = pressure_ref.shape[0]
+    per_block = modes_ref.shape[0] // each
+    panel_block = 2 * row + col // per_block
+    first = (panel_block // 2 ^ chip) * modes_ref.shape[0] + col % per_block * each
+    rows = pl.ds(pl.multiple_of(first, each), each)
+    pressure_ref[...] = jnp.where(panel_block % 2 == core, own_ref[rows, :], other_ref[rows, :])
+
+
+def swap(value, axis, mask):
+    return lax.ppermute(value, axis, [(i, i ^ mask) for i in range(lax.axis_size(axis))])
+
+
+def col_scatter(value):
+    col = lax.axis_index("col")
+    core, chip = col % 2, col // 2
+    blocks = value.reshape(4, 2, value.shape[0] // 8, value.shape[1])
+    kept = lax.dynamic_index_in_dim(blocks, core, 1, False)
+    kept = kept + swap(lax.dynamic_index_in_dim(blocks, 1 - core, 1, False), "col", 1)
+    total = lax.dynamic_index_in_dim(kept, chip, 0, False)
+    for mask in (1, 2, 3):
+        total = total + swap(lax.dynamic_index_in_dim(kept, chip ^ mask, 0, False), "col", 2 * mask)
+    return total
+
+
+def local(modal_velocity, mode_shapes, coords, panel_order, areas, weights):
+    panels = panel_order.shape[0]
+    norm_const = math.sqrt(4.0 * math.pi * panels)
+    own_rows, load_columns = mode_shapes.shape[0], modal_velocity.shape[1]
+    half = 4 * own_rows
+    part_rows = half // 2
+    terms = jnp.dot(mode_shapes, modal_velocity, preferred_element_type=jnp.float32)
+    sent = terms.astype(jnp.bfloat16)
+    received = [swap(sent, "row", mask) for mask in (1, 2, 3)]
+    tiles = first_tile(coords, panel_order, areas, weights, norm_const, part_rows, own_rows)
+    received, tiles = lax.optimization_barrier((received, tiles))
+    tile, own_tile, columns, down = tiles
+    surface = (terms + sum(part.astype(jnp.float32) for part in received)).astype(jnp.bfloat16)
+    received = [swap(surface, "col", 2 * mask) for mask in (1, 2, 3)]
+    last_tile = next_tile(columns, down, norm_const, part_rows, half - part_rows)
+    received, last_tile = lax.optimization_barrier((received, last_tile))
+    own = jnp.concatenate([surface] + received, 0)
+    other = swap(own, "col", 1)
+    out = (((half, load_columns), jnp.float32),)
+    term = call(functools.partial(pressure_kernel, 0), out, (), tile, last_tile, own)[0]
+    pressure = call(functools.partial(pressure_kernel, 1), out, (), tile, last_tile, other, term)[0]
+    other = swap(pressure, "col", 1)
+    out = (((own_rows, load_columns), jnp.float32),)
+    term = call(own_adjoint_kernel, out, (), own_tile, pressure, down)[0]
+    modal_terms, own_pressure = call(
+        modal_kernel,
+        (
+            ((mode_shapes.shape[1], load_columns), jnp.float32),
+            ((own_rows // lax.axis_size("row"), load_columns), jnp.float32),
+        ),
+        (),
+        own_tile,
+        pressure,
+        other,
+        down,
+        term,
+        mode_shapes,
+    )
+    return (own_pressure, col_scatter(modal_terms))
+
+
 def solution(mesh):
     in_specs = (P("row", None), P("col", "row"), P(), P(), P(), P())
     out_specs = (P(("row", "col"), None), P(("row", "col"), None))
-    return jax.shard_map(local, mesh=mesh, in_specs=in_specs, out_specs=out_specs, check_vma=False)
+
+    def body(*args):
+        panels = args[3].shape[0]
+        small = mesh.shape["row"] == 4 and mesh.shape["col"] == 8 and panels == 1536
+        return (local if small else local_general)(*args)
+
+    return jax.shard_map(body, mesh=mesh, in_specs=in_specs, out_specs=out_specs, check_vma=False)

time: 143 us -> 37.8 us (0.26)
  waiting for transfers between devices: 63.1 us -> 6.48 us
  blocking collectives: 51.6 us -> 0 us
  between operations: 14.2 us -> 0.77 us
  starting transfers between devices: 0.08 us -> 13.3 us
  Pallas kernels: 0 us -> 11.3 us
  local copies, waits for them, and re-layouts: 9.73 us -> 3.83 us
  other arithmetic: 3.15 us -> 0.69 us
    unnamed x4 -> x0, waiting for transfers between devices: 63.1 us -> none
    psum x2 -> x0, blocking collectives: 42.4 us -> none  [row_total(): return lax.psum(partial_value, 'row').astype(jnp.bfloat16)]
    ppermute x0 -> x12, starting transfers between devices: none -> 13.3 us  [swap(): lax.ppermute(value, axis, [(i, i ^ mask) for i in range(lax.axis_size(axi...]
    pallas_call x0 -> x6, Pallas kernels: none -> 11.3 us  [call(): pl.pallas_call(kernel, out_shape=shapes, in_specs=[whole] * len(args), ou...]
    all_gather x1 -> x0, blocking collectives: 9.17 us -> none  [local(): lax.all_gather(source_terms, 'col', axis=0, tiled=True)]
    ppermute x0 -> x12, waiting for transfers between devices: none -> 6.48 us  [swap(): lax.ppermute(value, axis, [(i, i ^ mask) for i in range(lax.axis_size(axi...]
    gather x4 -> x0, local copies, waits for them, and re-layouts: 5.79 us -> none  [the longest x1 2.54 us: local(): target_weight = jnp.take(weights, target_ids)]
    another operation x1 -> x0, other arithmetic: 1.52 us -> none
  transfers between devices with their start and end apart: 2 -> 12, of which waited for: 2 -> 7; matrix products, arithmetic and copies ran while one was open for 0% -> 2% of each run, Pallas kernels for 0% -> 24%
where the time goes in v2:
time: 37.8 us; the launch traced here: 37.5 us
  starting transfers between devices  13.3 us (35%)
  Pallas kernels  11.3 us (30%)
  waiting for transfers between devices  6.48 us (17%)
  local copies, waits for them, and re-layouts  3.83 us (10%)
  matrix products  1.12 us (3%)
  between operations  0.77 us (2%)
  other arithmetic  0.69 us (2%)
    ppermute x12, starting transfers between devices, swap(): lax.ppermute(value, axis, [(i, i ^ mask) for i in range(lax.axis_size(axi...  13.3 us
    pallas_call x6, Pallas kernels, call(): pl.pallas_call(kernel, out_shape=shapes, in_specs=[whole] * len(args), ou...  11.3 us
    ppermute x12, waiting for transfers between devices, swap(): lax.ppermute(value, axis, [(i, i ^ mask) for i in range(lax.axis_size(axi...  6.48 us
    unnamed x10, local copies, waits for them, and re-layouts  3.04 us
    dot_general x1, matrix products, local(): jnp.dot(mode_shapes, modal_velocity, preferred_element_type=jnp.float32)  1.12 us
    reshape x1, local copies, waits for them, and re-layouts, first_tile(): panel_order.reshape(panels // piece, piece)  0.77 us
  transfers between devices with their start and end apart: 12, of which 7 were waited for; matrix products, arithmetic and copies ran while one was open for 2% of the time, Pallas kernels for 24%

profile of v2, /device:TPU:0, one launch (start us, length us, event | category | flops | bytes accessed | tf_op | source)
XLA Modules:
  0.0 37.5 jit_solution(16966637022148936772)
XLA Ops:
  0.6 0.0 copy-start
  0.6 0.9 %copy-done = bf16[512,128]{1,0:T(8,128)(2,1)S(1)} copy-done((bf16[512,128]{1,0:T(8,128)(2,1)S(1)}, bf16[512,128]{1,0:T(8,128)(2,1)}, u32[]{:S(2)}) %copy-start) | copy-done | bytes 131096
  1.5 1.1 %fusion.2 = (bf16[192,128]{1,0:T(8,128)(2,1)S(1)}, f32[192,128]{1,0:T(8,128)S(1)}) fusion(bf16[192,512]{1,0:T(8,128)(2,1)} %modes_ref.1, bf16[512,128]{1,0:T(8,128)(2,1)S(1)} %copy-done), kind=kOutput, calls=%fused_computation.10 | convolution fusion | flops 25190400 | bytes 475136 | tf_op jit(solution)/shard_map/dot_general | solution.py:361
  2.7 3.1 %collective-permute-start = (bf16[192,128]{1,0:T(8,128)(2,1)S(1)}, bf16[192,128]{1,0:T(8,128)(2,1)S(1)}, u32[]{:S(2)}, u32[]{:S(2)}) collective-permute-start(bf16[192,128]{1,0:T(8,128)(2,1)S(1)} %get-tuple-element.39), channel_id=1, source_target_pairs={{0,8},{8,0},{16,24},{24,16},{1,9},{9,1},{17,25},{25,17},{2,10},{10... | collective-permute-start | bytes 147464 | tf_op jit(solution)/shard_map/ppermute | solution.py:340
  5.8 2.6 %collective-permute-start.1 = (bf16[192,128]{1,0:T(8,128)(2,1)S(1)}, bf16[192,128]{1,0:T(8,128)(2,1)S(1)}, u32[]{:S(2)}, u32[]{:S(2)}) collective-permute-start(bf16[192,128]{1,0:T(8,128)(2,1)S(1)} %get-tuple-element.39), channel_id=1, source_target_pairs={{0,16},{8,24},{16,0},{24,8},{1,17},{9,25},{17,1},{25,9},{2,18},{10... | collective-permute-start | bytes 147464 | tf_op jit(solution)/shard_map/ppermute | solution.py:340
  8.3 0.8 %reshape.16.order_ref = s32[24,64]{1,0:T(8,128)S(1)} reshape(s32[1536]{0:T(1024)} %param.9) | data formatting | bytes 12288 | tf_op jit(solution)/shard_map/reshape | solution.py:256
  9.1 0.7 %copy-done.2 = f32[3,1536]{1,0:T(4,128)S(1)} copy-done((f32[3,1536]{1,0:T(4,128)S(1)}, f32[3,1536]{1,0:T(4,128)}, u32[]{:S(2)}) %copy-start.2) | copy-done | bytes 18456
  9.9 0.7 %copy-done.3 = f32[1536]{0:T(1024)S(1)} copy-done((f32[1536]{0:T(1024)S(1)}, f32[1536]{0:T(1024)}, u32[]{:S(2)}) %copy-start.3) | copy-done | bytes 6168
  10.6 0.7 %copy-done.4 = f32[1536]{0:T(1024)S(1)} copy-done((f32[1536]{0:T(1024)S(1)}, f32[1536]{0:T(1024)}, u32[]{:S(2)}) %copy-start.4) | copy-done | bytes 6168
  11.2 4.3 %shard_map.77 = (bf16[2,384,1536]{2,1,0:T(8,128)(2,1)S(1)}, bf16[2,192,1536]{2,1,0:T(8,128)(2,1)S(1)}, f32[4,8,1536]{2,1,0:T(8,128)S(1)}, f32[5,128,16]{2,1,0:T(8,128)S(1)}) custom-call(s32[24,64]{1,0:T(8,128)S(1)} %reshape.16.order_ref, f32[3,1536]{1,0:T(4,128)S(1)} %copy-done.2, f32[12,128]{1,0:T(8,128)S(1)} %bitcast.23, f32[12,128]{1,0:T(8,128)S(1)} %bitcast.24), custom_call_target="tpu_custom_call" | custom-call | flops 1000000000 | bytes 4194304 | tf_op jit(solution)/shard_map/pallas_call | solution.py:120
  15.6 1.8 %collective-permute-start.3 = (bf16[192,128]{1,0:T(8,128)(2,1)S(1)}, bf16[192,128]{1,0:T(8,128)(2,1)S(1)}, u32[]{:S(2)}, u32[]{:S(2)}) collective-permute-start(bf16[192,128]{1,0:T(8,128)(2,1)S(1)} %add_convert_fusion), channel_id=1, source_target_pairs={{0,2},{1,3},{2,0},{3,1},{4,6},{5,7},{6,4},{7,5},{8,10},{9,11},{10,... | collective-permute-start | bytes 147464 | tf_op jit(solution)/shard_map/ppermute | solution.py:340
  17.4 1.5 %collective-permute-start.4 = (bf16[192,128]{1,0:T(8,128)(2,1)S(1)}, bf16[192,128]{1,0:T(8,128)(2,1)S(1)}, u32[]{:S(2)}, u32[]{:S(2)}) collective-permute-start(bf16[192,128]{1,0:T(8,128)(2,1)S(1)} %add_convert_fusion), channel_id=1, source_target_pairs={{0,4},{1,5},{2,6},{3,7},{4,0},{5,1},{6,2},{7,3},{8,12},{9,13},{10,... | collective-permute-start | bytes 147464 | tf_op jit(solution)/shard_map/ppermute | solution.py:340
  18.9 0.3 collective-permute-start.5
  19.2 3.4 %shard_map.78.refs_1_ = bf16[2,384,1536]{2,1,0:T(8,128)(2,1)S(1)} custom-call(f32[4,8,1536]{2,1,0:T(8,128)S(1)} %get-tuple-element.28.columns_ref, f32[5,128,16]{2,1,0:T(8,128)S(1)} %get-tuple-element.29.down_ref), custom_call_target="tpu_custom_call" | custom-call | flops 1000000000 | bytes 4194304 | tf_op jit(solution)/shard_map/pallas_call | solution.py:120
  22.6 1.3 %collective-permute-done.5 = bf16[192,128]{1,0:T(8,128)(2,1)S(1)} collective-permute-done((bf16[192,128]{1,0:T(8,128)(2,1)S(1)}, bf16[192,128]{1,0:T(8,128)(2,1)S(1)}, u32[]{:S(2)}, u32[]{:S(2)}) %collective-permute-start.5) | collective-permute-done | bytes 49184 | tf_op jit(solution)/shard_map/ppermute | solution.py:340
  23.9 0.1 collective-permute-start.6
  24.0 0.9 %shard_map.79.refs_3_ = f32[768,128]{1,0:T(8,128)S(1)} custom-call(bf16[2,384,1536]{2,1,0:T(8,128)(2,1)S(1)} %get-tuple-element.24.refs_0_, bf16[2,384,1536]{2,1,0:T(8,128)(2,1)S(1)} %shard_map.78.refs_1_, bf16[768,128]{1,0:T(8,128)(2,1)S(1)} %pad_maximum_fusion.refs_2_), custom_call_target="tpu_custom_call" | custom-call | tf_op jit(solution)/shard_map/pallas_call | solution.py:120
  24.9 0.5 %collective-permute-done.6.refs_2_ = bf16[768,128]{1,0:T(8,128)(2,1)S(1)} collective-permute-done((bf16[768,128]{1,0:T(8,128)(2,1)S(1)}, bf16[768,128]{1,0:T(8,128)(2,1)S(1)}, u32[]{:S(2)}, u32[]{:S(2)}) %collective-permute-start.6) | collective-permute-done | bytes 196640 | tf_op jit(solution)/shard_map/ppermute | solution.py:340
  25.4 0.9 %shard_map.80.pressure_ref.own_ref = f32[768,128]{1,0:T(8,128)S(1)} custom-call(bf16[2,384,1536]{2,1,0:T(8,128)(2,1)S(1)} %get-tuple-element.24.refs_0_, bf16[2,384,1536]{2,1,0:T(8,128)(2,1)S(1)} %shard_map.78.refs_1_, bf16[768,128]{1,0:T(8,128)(2,1)S(1)} %collective-permute-done.6.refs_2_, f32[768,128]{1,0:T(8,128)S(1)} %shard_map.79.refs_3_), custom_call_target="tpu_custom_call" | custom-call | tf_op jit(solution)/shard_map/pallas_call | solution.py:120
  26.3 0.2 collective-permute-start.7
  26.5 0.6 %shard_map.81.term_ref = f32[192,128]{1,0:T(8,128)S(1)} custom-call(bf16[2,192,1536]{2,1,0:T(8,128)(2,1)S(1)} %get-tuple-element.23.tile_ref, f32[768,128]{1,0:T(8,128)S(1)} %shard_map.80.pressure_ref.own_ref, f32[5,128,16]{2,1,0:T(8,128)S(1)} %get-tuple-element.29.down_ref), custom_call_target="tpu_custom_call" | custom-call | tf_op jit(solution)/shard_map/pallas_call | solution.py:120
  27.1 1.0 %collective-permute-done.7.other_ref = f32[768,128]{1,0:T(8,128)S(1)} collective-permute-done((f32[768,128]{1,0:T(8,128)S(1)}, f32[768,128]{1,0:T(8,128)S(1)}, u32[]{:S(2)}, u32[]{:S(2)}) %collective-permute-start.7) | collective-permute-done | bytes 393248 | tf_op jit(solution)/shard_map/ppermute | solution.py:340
  28.1 1.3 %shard_map.82 = (f32[512,128]{1,0:T(8,128)S(1)}, f32[48,128]{1,0:T(8,128)}) custom-call(bf16[2,192,1536]{2,1,0:T(8,128)(2,1)S(1)} %get-tuple-element.23.tile_ref, f32[768,128]{1,0:T(8,128)S(1)} %shard_map.80.pressure_ref.own_ref, f32[768,128]{1,0:T(8,128)S(1)} %collective-permute-done.7.other_ref, f32[5,128,16]{2,1,0:T(8,128)S(1)} %get-tuple-element.29.down_ref, ...), custom_call_target="tpu_custom_call" | custom-call | tf_op jit(solution)/shard_map/pallas_call | solution.py:120
  29.4 0.2 collective-permute-start.8
  29.6 1.2 %collective-permute-done.8 = f32[4,64,128]{2,1,0:T(8,128)S(1)} collective-permute-done((f32[4,64,128]{2,1,0:T(8,128)S(1)}, f32[4,64,128]{2,1,0:T(8,128)S(1)}, u32[]{:S(2)}, u32[]{:S(2)}) %collective-permute-start.8) | collective-permute-done | bytes 131104 | tf_op jit(solution)/shard_map/ppermute | solution.py:340
  30.9 1.4 %collective-permute-start.11 = (f32[64,128]{1,0:T(8,128)S(1)}, f32[64,128]{1,0:T(8,128)S(1)}, u32[]{:S(2)}, u32[]{:S(2)}) collective-permute-start(f32[64,128]{1,0:T(8,128)S(1)} %get-tuple-element.37), channel_id=1, source_target_pairs={{0,6},{1,7},{2,4},{3,5},{4,2},{5,3},{6,0},{7,1},{8,14},{9,15},{10,... | collective-permute-start | bytes 98312 | tf_op jit(solution)/shard_map/ppermute | solution.py:340
  32.3 0.7 %collective-permute-start.10 = (f32[64,128]{1,0:T(8,128)S(1)}, f32[64,128]{1,0:T(8,128)S(1)}, u32[]{:S(2)}, u32[]{:S(2)}) collective-permute-start(f32[64,128]{1,0:T(8,128)S(1)} %get-tuple-element.38), channel_id=1, source_target_pairs={{0,4},{1,5},{2,6},{3,7},{4,0},{5,1},{6,2},{7,3},{8,12},{9,13},{10,... | collective-permute-start | bytes 98312 | tf_op jit(solution)/shard_map/ppermute | solution.py:340
  32.9 1.5 %collective-permute-start.9 = (f32[64,128]{1,0:T(8,128)S(1)}, f32[64,128]{1,0:T(8,128)S(1)}, u32[]{:S(2)}, u32[]{:S(2)}) collective-permute-start(f32[64,128]{1,0:T(8,128)S(1)} %get-tuple-element.36), channel_id=1, source_target_pairs={{0,2},{1,3},{2,0},{3,1},{4,6},{5,7},{6,4},{7,5},{8,10},{9,11},{10,... | collective-permute-start | bytes 98312 | tf_op jit(solution)/shard_map/ppermute | solution.py:340
  34.4 1.3 %collective-permute-done.11 = f32[64,128]{1,0:T(8,128)S(1)} collective-permute-done((f32[64,128]{1,0:T(8,128)S(1)}, f32[64,128]{1,0:T(8,128)S(1)}, u32[]{:S(2)}, u32[]{:S(2)}) %collective-permute-start.11) | collective-permute-done | bytes 32800 | tf_op jit(solution)/shard_map/ppermute | solution.py:340
  35.7 0.4 %collective-permute-done.10 = f32[64,128]{1,0:T(8,128)S(1)} collective-permute-done((f32[64,128]{1,0:T(8,128)S(1)}, f32[64,128]{1,0:T(8,128)S(1)}, u32[]{:S(2)}, u32[]{:S(2)}) %collective-permute-start.10) | collective-permute-done | bytes 32800 | tf_op jit(solution)/shard_map/ppermute | solution.py:340
  36.2 0.7 %collective-permute-done.9 = f32[64,128]{1,0:T(8,128)S(1)} collective-permute-done((f32[64,128]{1,0:T(8,128)S(1)}, f32[64,128]{1,0:T(8,128)S(1)}, u32[]{:S(2)}, u32[]{:S(2)}) %collective-permute-start.9) | collective-permute-done | bytes 32800 | tf_op jit(solution)/shard_map/ppermute | solution.py:340
  36.8 0.6 %fusion.1 = f32[64,128]{1,0:T(8,128)} fusion(f32[64,128]{1,0:T(8,128)S(1)} %collective-permute-done.11, f32[64,128]{1,0:T(8,128)S(1)} %collective-permute-done.10, f32[64,128]{1,0:T(8,128)S(1)} %collective-permute-done.9, f32[4,64,128]{2,1,0:T(8,128)S(1)} %bitcast_add_fusion, s32[]{:T(128)S(6)} %select_n.35), kind=kLoop, calls=%fused_computation.6 | loop fusion | flops 24576 | bytes 163844 | tf_op jit(solution)/shard_map/add | solution.py:351
  (16 shorter events, 0.1 us)
Async XLA Ops:
  0.6 0.9 %copy-start = (bf16[512,128]{1,0:T(8,128)(2,1)S(1)}, bf16[512,128]{1,0:T(8,128)(2,1)}, u32[]{:S(2)}) copy-start(bf16[512,128]{1,0:T(8,128)(2,1)} %param.6) | copy-start | bytes 393220
  2.7 12.9 %collective-permute-start = (bf16[192,128]{1,0:T(8,128)(2,1)S(1)}, bf16[192,128]{1,0:T(8,128)(2,1)S(1)}, u32[]{:S(2)}, u32[]{:S(2)}) collective-permute-start(bf16[192,128]{1,0:T(8,128)(2,1)S(1)} %get-tuple-element.39), channel_id=1, source_target_pairs={{0,8},{8,0},{16,24},{24,16},{1,9},{9,1},{17,25},{25,17},{2,10},{10... | collective-permute-start | bytes 147464 | tf_op jit(solution)/shard_map/ppermute | solution.py:340
  5.8 9.8 %collective-permute-start.1 = (bf16[192,128]{1,0:T(8,128)(2,1)S(1)}, bf16[192,128]{1,0:T(8,128)(2,1)S(1)}, u32[]{:S(2)}, u32[]{:S(2)}) collective-permute-start(bf16[192,128]{1,0:T(8,128)(2,1)S(1)} %get-tuple-element.39), channel_id=1, source_target_pairs={{0,16},{8,24},{16,0},{24,8},{1,17},{9,25},{17,1},{25,9},{2,18},{10... | collective-permute-start | bytes 147464 | tf_op jit(solution)/shard_map/ppermute | solution.py:340
  8.3 7.2 %collective-permute-start.2 = (bf16[192,128]{1,0:T(8,128)(2,1)S(1)}, bf16[192,128]{1,0:T(8,128)(2,1)S(1)}, u32[]{:S(2)}, u32[]{:S(2)}) collective-permute-start(bf16[192,128]{1,0:T(8,128)(2,1)S(1)} %get-tuple-element.39), channel_id=1, source_target_pairs={{0,24},{8,16},{16,8},{24,0},{1,25},{9,17},{17,9},{25,1},{2,26},{10... | collective-permute-start | bytes 147464 | tf_op jit(solution)/shard_map/ppermute | solution.py:340
  9.1 0.7 %copy-start.2 = (f32[3,1536]{1,0:T(4,128)S(1)}, f32[3,1536]{1,0:T(4,128)}, u32[]{:S(2)}) copy-start(f32[3,1536]{1,0:T(4,128)} %coords_ref.1) | copy-start | bytes 55300
  9.9 0.7 %copy-start.3 = (f32[1536]{0:T(1024)S(1)}, f32[1536]{0:T(1024)}, u32[]{:S(2)}) copy-start(f32[1536]{0:T(1024)} %param.10) | copy-start | bytes 18436
  10.6 0.7 %copy-start.4 = (f32[1536]{0:T(1024)S(1)}, f32[1536]{0:T(1024)}, u32[]{:S(2)}) copy-start(f32[1536]{0:T(1024)} %param.11) | copy-start | bytes 18436
  15.6 6.9 %collective-permute-start.3 = (bf16[192,128]{1,0:T(8,128)(2,1)S(1)}, bf16[192,128]{1,0:T(8,128)(2,1)S(1)}, u32[]{:S(2)}, u32[]{:S(2)}) collective-permute-start(bf16[192,128]{1,0:T(8,128)(2,1)S(1)} %add_convert_fusion), channel_id=1, source_target_pairs={{0,2},{1,3},{2,0},{3,1},{4,6},{5,7},{6,4},{7,5},{8,10},{9,11},{10,... | collective-permute-start | bytes 147464 | tf_op jit(solution)/shard_map/ppermute | solution.py:340
  17.4 5.2 %collective-permute-start.4 = (bf16[192,128]{1,0:T(8,128)(2,1)S(1)}, bf16[192,128]{1,0:T(8,128)(2,1)S(1)}, u32[]{:S(2)}, u32[]{:S(2)}) collective-permute-start(bf16[192,128]{1,0:T(8,128)(2,1)S(1)} %add_convert_fusion), channel_id=1, source_target_pairs={{0,4},{1,5},{2,6},{3,7},{4,0},{5,1},{6,2},{7,3},{8,12},{9,13},{10,... | collective-permute-start | bytes 147464 | tf_op jit(solution)/shard_map/ppermute | solution.py:340
  18.9 5.0 %collective-permute-start.5 = (bf16[192,128]{1,0:T(8,128)(2,1)S(1)}, bf16[192,128]{1,0:T(8,128)(2,1)S(1)}, u32[]{:S(2)}, u32[]{:S(2)}) collective-permute-start(bf16[192,128]{1,0:T(8,128)(2,1)S(1)} %add_convert_fusion), channel_id=1, source_target_pairs={{0,6},{1,7},{2,4},{3,5},{4,2},{5,3},{6,0},{7,1},{8,14},{9,15},{10,... | collective-permute-start | bytes 147464 | tf_op jit(solution)/shard_map/ppermute | solution.py:340
  23.9 1.5 %collective-permute-start.6 = (bf16[768,128]{1,0:T(8,128)(2,1)S(1)}, bf16[768,128]{1,0:T(8,128)(2,1)S(1)}, u32[]{:S(2)}, u32[]{:S(2)}) collective-permute-start(bf16[768,128]{1,0:T(8,128)(2,1)S(1)} %pad_maximum_fusion.refs_2_), channel_id=1, source_target_pairs={{0,1},{1,0},{2,3},{3,2},{4,5},{5,4},{6,7},{7,6},{8,9},{9,8},{10,11... | collective-permute-start | bytes 589832 | tf_op jit(solution)/shard_map/ppermute | solution.py:340
  24.9 3.2 %copy-start.1 = (bf16[192,512]{1,0:T(8,128)(2,1)S(1)}, bf16[192,512]{1,0:T(8,128)(2,1)}, u32[]{:S(2)}) copy-start(bf16[192,512]{1,0:T(8,128)(2,1)} %modes_ref.1) | copy-start | bytes 589828
  26.3 1.8 %collective-permute-start.7 = (f32[768,128]{1,0:T(8,128)S(1)}, f32[768,128]{1,0:T(8,128)S(1)}, u32[]{:S(2)}, u32[]{:S(2)}) collective-permute-start(f32[768,128]{1,0:T(8,128)S(1)} %shard_map.80.pressure_ref.own_ref), channel_id=1, source_target_pairs={{0,1},{1,0},{2,3},{3,2},{4,5},{5,4},{6,7},{7,6},{8,9},{9,8},{10,11... | collective-permute-start | bytes 1179656 | tf_op jit(solution)/shard_map/ppermute | solution.py:340
  29.4 1.4 %collective-permute-start.8 = (f32[4,64,128]{2,1,0:T(8,128)S(1)}, f32[4,64,128]{2,1,0:T(8,128)S(1)}, u32[]{:S(2)}, u32[]{:S(2)}) collective-permute-start(f32[4,64,128]{2,1,0:T(8,128)S(1)} %dynamic-slice_bitcast_fusion), channel_id=1, source_target_pairs={{0,1},{1,0},{2,3},{3,2},{4,5},{5,4},{6,7},{7,6},{8,9},{9,8},{10,11... | collective-permute-start | bytes 393224 | tf_op jit(solution)/shard_map/ppermute | solution.py:340
  30.9 4.9 %collective-permute-start.11 = (f32[64,128]{1,0:T(8,128)S(1)}, f32[64,128]{1,0:T(8,128)S(1)}, u32[]{:S(2)}, u32[]{:S(2)}) collective-permute-start(f32[64,128]{1,0:T(8,128)S(1)} %get-tuple-element.37), channel_id=1, source_target_pairs={{0,6},{1,7},{2,4},{3,5},{4,2},{5,3},{6,0},{7,1},{8,14},{9,15},{10,... | collective-permute-start | bytes 98312 | tf_op jit(solution)/shard_map/ppermute | solution.py:340
  32.3 3.9 %collective-permute-start.10 = (f32[64,128]{1,0:T(8,128)S(1)}, f32[64,128]{1,0:T(8,128)S(1)}, u32[]{:S(2)}, u32[]{:S(2)}) collective-permute-start(f32[64,128]{1,0:T(8,128)S(1)} %get-tuple-element.38), channel_id=1, source_target_pairs={{0,4},{1,5},{2,6},{3,7},{4,0},{5,1},{6,2},{7,3},{8,12},{9,13},{10,... | collective-permute-start | bytes 98312 | tf_op jit(solution)/shard_map/ppermute | solution.py:340
  32.9 3.9 %collective-permute-start.9 = (f32[64,128]{1,0:T(8,128)S(1)}, f32[64,128]{1,0:T(8,128)S(1)}, u32[]{:S(2)}, u32[]{:S(2)}) collective-permute-start(f32[64,128]{1,0:T(8,128)S(1)} %get-tuple-element.36), channel_id=1, source_target_pairs={{0,2},{1,3},{2,0},{3,1},{4,6},{5,7},{6,4},{7,5},{8,10},{9,11},{10,... | collective-permute-start | bytes 98312 | tf_op jit(solution)/shard_map/ppermute | solution.py:340

commit v3 on v2

--- a/solution.py
+++ b/solution.py
@@ -109,20 +109,21 @@
     1.883557915687561,
     -0.3106880187988281,
 )
+turn_scale = wavenumber / (2.0 * math.pi)
 lanes = 128
-piece = 64
 step_rows = 64
 whole = pl.BlockSpec(memory_space=pltpu.VMEM)
-
-
-def call(kernel, outs, scratch, *args, cost=None):
+remote = pl.BlockSpec(memory_space=pltpu.HBM)
+
+
+def call(kernel, outs, scratch, *args, cost=None, specs=None):
     shapes = tuple(jax.ShapeDtypeStruct(shape, dtype) for shape, dtype in outs)
     return pl.pallas_call(
         kernel,
         out_shape=shapes,
-        in_specs=[whole] * len(args),
+        in_specs=specs or [whole] * len(args),
         out_specs=(whole,) * len(shapes),
-        scratch_shapes=[pltpu.VMEM(shape, dtype) for shape, dtype in scratch],
+        scratch_shapes=[entry if not isinstance(entry, tuple) else pltpu.VMEM(*entry) for entry in scratch],
         compiler_params=pltpu.CompilerParams(vmem_limit_bytes=16 * 2**20),
         cost_estimate=cost,
     )(*args)
@@ -135,16 +136,22 @@
     return total
 
 
-def place_panels(order_ref, coords_ref, areas_ref, weights_ref, ids, along, down):
+def place_panels(order_ref, coords_ref, areas_ref, weights_ref, halves, ids, along, down):
     col = lax.axis_index("col")
     chip, core = col // 2, col % 2
+    blocks = order_ref.shape[0]
+    first_half = lax.broadcasted_iota(jnp.int32, (1, lanes), 1) < lanes // 2
+    halves[0, :blocks, :] = order_ref[...]
+    halves[1, :blocks, :] = pltpu.roll(order_ref[...], lanes // 2, 1)
     ids[...] = jnp.zeros(ids.shape, jnp.int32)
-    count = order_ref.shape[0]
-    for at in range(count):
-        side, slot, part = at // (count // 2), at % (count // 2) // 3, at % 3
-        panel_block = 2 * (chip ^ slot) + (core if side == 0 else 1 - core)
-        first = at % 2 * piece
-        ids[at // 2 : at // 2 + 1, first : first + piece] = order_ref[pl.ds(3 * panel_block + part, 1), :]
+    for block in range(blocks):
+        found = []
+        for at in (2 * block, 2 * block + 1):
+            side, slot, part = at // blocks, at % blocks // 3, at % 3
+            panel_block = 2 * (chip ^ slot) + (core if side == 0 else 1 - core)
+            source = 3 * panel_block + part
+            found.append(halves[(source + at) % 2, pl.ds(source // 2, 1), :])
+        ids[block : block + 1, :] = jnp.where(first_half, found[0], found[1])
     for group in range(ids.shape[0] // 8):
         index = ids[8 * group : 8 * group + 8, :]
         high, low = index // lanes, index % lanes
@@ -160,6 +167,8 @@
                 values[which] = jnp.where(chosen, found, values[which])
         for which, value in enumerate(values):
             along[which, 8 * group : 8 * group + 8, :] = value
+            if which < 3:
+                value = value * jnp.float32(turn_scale)
             down[which, :, 8 * group : 8 * group + 8] = jnp.transpose(value)
 
 
@@ -172,11 +181,11 @@
             )
 
 
-def fill_green(rows_ref, columns_ref, norm_const, forward_ref, first_row, row_count, adjoint_ref=None):
+def fill_green(rows_ref, columns_ref, norm_const, forward_ref, adjoint_ref):
     def fill(step, carry):
-        rows = pl.ds(pl.multiple_of(first_row + step * step_rows, step_rows), step_rows)
+        rows = pl.ds(pl.multiple_of(step * step_rows, step_rows), step_rows)
         row_x, row_y, row_z, row_area = [rows_ref[which, rows, :] for which in range(4)]
-        row_area = row_area * jnp.float32(1.0 / norm_const)
+        row_area = row_area * jnp.float32(turn_scale / norm_const)
         for part in range(columns_ref.shape[2] // lanes):
             columns = slice(part * lanes, (part + 1) * lanes)
             col_x, col_y, col_z, col_area = [
@@ -184,24 +193,21 @@
             ]
             offset_x, offset_y, offset_z = row_x - col_x, row_y - col_y, row_z - col_z
             square = offset_x * offset_x + offset_y * offset_y
-            square = square + (offset_z * offset_z + jnp.float32(smoothing * smoothing))
+            square = square + (offset_z * offset_z + jnp.float32((smoothing * turn_scale) ** 2))
             inverse = lax.rsqrt(square)
-            turns = (square * jnp.float32(wavenumber / (2.0 * math.pi))) * inverse
+            turns = square * inverse
             half_turn = turns - jnp.floor(turns) - jnp.float32(0.5)
             power = half_turn * half_turn
             sine = half_turn * horner(sine_terms, power)
-            real_part = sine * sine - jnp.float32(1.0)
-            imag_part = sine * horner(cosine_terms, power)
-            factor = inverse * col_area
-            forward_ref[0, rows, columns] = (real_part * factor).astype(jnp.bfloat16)
-            forward_ref[1, rows, columns] = (imag_part * factor).astype(jnp.bfloat16)
-            if adjoint_ref is not None:
-                factor = inverse * row_area
-                adjoint_ref[0, rows, columns] = (real_part * factor).astype(jnp.bfloat16)
-                adjoint_ref[1, rows, columns] = (imag_part * factor).astype(jnp.bfloat16)
+            cosine = horner(cosine_terms, power)
+            for out_ref, area in ((forward_ref, col_area), (adjoint_ref, row_area)):
+                factor = inverse * area
+                scaled = sine * factor
+                out_ref[0, rows, columns] = (scaled * sine - factor).astype(jnp.bfloat16)
+                out_ref[1, rows, columns] = (scaled * cosine).astype(jnp.bfloat16)
         return carry
 
-    lax.fori_loop(0, row_count // step_rows, fill, 0)
+    lax.fori_loop(0, forward_ref.shape[1] // step_rows, fill, 0)
 
 
 def first_tile_kernel(
@@ -214,50 +220,55 @@
     adjoint_ref,
     columns_ref,
     down_ref,
+    halves,
     ids,
     along,
     rows_ref,
 ):
-    place_panels(order_ref, coords_ref, areas_ref, weights_ref, ids, along, down_ref)
+    place_panels(order_ref, coords_ref, areas_ref, weights_ref, halves, ids, along, down_ref)
     for which in range(4):
-        scale = jnp.float32(1.0 / norm_const if which == 3 else 1.0)
+        scale = jnp.float32(turn_scale / norm_const if which == 3 else turn_scale)
         for block in range(columns_ref.shape[2] // lanes):
             columns_ref[which, :, block * lanes : (block + 1) * lanes] = jnp.broadcast_to(
                 along[which, block : block + 1, :] * scale, (8, lanes)
             )
     spread_rows(down_ref, rows_ref, 0)
-    own = adjoint_ref.shape[1]
-    fill_green(rows_ref, columns_ref, norm_const, forward_ref, 0, own, adjoint_ref)
-    fill_green(rows_ref, columns_ref, norm_const, forward_ref, own, forward_ref.shape[1] - own)
-
-
-def next_tile_kernel(norm_const, first, columns_ref, down_ref, forward_ref, rows_ref):
+    fill_green(rows_ref, columns_ref, norm_const, forward_ref, adjoint_ref)
+
+
+def next_tile_kernel(norm_const, first, columns_ref, down_ref, forward_ref, adjoint_ref, rows_ref):
     spread_rows(down_ref, rows_ref, first // lanes)
-    fill_green(rows_ref, columns_ref, norm_const, forward_ref, 0, forward_ref.shape[1])
-
-
-def first_tile(coords, panel_order, areas, weights, norm_const, row_count, own_rows):
-    panels = panel_order.shape[0]
-    blocks = -(-panels // (8 * lanes)) * 8
-    wide = (panels // lanes, lanes)
+    fill_green(rows_ref, columns_ref, norm_const, forward_ref, adjoint_ref)
+
+
+def tile_cost(row_count, panels):
+    pairs = row_count * panels
+    return pl.CostEstimate(flops=40 * pairs, bytes_accessed=8 * pairs, transcendentals=3 * pairs)
+
+
+def first_tile(order, coords, areas, weights, norm_const, row_count):
+    blocks = order.shape[0]
+    panels = blocks * lanes
+    padded = -(-blocks // 8) * 8
     return call(
         functools.partial(first_tile_kernel, norm_const),
         (
             ((2, row_count, panels), jnp.bfloat16),
-            ((2, own_rows, panels), jnp.bfloat16),
+            ((2, row_count, panels), jnp.bfloat16),
             ((4, 8, panels), jnp.float32),
-            ((5, lanes, blocks), jnp.float32),
+            ((5, lanes, padded), jnp.float32),
         ),
         (
-            ((blocks, lanes), jnp.int32),
-            ((5, blocks, lanes), jnp.float32),
-            ((4, row_count, lanes), jnp.float32),
+            ((2, padded, lanes), jnp.int32),
+            ((padded, lanes), jnp.int32),
+            ((5, padded, lanes), jnp.float32),
+            ((4, -(-row_count // lanes) * lanes, lanes), jnp.float32),
         ),
-        panel_order.reshape(panels // piece, piece),
+        order,
         coords,
-        areas.reshape(wide),
-        weights.reshape(wide),
-        cost=pl.CostEstimate(flops=10**9, bytes_accessed=2**22, transcendentals=10**6),
+        areas,
+        weights,
+        cost=tile_cost(row_count, panels),
     )
 
 
@@ -265,12 +276,56 @@
     panels = columns.shape[2]
     return call(
         functools.partial(next_tile_kernel, norm_const, first),
-        (((2, row_count, panels), jnp.bfloat16),),
+        (((2, row_count, panels), jnp.bfloat16),) * 2,
         (((4, row_count, lanes), jnp.float32),),
         columns,
         down,
-        cost=pl.CostEstimate(flops=10**9, bytes_accessed=2**22, transcendentals=10**6),
-    )[0]
+        cost=tile_cost(row_count, panels),
+    )
+
+
+def load_kernel(*refs):
+    count = 6
+    sources, kept = refs[:count], refs[count : 2 * count - 1]
+    terms_ref, sent_ref, velocity, sems = refs[2 * count - 1 :]
+    copies = [
+        pltpu.make_async_copy(source, target, sems.at[at])
+        for at, (source, target) in enumerate(zip(sources, (velocity, *kept)))
+    ]
+    for copy in copies:
+        copy.start()
+    copies[0].wait()
+    copies[1].wait()
+    terms = jnp.dot(kept[0][...], velocity[...], preferred_element_type=jnp.float32)
+    terms_ref[...] = terms
+    sent_ref[...] = terms.astype(jnp.bfloat16)
+    for copy in copies[2:]:
+        copy.wait()
+
+
+def load(modal_velocity, mode_shapes, *tables):
+    out = (mode_shapes.shape[0], modal_velocity.shape[1])
+    return call(
+        load_kernel,
+        tuple((value.shape, value.dtype) for value in (mode_shapes, *tables))
+        + ((out, jnp.float32), (out, jnp.bfloat16)),
+        ((modal_velocity.shape, modal_velocity.dtype), pltpu.SemaphoreType.DMA((6,))),
+        *[pltpu.with_memory_space_constraint(value, pltpu.HBM) for value in (modal_velocity, mode_shapes, *tables)],
+        specs=[remote] * 6,
+    )
+
+
+def join_kernel(terms_ref, first_ref, second_ref, third_ref, modes_ref, *out_refs):
+    chip = lax.axis_index("col") // 2
+    count = terms_ref.shape[0]
+    total = terms_ref[...]
+    for part in (first_ref, second_ref, third_ref):
+        total = total + part[...].astype(jnp.float32)
+    total = total.astype(jnp.bfloat16)
+    for slot, out_ref in enumerate(out_refs):
+        out_ref[:count, :] = total
+        first = pl.multiple_of((chip ^ slot) * lanes, lanes)
+        out_ref[count:, :] = modes_ref[:, pl.ds(first, lanes)]
 
 
 def turned(value, sign):
@@ -309,47 +364,48 @@
     return jnp.concatenate(parts, 0)
 
 
-def own_adjoint_kernel(tile_ref, pressure_ref, down_ref, out_ref):
+def own_adjoint_kernel(first_ref, second_ref, pressure_ref, down_ref, out_ref):
     half = pressure_ref.shape[0]
-    out_ref[...] = tile_dot(tile_ref, slice(0, half), sources(pressure_ref, down_ref, 0), -1)
-
-
-def modal_kernel(tile_ref, own_ref, other_ref, down_ref, term_ref, modes_ref, modal_ref, pressure_ref):
+    value = sources(pressure_ref, down_ref, 0)
+    first = 0
+    for tile_ref in (first_ref, second_ref):
+        rows = slice(first, first + tile_ref.shape[1])
+        out_ref[rows, :] = tile_dot(tile_ref, slice(0, half), value, -1)
+        first = rows.stop
+
+
+def modal_kernel(first_ref, second_ref, own_ref, other_ref, down_ref, term_ref, *refs):
+    modes_refs, (kept_ref, sent_ref, pressure_ref, sensitivity) = refs[:4], refs[4:]
     row = lax.axis_index("row")
     col = lax.axis_index("col")
     chip, core = col // 2, col % 2
     half = own_ref.shape[0]
-    sensitivity = term_ref[...] + tile_dot(
-        tile_ref, slice(half, 2 * half), sources(other_ref, down_ref, 1), -1
-    )
-    modal_ref[...] = lax.dot_general(
-        modes_ref[...],
-        sensitivity.astype(jnp.bfloat16),
-        (((0,), (0,)), ((), ())),
-        preferred_element_type=jnp.float32,
-    )
+    count = half // 4
+    value = sources(other_ref, down_ref, 1)
+    first = 0
+    for tile_ref in (first_ref, second_ref):
+        rows = slice(first, first + tile_ref.shape[1])
+        term = term_ref[rows, :] + tile_dot(tile_ref, slice(half, 2 * half), value, -1)
+        sensitivity[rows, :] = term.astype(jnp.bfloat16)
+        first = rows.stop
+    modes = jnp.concatenate([modes_ref[count:, :] for modes_ref in modes_refs], 0)
+    modal = lax.dot_general(
+        modes, sensitivity[...], (((0,), (0,)), ((), ())), preferred_element_type=jnp.float32
+    )
+    modes_each = kept_ref.shape[0]
+    low, high = modal[:modes_each, :], modal[modes_each:, :]
+    kept_ref[...] = jnp.where(core == 0, low, high)
+    sent_ref[...] = jnp.where(core == 0, high, low)
     each = pressure_ref.shape[0]
-    per_block = modes_ref.shape[0] // each
+    per_block = count // each
     panel_block = 2 * row + col // per_block
-    first = (panel_block // 2 ^ chip) * modes_ref.shape[0] + col % per_block * each
+    first = (panel_block // 2 ^ chip) * count + col % per_block * each
     rows = pl.ds(pl.multiple_of(first, each), each)
     pressure_ref[...] = jnp.where(panel_block % 2 == core, own_ref[rows, :], other_ref[rows, :])
 
 
 def swap(value, axis, mask):
     return lax.ppermute(value, axis, [(i, i ^ mask) for i in range(lax.axis_size(axis))])
-
-
-def col_scatter(value):
-    col = lax.axis_index("col")
-    core, chip = col % 2, col // 2
-    blocks = value.reshape(4, 2, value.shape[0] // 8, value.shape[1])
-    kept = lax.dynamic_index_in_dim(blocks, core, 1, False)
-    kept = kept + swap(lax.dynamic_index_in_dim(blocks, 1 - core, 1, False), "col", 1)
-    total = lax.dynamic_index_in_dim(kept, chip, 0, False)
-    for mask in (1, 2, 3):
-        total = total + swap(lax.dynamic_index_in_dim(kept, chip ^ mask, 0, False), "col", 2 * mask)
-    return total
 
 
 def local(modal_velocity, mode_shapes, coords, panel_order, areas, weights):
@@ -357,40 +413,52 @@
     norm_const = math.sqrt(4.0 * math.pi * panels)
     own_rows, load_columns = mode_shapes.shape[0], modal_velocity.shape[1]
     half = 4 * own_rows
-    part_rows = half // 2
-    terms = jnp.dot(mode_shapes, modal_velocity, preferred_element_type=jnp.float32)
-    sent = terms.astype(jnp.bfloat16)
+    part_rows = 256 * half // 768
+    wide = (panels // lanes, lanes)
+    modes, order, coords, areas, weights, terms, sent = load(
+        modal_velocity,
+        mode_shapes,
+        panel_order.reshape(wide),
+        coords,
+        areas.reshape(wide),
+        weights.reshape(wide),
+    )
     received = [swap(sent, "row", mask) for mask in (1, 2, 3)]
-    tiles = first_tile(coords, panel_order, areas, weights, norm_const, part_rows, own_rows)
+    tiles = first_tile(order, coords, areas, weights, norm_const, part_rows)
     received, tiles = lax.optimization_barrier((received, tiles))
     tile, own_tile, columns, down = tiles
-    surface = (terms + sum(part.astype(jnp.float32) for part in received)).astype(jnp.bfloat16)
-    received = [swap(surface, "col", 2 * mask) for mask in (1, 2, 3)]
-    last_tile = next_tile(columns, down, norm_const, part_rows, half - part_rows)
-    received, last_tile = lax.optimization_barrier((received, last_tile))
-    own = jnp.concatenate([surface] + received, 0)
+    joined = call(
+        join_kernel, (((2 * own_rows, load_columns), jnp.bfloat16),) * 4, (), terms, *received, modes
+    )
+    received = [swap(value, "col", 2 * mask) for mask, value in zip((1, 2, 3), joined[1:])]
+    tiles = next_tile(columns, down, norm_const, part_rows, half - part_rows)
+    received, (last_tile, last_own_tile) = lax.optimization_barrier((received, tiles))
+    joined = [joined[0], *received]
+    own = jnp.concatenate([value[:own_rows] for value in joined], 0)
     other = swap(own, "col", 1)
     out = (((half, load_columns), jnp.float32),)
     term = call(functools.partial(pressure_kernel, 0), out, (), tile, last_tile, own)[0]
     pressure = call(functools.partial(pressure_kernel, 1), out, (), tile, last_tile, other, term)[0]
     other = swap(pressure, "col", 1)
-    out = (((own_rows, load_columns), jnp.float32),)
-    term = call(own_adjoint_kernel, out, (), own_tile, pressure, down)[0]
-    modal_terms, own_pressure = call(
+    term = call(own_adjoint_kernel, out, (), own_tile, last_own_tile, pressure, down)[0]
+    modes_each = mode_shapes.shape[1] // 8
+    kept, sent, own_pressure = call(
         modal_kernel,
         (
-            ((mode_shapes.shape[1], load_columns), jnp.float32),
+            ((modes_each, load_columns), jnp.float32),
+            ((modes_each, load_columns), jnp.float32),
             ((own_rows // lax.axis_size("row"), load_columns), jnp.float32),
         ),
-        (),
+        (((half, load_columns), jnp.bfloat16),),
         own_tile,
+        last_own_tile,
         pressure,
         other,
         down,
         term,
-        mode_shapes,
-    )
-    return (own_pressure, col_scatter(modal_terms))
+        *joined,
+    )
+    return (own_pressure, kept + swap(sent, "col", 1))
 
 
 def solution(mesh):

time: 37.8 us -> 28.7 us (0.76)
  local copies, waits for them, and re-layouts: 3.83 us -> 0.02 us
  starting transfers between devices: 13.3 us -> 9.72 us
  waiting for transfers between devices: 6.48 us -> 3.25 us
  Pallas kernels: 11.3 us -> 14.2 us
  matrix products: 1.12 us -> 0 us
    ppermute x12 -> x9, starting transfers between devices: 13.3 us -> 9.72 us  [swap(): lax.ppermute(value, axis, [(i, i ^ mask) for i in range(lax.axis_size(axi...]
    ppermute x12 -> x9, waiting for transfers between devices: 6.48 us -> 3.25 us  [swap(): lax.ppermute(value, axis, [(i, i ^ mask) for i in range(lax.axis_size(axi...]
    unnamed x10 -> x0, local copies, waits for them, and re-layouts: 3.04 us -> none
    pallas_call x6 -> x8, Pallas kernels: 11.3 us -> 14.2 us  [call(): pl.pallas_call(kernel, out_shape=shapes, in_specs=specs or [whole] * len(...]
    dot_general x1 -> x0, matrix products: 1.12 us -> none  [local(): jnp.dot(mode_shapes, modal_velocity, preferred_element_type=jnp.float32)]
    reshape x1 -> x0, local copies, waits for them, and re-layouts: 0.77 us -> none  [first_tile(): panel_order.reshape(panels // piece, piece)]
  transfers between devices with their start and end apart: 12 -> 9, of which waited for: 7 -> 4; matrix products, arithmetic and copies ran while one was open for 2% -> 0% of each run, Pallas kernels for 24% -> 36%
where the time goes in v3:
time: 28.7 us; the launch traced here: 28.6 us
  Pallas kernels  14.2 us (49%)
  starting transfers between devices  9.72 us (34%)
  waiting for transfers between devices  3.25 us (11%)
  between operations  0.75 us (3%)
  other arithmetic  0.64 us (2%)
    pallas_call x8, Pallas kernels, call(): pl.pallas_call(kernel, out_shape=shapes, in_specs=specs or [whole] * len(...  14.2 us
    ppermute x9, starting transfers between devices, swap(): lax.ppermute(value, axis, [(i, i ^ mask) for i in range(lax.axis_size(axi...  9.72 us
    ppermute x9, waiting for transfers between devices, swap(): lax.ppermute(value, axis, [(i, i ^ mask) for i in range(lax.axis_size(axi...  3.25 us
    add x1, other arithmetic, local(): return (own_pressure, kept + swap(sent, 'col', 1))  0.62 us
  transfers between devices with their start and end apart: 9, of which 4 were waited for; matrix products, arithmetic and copies ran while one was open for 0% of the time, Pallas kernels for 36%

profile of v3, /device:TPU:0, one launch (start us, length us, event | category | flops | bytes accessed | tf_op | source)
XLA Modules:
  0.0 28.6 jit_solution(6063006230839183133)
XLA Ops:
  0.6 1.2 %shard_map.77 = (bf16[192,512]{1,0:T(8,128)(2,1)S(1)}, s32[12,128]{1,0:T(8,128)S(1)}, f32[3,1536]{1,0:T(4,128)S(1)}, f32[12,128]{1,0:T(8,128)S(1)}, f32[12,128]{...) custom-call(bf16[512,128]{1,0:T(8,128)(2,1)} %refs_0_.1, bf16[192,512]{1,0:T(8,128)(2,1)} %refs_1_.1, ...), custom_call_target="tpu_custom_call" | custom-call | tf_op jit(solution)/shard_map/pallas_call | solution.py:121
  1.9 5.1 %collective-permute-start.2 = (bf16[192,128]{1,0:T(8,128)(2,1)S(1)}, bf16[192,128]{1,0:T(8,128)(2,1)S(1)}, u32[]{:S(2)}, u32[]{:S(2)}) collective-permute-start(bf16[192,128]{1,0:T(8,128)(2,1)S(1)} %get-tuple-element.34), channel_id=1, source_target_pairs={{0,24},{8,16},{16,8},{24,0},{1,25},{9,17},{17,9},{25,1},{2,26},{10... | collective-permute-start | bytes 147464 | tf_op jit(solution)/shard_map/ppermute | solution.py:408
  7.0 0.0 collective-permute-start.1
  7.0 0.6 %collective-permute-start = (bf16[192,128]{1,0:T(8,128)(2,1)S(1)}, bf16[192,128]{1,0:T(8,128)(2,1)S(1)}, u32[]{:S(2)}, u32[]{:S(2)}) collective-permute-start(bf16[192,128]{1,0:T(8,128)(2,1)S(1)} %get-tuple-element.34), channel_id=1, source_target_pairs={{0,8},{8,0},{16,24},{24,16},{1,9},{9,1},{17,25},{25,17},{2,10},{10... | collective-permute-start | bytes 147464 | tf_op jit(solution)/shard_map/ppermute | solution.py:408
  7.6 3.2 %shard_map.78 = (bf16[2,256,1536]{2,1,0:T(8,128)(2,1)S(1)}, bf16[2,256,1536]{2,1,0:T(8,128)(2,1)S(1)}, f32[4,8,1536]{2,1,0:T(8,128)S(1)}, f32[5,128,16]{2,1,0:T(8,128)S(1)}) custom-call(s32[12,128]{1,0:T(8,128)S(1)} %get-tuple-element.35.order_ref, f32[3,1536]{1,0:T(4,128)S(1)} %get-tuple-element.36.coords_ref, f32[12,128]{1,0:T(8,128)S(1)} %get-tuple-element.37.areas_ref, ...), custom_call_target="tpu_custom_call" | custom-call | flops 15728640 | bytes 3145728 | tf_op jit(solution)/shard_map/pallas_call | solution.py:121
  10.9 0.0 collective-permute-done.2.third_ref
  10.9 1.1 %collective-permute-done.1.second_ref = bf16[192,128]{1,0:T(8,128)(2,1)S(1)} collective-permute-done((bf16[192,128]{1,0:T(8,128)(2,1)S(1)}, bf16[192,128]{1,0:T(8,128)(2,1)S(1)}, u32[]{:S(2)}, u32[]{:S(2)}) %collective-permute-start.1) | collective-permute-done | bytes 49184 | tf_op jit(solution)/shard_map/ppermute | solution.py:408
  12.0 0.0 collective-permute-done.first_ref
  12.0 0.1 shard_map.79
  12.1 1.6 %collective-permute-start.3 = (bf16[384,128]{1,0:T(8,128)(2,1)S(1)}, bf16[384,128]{1,0:T(8,128)(2,1)S(1)}, u32[]{:S(2)}, u32[]{:S(2)}) collective-permute-start(bf16[384,128]{1,0:T(8,128)(2,1)S(1)} %get-tuple-element.49), channel_id=1, source_target_pairs={{0,2},{1,3},{2,0},{3,1},{4,6},{5,7},{6,4},{7,5},{8,10},{9,11},{10,... | collective-permute-start | bytes 294920 | tf_op jit(solution)/shard_map/ppermute | solution.py:408
  13.6 1.5 %collective-permute-start.4 = (bf16[384,128]{1,0:T(8,128)(2,1)S(1)}, bf16[384,128]{1,0:T(8,128)(2,1)S(1)}, u32[]{:S(2)}, u32[]{:S(2)}) collective-permute-start(bf16[384,128]{1,0:T(8,128)(2,1)S(1)} %get-tuple-element.50), channel_id=1, source_target_pairs={{0,4},{1,5},{2,6},{3,7},{4,0},{5,1},{6,2},{7,3},{8,12},{9,13},{10,... | collective-permute-start | bytes 294920 | tf_op jit(solution)/shard_map/ppermute | solution.py:408
  15.1 0.5 %collective-permute-start.5 = (bf16[384,128]{1,0:T(8,128)(2,1)S(1)}, bf16[384,128]{1,0:T(8,128)(2,1)S(1)}, u32[]{:S(2)}, u32[]{:S(2)}) collective-permute-start(bf16[384,128]{1,0:T(8,128)(2,1)S(1)} %get-tuple-element.51), channel_id=1, source_target_pairs={{0,6},{1,7},{2,4},{3,5},{4,2},{5,3},{6,0},{7,1},{8,14},{9,15},{10,... | collective-permute-start | bytes 294920 | tf_op jit(solution)/shard_map/ppermute | solution.py:408
  15.6 5.1 %shard_map.80 = (bf16[2,512,1536]{2,1,0:T(8,128)(2,1)S(1)}, bf16[2,512,1536]{2,1,0:T(8,128)(2,1)S(1)}) custom-call(f32[4,8,1536]{2,1,0:T(8,128)S(1)} %get-tuple-element.52.columns_ref, f32[5,128,16]{2,1,0:T(8,128)S(1)} %get-tuple-element.53.down_ref), custom_call_target="tpu_custom_call" | custom-call | flops 31457280 | bytes 6291456 | tf_op jit(solution)/shard_map/pallas_call | solution.py:121
  20.7 0.0 collective-permute-done.3.refs_1_
  20.7 0.0 collective-permute-done.4.refs_2_
  20.7 0.0 collective-permute-done.5.refs_3_
  20.8 0.1 collective-permute-start.6
  20.9 0.9 %shard_map.81.refs_3_ = f32[768,128]{1,0:T(8,128)S(1)} custom-call(bf16[2,256,1536]{2,1,0:T(8,128)(2,1)S(1)} %get-tuple-element.57.refs_0_, bf16[2,512,1536]{2,1,0:T(8,128)(2,1)S(1)} %get-tuple-element.58.refs_1_, bf16[768,128]{1,0:T(8,128)(2,1)S(1)} %pad_maximum_fusion.refs_2_), custom_call_target="tpu_custom_call" | custom-call | tf_op jit(solution)/shard_map/pallas_call | solution.py:121
  21.8 0.5 %collective-permute-done.6.refs_2_ = bf16[768,128]{1,0:T(8,128)(2,1)S(1)} collective-permute-done((bf16[768,128]{1,0:T(8,128)(2,1)S(1)}, bf16[768,128]{1,0:T(8,128)(2,1)S(1)}, u32[]{:S(2)}, u32[]{:S(2)}) %collective-permute-start.6) | collective-permute-done | bytes 196640 | tf_op jit(solution)/shard_map/ppermute | solution.py:408
  22.3 0.9 %shard_map.82.pressure_ref.own_ref = f32[768,128]{1,0:T(8,128)S(1)} custom-call(bf16[2,256,1536]{2,1,0:T(8,128)(2,1)S(1)} %get-tuple-element.57.refs_0_, bf16[2,512,1536]{2,1,0:T(8,128)(2,1)S(1)} %get-tuple-element.58.refs_1_, bf16[768,128]{1,0:T(8,128)(2,1)S(1)} %collective-permute-done.6.refs_2_, f32[768,128]{1,0:T(8,128)S(1)} %shard_map.81.refs_3_), custom_call_target="tpu_custom_call" | custom-call | tf_op jit(solution)/shard_map/pallas_call | solution.py:121
  23.2 0.2 collective-permute-start.7
  23.4 1.0 %shard_map.83.term_ref = f32[768,128]{1,0:T(8,128)S(1)} custom-call(bf16[2,256,1536]{2,1,0:T(8,128)(2,1)S(1)} %get-tuple-element.43.first_ref, bf16[2,512,1536]{2,1,0:T(8,128)(2,1)S(1)} %get-tuple-element.56.second_ref, f32[768,128]{1,0:T(8,128)S(1)} %shard_map.82.pressure_ref.own_ref, f32[5,128,16]{2,1,0:T(8,128)S(1)} %get-tuple-element.53.down_ref), custom_call_target="tpu_custom_call" | custom-call | tf_op jit(solution)/shard_map/pallas_call | solution.py:121
  24.5 0.5 %collective-permute-done.7.other_ref = f32[768,128]{1,0:T(8,128)S(1)} collective-permute-done((f32[768,128]{1,0:T(8,128)S(1)}, f32[768,128]{1,0:T(8,128)S(1)}, u32[]{:S(2)}, u32[]{:S(2)}) %collective-permute-start.7) | collective-permute-done | bytes 393248 | tf_op jit(solution)/shard_map/ppermute | solution.py:408
  25.0 1.7 %shard_map.84 = (f32[64,128]{1,0:T(8,128)S(1)}, f32[64,128]{1,0:T(8,128)S(1)}, f32[48,128]{1,0:T(8,128)}) custom-call(bf16[2,256,1536]{2,1,0:T(8,128)(2,1)S(1)} %get-tuple-element.43.first_ref, bf16[2,512,1536]{2,1,0:T(8,128)(2,1)S(1)} %get-tuple-element.56.second_ref, f32[768,128]{1,0:T(8,128)S(1)} %shard_map.82.pressure_ref.own_ref, ...), custom_call_target="tpu_custom_call" | custom-call | tf_op jit(solution)/shard_map/pallas_call | solution.py:121
  26.8 0.1 collective-permute-start.8
  26.9 1.1 %collective-permute-done.8 = f32[64,128]{1,0:T(8,128)S(1)} collective-permute-done((f32[64,128]{1,0:T(8,128)S(1)}, f32[64,128]{1,0:T(8,128)S(1)}, u32[]{:S(2)}, u32[]{:S(2)}) %collective-permute-start.8) | collective-permute-done | bytes 32800 | tf_op jit(solution)/shard_map/ppermute | solution.py:408
  28.0 0.6 %add.3 = f32[64,128]{1,0:T(8,128)} add(f32[64,128]{1,0:T(8,128)S(1)} %get-tuple-element.64, f32[64,128]{1,0:T(8,128)S(1)} %collective-permute-done.8) | non-fusion elementwise | flops 8192 | bytes 98304 | tf_op jit(solution)/shard_map/add | solution.py:461
  (5 shorter events, 0.0 us)
Async XLA Ops:
  1.9 9.0 %collective-permute-start.2 = (bf16[192,128]{1,0:T(8,128)(2,1)S(1)}, bf16[192,128]{1,0:T(8,128)(2,1)S(1)}, u32[]{:S(2)}, u32[]{:S(2)}) collective-permute-start(bf16[192,128]{1,0:T(8,128)(2,1)S(1)} %get-tuple-element.34), channel_id=1, source_target_pairs={{0,24},{8,16},{16,8},{24,0},{1,25},{9,17},{17,9},{25,1},{2,26},{10... | collective-permute-start | bytes 147464 | tf_op jit(solution)/shard_map/ppermute | solution.py:408
  7.0 5.0 %collective-permute-start.1 = (bf16[192,128]{1,0:T(8,128)(2,1)S(1)}, bf16[192,128]{1,0:T(8,128)(2,1)S(1)}, u32[]{:S(2)}, u32[]{:S(2)}) collective-permute-start(bf16[192,128]{1,0:T(8,128)(2,1)S(1)} %get-tuple-element.34), channel_id=1, source_target_pairs={{0,16},{8,24},{16,0},{24,8},{1,17},{9,25},{17,1},{25,9},{2,18},{10... | collective-permute-start | bytes 147464 | tf_op jit(solution)/shard_map/ppermute | solution.py:408
  7.0 5.0 %collective-permute-start = (bf16[192,128]{1,0:T(8,128)(2,1)S(1)}, bf16[192,128]{1,0:T(8,128)(2,1)S(1)}, u32[]{:S(2)}, u32[]{:S(2)}) collective-permute-start(bf16[192,128]{1,0:T(8,128)(2,1)S(1)} %get-tuple-element.34), channel_id=1, source_target_pairs={{0,8},{8,0},{16,24},{24,16},{1,9},{9,1},{17,25},{25,17},{2,10},{10... | collective-permute-start | bytes 147464 | tf_op jit(solution)/shard_map/ppermute | solution.py:408
  12.1 8.7 %collective-permute-start.3 = (bf16[384,128]{1,0:T(8,128)(2,1)S(1)}, bf16[384,128]{1,0:T(8,128)(2,1)S(1)}, u32[]{:S(2)}, u32[]{:S(2)}) collective-permute-start(bf16[384,128]{1,0:T(8,128)(2,1)S(1)} %get-tuple-element.49), channel_id=1, source_target_pairs={{0,2},{1,3},{2,0},{3,1},{4,6},{5,7},{6,4},{7,5},{8,10},{9,11},{10,... | collective-permute-start | bytes 294920 | tf_op jit(solution)/shard_map/ppermute | solution.py:408
  13.6 7.1 %collective-permute-start.4 = (bf16[384,128]{1,0:T(8,128)(2,1)S(1)}, bf16[384,128]{1,0:T(8,128)(2,1)S(1)}, u32[]{:S(2)}, u32[]{:S(2)}) collective-permute-start(bf16[384,128]{1,0:T(8,128)(2,1)S(1)} %get-tuple-element.50), channel_id=1, source_target_pairs={{0,4},{1,5},{2,6},{3,7},{4,0},{5,1},{6,2},{7,3},{8,12},{9,13},{10,... | collective-permute-start | bytes 294920 | tf_op jit(solution)/shard_map/ppermute | solution.py:408
  15.1 5.6 %collective-permute-start.5 = (bf16[384,128]{1,0:T(8,128)(2,1)S(1)}, bf16[384,128]{1,0:T(8,128)(2,1)S(1)}, u32[]{:S(2)}, u32[]{:S(2)}) collective-permute-start(bf16[384,128]{1,0:T(8,128)(2,1)S(1)} %get-tuple-element.51), channel_id=1, source_target_pairs={{0,6},{1,7},{2,4},{3,5},{4,2},{5,3},{6,0},{7,1},{8,14},{9,15},{10,... | collective-permute-start | bytes 294920 | tf_op jit(solution)/shard_map/ppermute | solution.py:408
  20.8 1.5 %collective-permute-start.6 = (bf16[768,128]{1,0:T(8,128)(2,1)S(1)}, bf16[768,128]{1,0:T(8,128)(2,1)S(1)}, u32[]{:S(2)}, u32[]{:S(2)}) collective-permute-start(bf16[768,128]{1,0:T(8,128)(2,1)S(1)} %pad_maximum_fusion.refs_2_), channel_id=1, source_target_pairs={{0,1},{1,0},{2,3},{3,2},{4,5},{5,4},{6,7},{7,6},{8,9},{9,8},{10,11... | collective-permute-start | bytes 589832 | tf_op jit(solution)/shard_map/ppermute | solution.py:408
  23.2 1.8 %collective-permute-start.7 = (f32[768,128]{1,0:T(8,128)S(1)}, f32[768,128]{1,0:T(8,128)S(1)}, u32[]{:S(2)}, u32[]{:S(2)}) collective-permute-start(f32[768,128]{1,0:T(8,128)S(1)} %shard_map.82.pressure_ref.own_ref), channel_id=1, source_target_pairs={{0,1},{1,0},{2,3},{3,2},{4,5},{5,4},{6,7},{7,6},{8,9},{9,8},{10,11... | collective-permute-start | bytes 1179656 | tf_op jit(solution)/shard_map/ppermute | solution.py:408
  26.8 1.2 %collective-permute-start.8 = (f32[64,128]{1,0:T(8,128)S(1)}, f32[64,128]{1,0:T(8,128)S(1)}, u32[]{:S(2)}, u32[]{:S(2)}) collective-permute-start(f32[64,128]{1,0:T(8,128)S(1)} %get-tuple-element.65), channel_id=1, source_target_pairs={{0,1},{1,0},{2,3},{3,2},{4,5},{5,4},{6,7},{7,6},{8,9},{9,8},{10,11... | collective-permute-start | bytes 98312 | tf_op jit(solution)/shard_map/ppermute | solution.py:408

commit v4 on v3

--- a/solution.py
+++ b/solution.py
@@ -102,13 +102,7 @@
 
 
 sine_terms = (4.442879676818848, -7.307816505432129, 3.5977742671966553, -0.7911993861198425)
-cosine_terms = (
-    -1.4142135381698608,
-    6.978850841522217,
-    -5.739460468292236,
-    1.883557915687561,
-    -0.3106880187988281,
-)
+cosine_terms = (1.4142040014266968, -6.97763729095459, 5.715188026428223, -1.728213906288147)
 turn_scale = wavenumber / (2.0 * math.pi)
 lanes = 128
 step_rows = 64
@@ -116,14 +110,14 @@
 remote = pl.BlockSpec(memory_space=pltpu.HBM)
 
 
-def call(kernel, outs, scratch, *args, cost=None, specs=None):
-    shapes = tuple(jax.ShapeDtypeStruct(shape, dtype) for shape, dtype in outs)
+def call(kernel, shapes, scratch, *args, cost=None, specs=None, outs=None):
+    shapes = tuple(jax.ShapeDtypeStruct(shape, dtype) for shape, dtype in shapes)
     return pl.pallas_call(
         kernel,
         out_shape=shapes,
         in_specs=specs or [whole] * len(args),
-        out_specs=(whole,) * len(shapes),
-        scratch_shapes=[entry if not isinstance(entry, tuple) else pltpu.VMEM(*entry) for entry in scratch],
+        out_specs=outs or (whole,) * len(shapes),
+        scratch_shapes=[pltpu.VMEM(*entry) if isinstance(entry, tuple) else entry for entry in scratch],
         compiler_params=pltpu.CompilerParams(vmem_limit_bytes=16 * 2**20),
         cost_estimate=cost,
     )(*args)
@@ -133,6 +127,18 @@
     total = jnp.float32(terms[-1])
     for term in terms[-2::-1]:
         total = jnp.float32(term) + value * total
+    return total
+
+
+def found_at(row_of, index, count):
+    high, low = index // lanes, index % lanes
+    total = None
+    for part in range(count):
+        row = row_of(part)
+        found = jnp.take_along_axis(
+            jnp.broadcast_to(row, index.shape), low, axis=1, mode="promise_in_bounds"
+        )
+        total = jnp.where(high == part, found, jnp.zeros_like(found) if total is None else total)
     return total
 
 
@@ -152,28 +158,29 @@
             source = 3 * panel_block + part
             found.append(halves[(source + at) % 2, pl.ds(source // 2, 1), :])
         ids[block : block + 1, :] = jnp.where(first_half, found[0], found[1])
+
+    def table(which):
+        if which < 3:
+            return lambda part: coords_ref[which : which + 1, part * lanes : (part + 1) * lanes]
+        source = areas_ref if which == 3 else weights_ref
+        return lambda part: source[part : part + 1, :]
+
     for group in range(ids.shape[0] // 8):
-        index = ids[8 * group : 8 * group + 8, :]
-        high, low = index // lanes, index % lanes
-        values = [jnp.zeros(index.shape, jnp.float32) for _ in range(5)]
-        for part in range(areas_ref.shape[0]):
-            chosen = high == part
-            rows = [coords_ref[axis : axis + 1, part * lanes : (part + 1) * lanes] for axis in range(3)]
-            rows += [areas_ref[part : part + 1, :], weights_ref[part : part + 1, :]]
-            for which, row in enumerate(rows):
-                found = jnp.take_along_axis(
-                    jnp.broadcast_to(row, index.shape), low, axis=1, mode="promise_in_bounds"
-                )
-                values[which] = jnp.where(chosen, found, values[which])
-        for which, value in enumerate(values):
-            along[which, 8 * group : 8 * group + 8, :] = value
-            if which < 3:
-                value = value * jnp.float32(turn_scale)
-            down[which, :, 8 * group : 8 * group + 8] = jnp.transpose(value)
+        rows = slice(8 * group, 8 * group + 8)
+        for which in range(4):
+            along[which, rows, :] = found_at(table(which), ids[rows, :], blocks)
+    shape = (8, lanes)
+    place = lax.broadcasted_iota(jnp.int32, shape, 0) * lanes + lax.broadcasted_iota(jnp.int32, shape, 1)
+    each = blocks * lanes // 32
+    block = ((place.astype(jnp.float32) + jnp.float32(0.5)) * jnp.float32(1.0 / each)).astype(jnp.int32)
+    index = found_at(lambda part: order_ref[part : part + 1, :], place + each * (block + core), blocks)
+    for at, which in enumerate((0, 1, 2, 4)):
+        value = found_at(table(which), index, blocks)
+        down[at] = jnp.transpose(value * jnp.float32(turn_scale) if which < 3 else value)
 
 
 def spread_rows(down_ref, rows_ref, first):
-    for which in range(4):
+    for which in range(3):
         for block in range(rows_ref.shape[1] // lanes):
             at = first + block
             rows_ref[which, block * lanes : (block + 1) * lanes, :] = jnp.broadcast_to(
@@ -181,11 +188,10 @@
             )
 
 
-def fill_green(rows_ref, columns_ref, norm_const, forward_ref, adjoint_ref):
+def fill_green(rows_ref, columns_ref, tile_ref):
     def fill(step, carry):
         rows = pl.ds(pl.multiple_of(step * step_rows, step_rows), step_rows)
-        row_x, row_y, row_z, row_area = [rows_ref[which, rows, :] for which in range(4)]
-        row_area = row_area * jnp.float32(turn_scale / norm_const)
+        row_x, row_y, row_z = [rows_ref[which, rows, :] for which in range(3)]
         for part in range(columns_ref.shape[2] // lanes):
             columns = slice(part * lanes, (part + 1) * lanes)
             col_x, col_y, col_z, col_area = [
@@ -196,18 +202,16 @@
             square = square + (offset_z * offset_z + jnp.float32((smoothing * turn_scale) ** 2))
             inverse = lax.rsqrt(square)
             turns = square * inverse
-            half_turn = turns - jnp.floor(turns) - jnp.float32(0.5)
+            half_turn = turns - jnp.round(turns)
             power = half_turn * half_turn
             sine = half_turn * horner(sine_terms, power)
-            cosine = horner(cosine_terms, power)
-            for out_ref, area in ((forward_ref, col_area), (adjoint_ref, row_area)):
-                factor = inverse * area
-                scaled = sine * factor
-                out_ref[0, rows, columns] = (scaled * sine - factor).astype(jnp.bfloat16)
-                out_ref[1, rows, columns] = (scaled * cosine).astype(jnp.bfloat16)
+            factor = inverse * col_area
+            scaled = sine * factor
+            tile_ref[0, rows, columns] = (factor - scaled * sine).astype(jnp.bfloat16)
+            tile_ref[1, rows, columns] = (scaled * horner(cosine_terms, power)).astype(jnp.bfloat16)
         return carry
 
-    lax.fori_loop(0, forward_ref.shape[1] // step_rows, fill, 0)
+    lax.fori_loop(0, tile_ref.shape[1] // step_rows, fill, 0)
 
 
 def first_tile_kernel(
@@ -216,8 +220,7 @@
     coords_ref,
     areas_ref,
     weights_ref,
-    forward_ref,
-    adjoint_ref,
+    tile_ref,
     columns_ref,
     down_ref,
     halves,
@@ -233,17 +236,17 @@
                 along[which, block : block + 1, :] * scale, (8, lanes)
             )
     spread_rows(down_ref, rows_ref, 0)
-    fill_green(rows_ref, columns_ref, norm_const, forward_ref, adjoint_ref)
-
-
-def next_tile_kernel(norm_const, first, columns_ref, down_ref, forward_ref, adjoint_ref, rows_ref):
+    fill_green(rows_ref, columns_ref, tile_ref)
+
+
+def next_tile_kernel(first, columns_ref, down_ref, tile_ref, rows_ref):
     spread_rows(down_ref, rows_ref, first // lanes)
-    fill_green(rows_ref, columns_ref, norm_const, forward_ref, adjoint_ref)
+    fill_green(rows_ref, columns_ref, tile_ref)
 
 
 def tile_cost(row_count, panels):
     pairs = row_count * panels
-    return pl.CostEstimate(flops=40 * pairs, bytes_accessed=8 * pairs, transcendentals=3 * pairs)
+    return pl.CostEstimate(flops=40 * pairs, bytes_accessed=4 * pairs, transcendentals=3 * pairs)
 
 
 def first_tile(order, coords, areas, weights, norm_const, row_count):
@@ -254,15 +257,14 @@
         functools.partial(first_tile_kernel, norm_const),
         (
             ((2, row_count, panels), jnp.bfloat16),
-            ((2, row_count, panels), jnp.bfloat16),
             ((4, 8, panels), jnp.float32),
-            ((5, lanes, padded), jnp.float32),
+            ((4, lanes, 8), jnp.float32),
         ),
         (
             ((2, padded, lanes), jnp.int32),
             ((padded, lanes), jnp.int32),
-            ((5, padded, lanes), jnp.float32),
-            ((4, -(-row_count // lanes) * lanes, lanes), jnp.float32),
+            ((4, padded, lanes), jnp.float32),
+            ((3, row_count, lanes), jnp.float32),
         ),
         order,
         coords,
@@ -272,16 +274,16 @@
     )
 
 
-def next_tile(columns, down, norm_const, first, row_count):
+def next_tile(columns, down, first, row_count):
     panels = columns.shape[2]
     return call(
-        functools.partial(next_tile_kernel, norm_const, first),
-        (((2, row_count, panels), jnp.bfloat16),) * 2,
-        (((4, row_count, lanes), jnp.float32),),
+        functools.partial(next_tile_kernel, first),
+        (((2, row_count, panels), jnp.bfloat16),),
+        (((3, row_count, lanes), jnp.float32),),
         columns,
         down,
         cost=tile_cost(row_count, panels),
-    )
+    )[0]
 
 
 def load_kernel(*refs):
@@ -342,66 +344,64 @@
     ) + jnp.dot(tile_ref[1, :, columns], turned(value, sign), preferred_element_type=jnp.float32)
 
 
-def pressure_kernel(side, *refs):
-    tile_refs, value_ref, out_ref = refs[:2], refs[2], refs[-1]
-    half = value_ref.shape[0]
-    columns = slice(side * half, (side + 1) * half)
+def tiles_dot(tile_refs, columns, value, sign, store):
     first = 0
     for tile_ref in tile_refs:
         rows = slice(first, first + tile_ref.shape[1])
-        term = tile_dot(tile_ref, columns, value_ref[...], 1)
-        out_ref[rows, :] = term if side == 0 else refs[3][rows, :] + term
+        store(rows, tile_dot(tile_ref, columns, value, sign))
         first = rows.stop
 
 
-def sources(pressure_ref, down_ref, side):
-    count = pressure_ref.shape[0] // lanes
-    parts = []
-    for block in range(count):
-        at = side * count + block
-        weight = down_ref[4, :, at : at + 1]
-        parts.append((pressure_ref[block * lanes : (block + 1) * lanes, :] * weight).astype(jnp.bfloat16))
-    return jnp.concatenate(parts, 0)
-
-
-def own_adjoint_kernel(first_ref, second_ref, pressure_ref, down_ref, out_ref):
-    half = pressure_ref.shape[0]
-    value = sources(pressure_ref, down_ref, 0)
+def own_pressure_kernel(first_ref, second_ref, value_ref, down_ref, out_ref, weight_ref):
+    half = value_ref.shape[0]
+
+    def store(rows, term):
+        out_ref[rows, :] = term
+
+    tiles_dot((first_ref, second_ref), slice(0, half), value_ref[...], 1, store)
+    for block in range(weight_ref.shape[0] // lanes):
+        weight_ref[block * lanes : (block + 1) * lanes, :] = jnp.broadcast_to(
+            down_ref[3, :, block : block + 1], (lanes, lanes)
+        )
+
+
+def other_pressure_kernel(first_ref, second_ref, value_ref, term_ref, out_ref):
+    half = value_ref.shape[0]
+
+    def store(rows, term):
+        out_ref[rows, :] = term_ref[rows, :] + term
+
+    tiles_dot((first_ref, second_ref), slice(half, 2 * half), value_ref[...], 1, store)
+
+
+def modal_kernel(first_ref, second_ref, value_ref, weight_ref, own_ref, other_ref, *refs):
+    kept_ref, sent_ref, pressure_ref, sem = refs
+    col = lax.axis_index("col")
+    each = pressure_ref.shape[0]
+    block = (lax.axis_index("row") * lax.axis_size("col") + col) // 2
+    rows = pl.ds(pl.multiple_of(block * each, each), each)
+    copy = pltpu.make_async_copy(value_ref.at[rows, :], pressure_ref, sem)
+    copy.start()
+    source = (value_ref[...] * weight_ref[...]).astype(jnp.bfloat16)
+    across, turned_across = jnp.transpose(source), jnp.transpose(turned(source, -1))
+    sensitivity = None
     first = 0
     for tile_ref in (first_ref, second_ref):
-        rows = slice(first, first + tile_ref.shape[1])
-        out_ref[rows, :] = tile_dot(tile_ref, slice(0, half), value, -1)
-        first = rows.stop
-
-
-def modal_kernel(first_ref, second_ref, own_ref, other_ref, down_ref, term_ref, *refs):
-    modes_refs, (kept_ref, sent_ref, pressure_ref, sensitivity) = refs[:4], refs[4:]
-    row = lax.axis_index("row")
-    col = lax.axis_index("col")
-    chip, core = col // 2, col % 2
+        targets = slice(first, first + tile_ref.shape[1])
+        first = targets.stop
+        for part, value in enumerate((across, turned_across)):
+            term = jnp.dot(value[:, targets], tile_ref[part], preferred_element_type=jnp.float32)
+            sensitivity = term if sensitivity is None else sensitivity + term
+    sensitivity = sensitivity.astype(jnp.bfloat16)
     half = own_ref.shape[0]
-    count = half // 4
-    value = sources(other_ref, down_ref, 1)
-    first = 0
-    for tile_ref in (first_ref, second_ref):
-        rows = slice(first, first + tile_ref.shape[1])
-        term = term_ref[rows, :] + tile_dot(tile_ref, slice(half, 2 * half), value, -1)
-        sensitivity[rows, :] = term.astype(jnp.bfloat16)
-        first = rows.stop
-    modes = jnp.concatenate([modes_ref[count:, :] for modes_ref in modes_refs], 0)
-    modal = lax.dot_general(
-        modes, sensitivity[...], (((0,), (0,)), ((), ())), preferred_element_type=jnp.float32
-    )
+    modal = jnp.dot(sensitivity[:, :half], own_ref[...], preferred_element_type=jnp.float32)
+    modal = modal + jnp.dot(sensitivity[:, half:], other_ref[...], preferred_element_type=jnp.float32)
+    modal = jnp.transpose(modal)
     modes_each = kept_ref.shape[0]
     low, high = modal[:modes_each, :], modal[modes_each:, :]
-    kept_ref[...] = jnp.where(core == 0, low, high)
-    sent_ref[...] = jnp.where(core == 0, high, low)
-    each = pressure_ref.shape[0]
-    per_block = count // each
-    panel_block = 2 * row + col // per_block
-    first = (panel_block // 2 ^ chip) * count + col % per_block * each
-    rows = pl.ds(pl.multiple_of(first, each), each)
-    pressure_ref[...] = jnp.where(panel_block % 2 == core, own_ref[rows, :], other_ref[rows, :])
+    kept_ref[...] = jnp.where(col % 2 == 0, low, high)
+    sent_ref[...] = jnp.where(col % 2 == 0, high, low)
+    copy.wait()
 
 
 def swap(value, axis, mask):
@@ -423,24 +423,27 @@
         areas.reshape(wide),
         weights.reshape(wide),
     )
-    received = [swap(sent, "row", mask) for mask in (1, 2, 3)]
+    received = [swap(sent, "row", mask) for mask in (3, 2, 1)]
     tiles = first_tile(order, coords, areas, weights, norm_const, part_rows)
     received, tiles = lax.optimization_barrier((received, tiles))
-    tile, own_tile, columns, down = tiles
+    tile, columns, down = tiles
     joined = call(
         join_kernel, (((2 * own_rows, load_columns), jnp.bfloat16),) * 4, (), terms, *received, modes
     )
     received = [swap(value, "col", 2 * mask) for mask, value in zip((1, 2, 3), joined[1:])]
-    tiles = next_tile(columns, down, norm_const, part_rows, half - part_rows)
-    received, (last_tile, last_own_tile) = lax.optimization_barrier((received, tiles))
+    last_tile = next_tile(columns, down, part_rows, half - part_rows)
+    received, last_tile = lax.optimization_barrier((received, last_tile))
     joined = [joined[0], *received]
     own = jnp.concatenate([value[:own_rows] for value in joined], 0)
     other = swap(own, "col", 1)
-    out = (((half, load_columns), jnp.float32),)
-    term = call(functools.partial(pressure_kernel, 0), out, (), tile, last_tile, own)[0]
-    pressure = call(functools.partial(pressure_kernel, 1), out, (), tile, last_tile, other, term)[0]
-    other = swap(pressure, "col", 1)
-    term = call(own_adjoint_kernel, out, (), own_tile, last_own_tile, pressure, down)[0]
+    out = ((half, load_columns), jnp.float32)
+    term, weight = call(
+        own_pressure_kernel, (out, ((half, lanes), jnp.float32)), (), tile, last_tile, own, down
+    )
+    modes = jnp.concatenate([value[own_rows:] for value in joined], 0)
+    modes, term = lax.optimization_barrier((modes, term))
+    other_modes = swap(modes, "col", 1)
+    pressure = call(other_pressure_kernel, (out,), (), tile, last_tile, other, term)[0]
     modes_each = mode_shapes.shape[1] // 8
     kept, sent, own_pressure = call(
         modal_kernel,
@@ -449,14 +452,14 @@
             ((modes_each, load_columns), jnp.float32),
             ((own_rows // lax.axis_size("row"), load_columns), jnp.float32),
         ),
-        (((half, load_columns), jnp.bfloat16),),
-        own_tile,
-        last_own_tile,
+        (pltpu.SemaphoreType.DMA,),
+        tile,
+        last_tile,
         pressure,
-        other,
-        down,
-        term,
-        *joined,
+        weight,
+        modes,
+        other_modes,
+        outs=(whole, whole, remote),
     )
     return (own_pressure, kept + swap(sent, "col", 1))
 

time: 28.7 us -> 26.9 us (0.937)
  Pallas kernels: 14.2 us -> 11 us
  waiting for transfers between devices: 3.25 us -> 3.95 us
  starting transfers between devices: 9.72 us -> 10.4 us
    pallas_call x8 -> x7, Pallas kernels: 14.2 us -> 11 us  [call(): pl.pallas_call(kernel, out_shape=shapes, in_specs=specs or [whole] * len(...]
    ppermute x9, waiting for transfers between devices: 3.25 us -> 3.95 us  [swap(): lax.ppermute(value, axis, [(i, i ^ mask) for i in range(lax.axis_size(axi...]
    ppermute x9, starting transfers between devices: 9.72 us -> 10.4 us  [swap(): lax.ppermute(value, axis, [(i, i ^ mask) for i in range(lax.axis_size(axi...]
  transfers between devices with their start and end apart: 9 -> 9, of which waited for: 4 -> 4; matrix products, arithmetic and copies ran while one was open for 0% -> 0% of each run, Pallas kernels for 36% -> 31%
where the time goes in v4:
time: 26.9 us; the launch traced here: 26.8 us
  Pallas kernels  11 us (41%)
  starting transfers between devices  10.4 us (39%)
  waiting for transfers between devices  3.95 us (15%)
  between operations  0.75 us (3%)
  other arithmetic  0.65 us (2%)
    pallas_call x7, Pallas kernels, call(): pl.pallas_call(kernel, out_shape=shapes, in_specs=specs or [whole] * len(...  11 us
    ppermute x9, starting transfers between devices, swap(): lax.ppermute(value, axis, [(i, i ^ mask) for i in range(lax.axis_size(axi...  10.4 us
    ppermute x9, waiting for transfers between devices, swap(): lax.ppermute(value, axis, [(i, i ^ mask) for i in range(lax.axis_size(axi...  3.95 us
    add x1, other arithmetic, local(): return (own_pressure, kept + swap(sent, 'col', 1))  0.62 us
  transfers between devices with their start and end apart: 9, of which 4 were waited for; matrix products, arithmetic and copies ran while one was open for 0% of the time, Pallas kernels for 31%

profile of v4, /device:TPU:0, one launch (start us, length us, event | category | flops | bytes accessed | tf_op | source)
XLA Modules:
  0.0 26.8 jit_solution(2960716769644229272)
XLA Ops:
  0.6 1.2 %shard_map.77 = (bf16[192,512]{1,0:T(8,128)(2,1)S(1)}, s32[12,128]{1,0:T(8,128)S(1)}, f32[3,1536]{1,0:T(4,128)S(1)}, f32[12,128]{1,0:T(8,128)S(1)}, f32[12,128]{...) custom-call(bf16[512,128]{1,0:T(8,128)(2,1)} %refs_0_.1, bf16[192,512]{1,0:T(8,128)(2,1)} %refs_1_.1, ...), custom_call_target="tpu_custom_call" | custom-call | tf_op jit(solution)/shard_map/pallas_call | solution.py:115
  1.9 5.1 %collective-permute-start = (bf16[192,128]{1,0:T(8,128)(2,1)S(1)}, bf16[192,128]{1,0:T(8,128)(2,1)S(1)}, u32[]{:S(2)}, u32[]{:S(2)}) collective-permute-start(bf16[192,128]{1,0:T(8,128)(2,1)S(1)} %get-tuple-element.33), channel_id=1, source_target_pairs={{0,24},{8,16},{16,8},{24,0},{1,25},{9,17},{17,9},{25,1},{2,26},{10... | collective-permute-start | bytes 147464 | tf_op jit(solution)/shard_map/ppermute | solution.py:408
  7.0 0.0 collective-permute-start.1
  7.0 0.6 %collective-permute-start.2 = (bf16[192,128]{1,0:T(8,128)(2,1)S(1)}, bf16[192,128]{1,0:T(8,128)(2,1)S(1)}, u32[]{:S(2)}, u32[]{:S(2)}) collective-permute-start(bf16[192,128]{1,0:T(8,128)(2,1)S(1)} %get-tuple-element.33), channel_id=1, source_target_pairs={{0,8},{8,0},{16,24},{24,16},{1,9},{9,1},{17,25},{25,17},{2,10},{10... | collective-permute-start | bytes 147464 | tf_op jit(solution)/shard_map/ppermute | solution.py:408
  7.6 2.6 %shard_map.78 = (bf16[2,256,1536]{2,1,0:T(8,128)(2,1)S(1)}, f32[4,8,1536]{2,1,0:T(8,128)S(1)}, f32[4,128,8]{2,1,0:T(8,128)S(1)}) custom-call(s32[12,128]{1,0:T(8,128)S(1)} %get-tuple-element.34.order_ref, f32[3,1536]{1,0:T(4,128)S(1)} %get-tuple-element.35.coords_ref, f32[12,128]{1,0:T(8,128)S(1)} %get-tuple-element.36.areas_ref, ...), custom_call_target="tpu_custom_call" | custom-call | flops 15728640 | bytes 1572864 | tf_op jit(solution)/shard_map/pallas_call | solution.py:115
  10.3 0.0 collective-permute-done.first_ref
  10.3 1.7 %collective-permute-done.1.second_ref = bf16[192,128]{1,0:T(8,128)(2,1)S(1)} collective-permute-done((bf16[192,128]{1,0:T(8,128)(2,1)S(1)}, bf16[192,128]{1,0:T(8,128)(2,1)S(1)}, u32[]{:S(2)}, u32[]{:S(2)}) %collective-permute-start.1) | collective-permute-done | bytes 49184 | tf_op jit(solution)/shard_map/ppermute | solution.py:408
  12.0 0.0 collective-permute-done.2.third_ref
  12.0 0.1 shard_map.79
  12.1 1.6 %collective-permute-start.3 = (bf16[384,128]{1,0:T(8,128)(2,1)S(1)}, bf16[384,128]{1,0:T(8,128)(2,1)S(1)}, u32[]{:S(2)}, u32[]{:S(2)}) collective-permute-start(bf16[384,128]{1,0:T(8,128)(2,1)S(1)} %get-tuple-element.47), channel_id=1, source_target_pairs={{0,2},{1,3},{2,0},{3,1},{4,6},{5,7},{6,4},{7,5},{8,10},{9,11},{10,... | collective-permute-start | bytes 294920 | tf_op jit(solution)/shard_map/ppermute | solution.py:408
  13.6 1.5 %collective-permute-start.4 = (bf16[384,128]{1,0:T(8,128)(2,1)S(1)}, bf16[384,128]{1,0:T(8,128)(2,1)S(1)}, u32[]{:S(2)}, u32[]{:S(2)}) collective-permute-start(bf16[384,128]{1,0:T(8,128)(2,1)S(1)} %get-tuple-element.48), channel_id=1, source_target_pairs={{0,4},{1,5},{2,6},{3,7},{4,0},{5,1},{6,2},{7,3},{8,12},{9,13},{10,... | collective-permute-start | bytes 294920 | tf_op jit(solution)/shard_map/ppermute | solution.py:408
  15.1 0.5 %collective-permute-start.5 = (bf16[384,128]{1,0:T(8,128)(2,1)S(1)}, bf16[384,128]{1,0:T(8,128)(2,1)S(1)}, u32[]{:S(2)}, u32[]{:S(2)}) collective-permute-start(bf16[384,128]{1,0:T(8,128)(2,1)S(1)} %get-tuple-element.49), channel_id=1, source_target_pairs={{0,6},{1,7},{2,4},{3,5},{4,2},{5,3},{6,0},{7,1},{8,14},{9,15},{10,... | collective-permute-start | bytes 294920 | tf_op jit(solution)/shard_map/ppermute | solution.py:408
  15.6 3.8 %shard_map.80.second_ref = bf16[2,512,1536]{2,1,0:T(8,128)(2,1)S(1)} custom-call(f32[4,8,1536]{2,1,0:T(8,128)S(1)} %get-tuple-element.50.columns_ref, f32[4,128,8]{2,1,0:T(8,128)S(1)} %get-tuple-element.51.down_ref), custom_call_target="tpu_custom_call" | custom-call | flops 31457280 | bytes 3145728 | tf_op jit(solution)/shard_map/pallas_call | solution.py:115
  19.4 0.0 collective-permute-done.3
  19.5 0.0 collective-permute-done.4
  19.5 1.2 %collective-permute-done.5 = bf16[384,128]{1,0:T(8,128)(2,1)S(1)} collective-permute-done((bf16[384,128]{1,0:T(8,128)(2,1)S(1)}, bf16[384,128]{1,0:T(8,128)(2,1)S(1)}, u32[]{:S(2)}, u32[]{:S(2)}) %collective-permute-start.5) | collective-permute-done | bytes 98336 | tf_op jit(solution)/shard_map/ppermute | solution.py:408
  20.7 0.1 collective-permute-start.6
  20.8 0.9 %shard_map.81 = (f32[768,128]{1,0:T(8,128)S(1)}, f32[768,128]{1,0:T(8,128)S(1)}) custom-call(bf16[2,256,1536]{2,1,0:T(8,128)(2,1)S(1)} %get-tuple-element.41.first_ref, bf16[2,512,1536]{2,1,0:T(8,128)(2,1)S(1)} %shard_map.80.second_ref, bf16[768,128]{1,0:T(8,128)(2,1)S(1)} %pad_maximum_fusion.value_ref, f32[4,128,8]{2,1,0:T(8,128)S(1)} %get-tuple-element.51.down_ref), custom_call_target="tpu_custom_call" | custom-call | tf_op jit(solution)/shard_map/pallas_call | solution.py:115
  21.7 0.6 %collective-permute-start.7 = (bf16[768,128]{1,0:T(8,128)(2,1)S(1)}, bf16[768,128]{1,0:T(8,128)(2,1)S(1)}, u32[]{:S(2)}, u32[]{:S(2)}) collective-permute-start(bf16[768,128]{1,0:T(8,128)(2,1)S(1)} %pad_maximum_fusion.1.own_ref), channel_id=1, source_target_pairs={{0,1},{1,0},{2,3},{3,2},{4,5},{5,4},{6,7},{7,6},{8,9},{9,8},{10,11... | collective-permute-start | bytes 589832 | tf_op jit(solution)/shard_map/ppermute | solution.py:408
  22.3 0.0 collective-permute-done.6.value_ref
  22.3 0.9 %shard_map.82.value_ref = f32[768,128]{1,0:T(8,128)S(1)} custom-call(bf16[2,256,1536]{2,1,0:T(8,128)(2,1)S(1)} %get-tuple-element.41.first_ref, bf16[2,512,1536]{2,1,0:T(8,128)(2,1)S(1)} %shard_map.80.second_ref, bf16[768,128]{1,0:T(8,128)(2,1)S(1)} %collective-permute-done.6.value_ref, f32[768,128]{1,0:T(8,128)S(1)} %get-tuple-element.58.term_ref), custom_call_target="tpu_custom_call" | custom-call | tf_op jit(solution)/shard_map/pallas_call | solution.py:115
  23.1 0.2 collective-permute-done.7.other_ref
  23.3 1.5 %shard_map.83 = (f32[64,128]{1,0:T(8,128)S(1)}, f32[64,128]{1,0:T(8,128)S(1)}, f32[48,128]{1,0:T(8,128)}) custom-call(bf16[2,256,1536]{2,1,0:T(8,128)(2,1)S(1)} %get-tuple-element.41.first_ref, bf16[2,512,1536]{2,1,0:T(8,128)(2,1)S(1)} %shard_map.80.second_ref, f32[768,128]{1,0:T(8,128)S(1)} %shard_map.82.value_ref, ...), custom_call_target="tpu_custom_call" | custom-call | tf_op jit(solution)/shard_map/pallas_call | solution.py:115
  24.9 0.4 %collective-permute-start.8 = (f32[64,128]{1,0:T(8,128)S(1)}, f32[64,128]{1,0:T(8,128)S(1)}, u32[]{:S(2)}, u32[]{:S(2)}) collective-permute-start(f32[64,128]{1,0:T(8,128)S(1)} %get-tuple-element.63), channel_id=1, source_target_pairs={{0,1},{1,0},{2,3},{3,2},{4,5},{5,4},{6,7},{7,6},{8,9},{9,8},{10,11... | collective-permute-start | bytes 98312 | tf_op jit(solution)/shard_map/ppermute | solution.py:408
  25.3 0.9 %collective-permute-done.8 = f32[64,128]{1,0:T(8,128)S(1)} collective-permute-done((f32[64,128]{1,0:T(8,128)S(1)}, f32[64,128]{1,0:T(8,128)S(1)}, u32[]{:S(2)}, u32[]{:S(2)}) %collective-permute-start.8) | collective-permute-done | bytes 32800 | tf_op jit(solution)/shard_map/ppermute | solution.py:408
  26.2 0.6 %add.3 = f32[64,128]{1,0:T(8,128)} add(f32[64,128]{1,0:T(8,128)S(1)} %get-tuple-element.62, f32[64,128]{1,0:T(8,128)S(1)} %collective-permute-done.8) | non-fusion elementwise | flops 8192 | bytes 98304 | tf_op jit(solution)/shard_map/add | solution.py:464
  (5 shorter events, 0.1 us)
Async XLA Ops:
  1.9 8.4 %collective-permute-start = (bf16[192,128]{1,0:T(8,128)(2,1)S(1)}, bf16[192,128]{1,0:T(8,128)(2,1)S(1)}, u32[]{:S(2)}, u32[]{:S(2)}) collective-permute-start(bf16[192,128]{1,0:T(8,128)(2,1)S(1)} %get-tuple-element.33), channel_id=1, source_target_pairs={{0,24},{8,16},{16,8},{24,0},{1,25},{9,17},{17,9},{25,1},{2,26},{10... | collective-permute-start | bytes 147464 | tf_op jit(solution)/shard_map/ppermute | solution.py:408
  7.0 5.0 %collective-permute-start.1 = (bf16[192,128]{1,0:T(8,128)(2,1)S(1)}, bf16[192,128]{1,0:T(8,128)(2,1)S(1)}, u32[]{:S(2)}, u32[]{:S(2)}) collective-permute-start(bf16[192,128]{1,0:T(8,128)(2,1)S(1)} %get-tuple-element.33), channel_id=1, source_target_pairs={{0,16},{8,24},{16,0},{24,8},{1,17},{9,25},{17,1},{25,9},{2,18},{10... | collective-permute-start | bytes 147464 | tf_op jit(solution)/shard_map/ppermute | solution.py:408
  7.0 5.0 %collective-permute-start.2 = (bf16[192,128]{1,0:T(8,128)(2,1)S(1)}, bf16[192,128]{1,0:T(8,128)(2,1)S(1)}, u32[]{:S(2)}, u32[]{:S(2)}) collective-permute-start(bf16[192,128]{1,0:T(8,128)(2,1)S(1)} %get-tuple-element.33), channel_id=1, source_target_pairs={{0,8},{8,0},{16,24},{24,16},{1,9},{9,1},{17,25},{25,17},{2,10},{10... | collective-permute-start | bytes 147464 | tf_op jit(solution)/shard_map/ppermute | solution.py:408
  12.1 7.4 %collective-permute-start.3 = (bf16[384,128]{1,0:T(8,128)(2,1)S(1)}, bf16[384,128]{1,0:T(8,128)(2,1)S(1)}, u32[]{:S(2)}, u32[]{:S(2)}) collective-permute-start(bf16[384,128]{1,0:T(8,128)(2,1)S(1)} %get-tuple-element.47), channel_id=1, source_target_pairs={{0,2},{1,3},{2,0},{3,1},{4,6},{5,7},{6,4},{7,5},{8,10},{9,11},{10,... | collective-permute-start | bytes 294920 | tf_op jit(solution)/shard_map/ppermute | solution.py:408
  13.6 5.8 %collective-permute-start.4 = (bf16[384,128]{1,0:T(8,128)(2,1)S(1)}, bf16[384,128]{1,0:T(8,128)(2,1)S(1)}, u32[]{:S(2)}, u32[]{:S(2)}) collective-permute-start(bf16[384,128]{1,0:T(8,128)(2,1)S(1)} %get-tuple-element.48), channel_id=1, source_target_pairs={{0,4},{1,5},{2,6},{3,7},{4,0},{5,1},{6,2},{7,3},{8,12},{9,13},{10,... | collective-permute-start | bytes 294920 | tf_op jit(solution)/shard_map/ppermute | solution.py:408
  15.1 5.5 %collective-permute-start.5 = (bf16[384,128]{1,0:T(8,128)(2,1)S(1)}, bf16[384,128]{1,0:T(8,128)(2,1)S(1)}, u32[]{:S(2)}, u32[]{:S(2)}) collective-permute-start(bf16[384,128]{1,0:T(8,128)(2,1)S(1)} %get-tuple-element.49), channel_id=1, source_target_pairs={{0,6},{1,7},{2,4},{3,5},{4,2},{5,3},{6,0},{7,1},{8,14},{9,15},{10,... | collective-permute-start | bytes 294920 | tf_op jit(solution)/shard_map/ppermute | solution.py:408
  20.7 1.6 %collective-permute-start.6 = (bf16[768,128]{1,0:T(8,128)(2,1)S(1)}, bf16[768,128]{1,0:T(8,128)(2,1)S(1)}, u32[]{:S(2)}, u32[]{:S(2)}) collective-permute-start(bf16[768,128]{1,0:T(8,128)(2,1)S(1)} %pad_maximum_fusion.value_ref), channel_id=1, source_target_pairs={{0,1},{1,0},{2,3},{3,2},{4,5},{5,4},{6,7},{7,6},{8,9},{9,8},{10,11... | collective-permute-start | bytes 589832 | tf_op jit(solution)/shard_map/ppermute | solution.py:408
  21.7 1.6 %collective-permute-start.7 = (bf16[768,128]{1,0:T(8,128)(2,1)S(1)}, bf16[768,128]{1,0:T(8,128)(2,1)S(1)}, u32[]{:S(2)}, u32[]{:S(2)}) collective-permute-start(bf16[768,128]{1,0:T(8,128)(2,1)S(1)} %pad_maximum_fusion.1.own_ref), channel_id=1, source_target_pairs={{0,1},{1,0},{2,3},{3,2},{4,5},{5,4},{6,7},{7,6},{8,9},{9,8},{10,11... | collective-permute-start | bytes 589832 | tf_op jit(solution)/shard_map/ppermute | solution.py:408
  24.9 1.3 %collective-permute-start.8 = (f32[64,128]{1,0:T(8,128)S(1)}, f32[64,128]{1,0:T(8,128)S(1)}, u32[]{:S(2)}, u32[]{:S(2)}) collective-permute-start(f32[64,128]{1,0:T(8,128)S(1)} %get-tuple-element.63), channel_id=1, source_target_pairs={{0,1},{1,0},{2,3},{3,2},{4,5},{5,4},{6,7},{7,6},{8,9},{9,8},{10,11... | collective-permute-start | bytes 98312 | tf_op jit(solution)/shard_map/ppermute | solution.py:408

commit v5 on v4

--- a/solution.py
+++ b/solution.py
@@ -110,7 +110,7 @@
 remote = pl.BlockSpec(memory_space=pltpu.HBM)
 
 
-def call(kernel, shapes, scratch, *args, cost=None, specs=None, outs=None):
+def call(kernel, shapes, scratch, *args, cost=None, specs=None, outs=None, aliases=None):
     shapes = tuple(jax.ShapeDtypeStruct(shape, dtype) for shape, dtype in shapes)
     return pl.pallas_call(
         kernel,
@@ -120,6 +120,7 @@
         scratch_shapes=[pltpu.VMEM(*entry) if isinstance(entry, tuple) else entry for entry in scratch],
         compiler_params=pltpu.CompilerParams(vmem_limit_bytes=16 * 2**20),
         cost_estimate=cost,
+        input_output_aliases=aliases or {},
     )(*args)
 
 
@@ -188,9 +189,10 @@
             )
 
 
-def fill_green(rows_ref, columns_ref, tile_ref):
+def fill_green(rows_ref, columns_ref, tile_ref, first):
     def fill(step, carry):
         rows = pl.ds(pl.multiple_of(step * step_rows, step_rows), step_rows)
+        out_rows = pl.ds(pl.multiple_of(first + step * step_rows, step_rows), step_rows)
         row_x, row_y, row_z = [rows_ref[which, rows, :] for which in range(3)]
         for part in range(columns_ref.shape[2] // lanes):
             columns = slice(part * lanes, (part + 1) * lanes)
@@ -207,11 +209,11 @@
             sine = half_turn * horner(sine_terms, power)
             factor = inverse * col_area
             scaled = sine * factor
-            tile_ref[0, rows, columns] = (factor - scaled * sine).astype(jnp.bfloat16)
-            tile_ref[1, rows, columns] = (scaled * horner(cosine_terms, power)).astype(jnp.bfloat16)
+            tile_ref[0, out_rows, columns] = (factor - scaled * sine).astype(jnp.bfloat16)
+            tile_ref[1, out_rows, columns] = (scaled * horner(cosine_terms, power)).astype(jnp.bfloat16)
         return carry
 
-    lax.fori_loop(0, tile_ref.shape[1] // step_rows, fill, 0)
+    lax.fori_loop(0, rows_ref.shape[1] // step_rows, fill, 0)
 
 
 def first_tile_kernel(
@@ -236,12 +238,12 @@
                 along[which, block : block + 1, :] * scale, (8, lanes)
             )
     spread_rows(down_ref, rows_ref, 0)
-    fill_green(rows_ref, columns_ref, tile_ref)
-
-
-def next_tile_kernel(first, columns_ref, down_ref, tile_ref, rows_ref):
+    fill_green(rows_ref, columns_ref, tile_ref, 0)
+
+
+def next_tile_kernel(first, columns_ref, down_ref, filled_ref, tile_ref, rows_ref):
     spread_rows(down_ref, rows_ref, first // lanes)
-    fill_green(rows_ref, columns_ref, tile_ref)
+    fill_green(rows_ref, columns_ref, tile_ref, first)
 
 
 def tile_cost(row_count, panels):
@@ -256,7 +258,7 @@
     return call(
         functools.partial(first_tile_kernel, norm_const),
         (
-            ((2, row_count, panels), jnp.bfloat16),
+            ((2, panels // 2, panels), jnp.bfloat16),
             ((4, 8, panels), jnp.float32),
             ((4, lanes, 8), jnp.float32),
         ),
@@ -274,15 +276,17 @@
     )
 
 
-def next_tile(columns, down, first, row_count):
-    panels = columns.shape[2]
+def next_tile(columns, down, tile, first):
+    row_count, panels = tile.shape[1] - first, tile.shape[2]
     return call(
         functools.partial(next_tile_kernel, first),
-        (((2, row_count, panels), jnp.bfloat16),),
+        ((tile.shape, jnp.bfloat16),),
         (((3, row_count, lanes), jnp.float32),),
         columns,
         down,
+        tile,
         cost=tile_cost(row_count, panels),
+        aliases={2: 0},
     )[0]
 
 
@@ -344,55 +348,27 @@
     ) + jnp.dot(tile_ref[1, :, columns], turned(value, sign), preferred_element_type=jnp.float32)
 
 
-def tiles_dot(tile_refs, columns, value, sign, store):
-    first = 0
-    for tile_ref in tile_refs:
-        rows = slice(first, first + tile_ref.shape[1])
-        store(rows, tile_dot(tile_ref, columns, value, sign))
-        first = rows.stop
-
-
-def own_pressure_kernel(first_ref, second_ref, value_ref, down_ref, out_ref, weight_ref):
-    half = value_ref.shape[0]
-
-    def store(rows, term):
-        out_ref[rows, :] = term
-
-    tiles_dot((first_ref, second_ref), slice(0, half), value_ref[...], 1, store)
+def own_pressure_kernel(tile_ref, value_ref, down_ref, out_ref, weight_ref):
+    out_ref[...] = tile_dot(tile_ref, slice(0, value_ref.shape[0]), value_ref[...], 1)
     for block in range(weight_ref.shape[0] // lanes):
         weight_ref[block * lanes : (block + 1) * lanes, :] = jnp.broadcast_to(
             down_ref[3, :, block : block + 1], (lanes, lanes)
         )
 
 
-def other_pressure_kernel(first_ref, second_ref, value_ref, term_ref, out_ref):
+def other_pressure_kernel(tile_ref, value_ref, term_ref, out_ref):
     half = value_ref.shape[0]
-
-    def store(rows, term):
-        out_ref[rows, :] = term_ref[rows, :] + term
-
-    tiles_dot((first_ref, second_ref), slice(half, 2 * half), value_ref[...], 1, store)
-
-
-def modal_kernel(first_ref, second_ref, value_ref, weight_ref, own_ref, other_ref, *refs):
-    kept_ref, sent_ref, pressure_ref, sem = refs
+    out_ref[...] = term_ref[...] + tile_dot(tile_ref, slice(half, 2 * half), value_ref[...], 1)
+
+
+def modal_kernel(tile_ref, value_ref, weight_ref, own_ref, other_ref, *refs):
+    kept_ref, sent_ref = refs
     col = lax.axis_index("col")
-    each = pressure_ref.shape[0]
-    block = (lax.axis_index("row") * lax.axis_size("col") + col) // 2
-    rows = pl.ds(pl.multiple_of(block * each, each), each)
-    copy = pltpu.make_async_copy(value_ref.at[rows, :], pressure_ref, sem)
-    copy.start()
     source = (value_ref[...] * weight_ref[...]).astype(jnp.bfloat16)
-    across, turned_across = jnp.transpose(source), jnp.transpose(turned(source, -1))
-    sensitivity = None
-    first = 0
-    for tile_ref in (first_ref, second_ref):
-        targets = slice(first, first + tile_ref.shape[1])
-        first = targets.stop
-        for part, value in enumerate((across, turned_across)):
-            term = jnp.dot(value[:, targets], tile_ref[part], preferred_element_type=jnp.float32)
-            sensitivity = term if sensitivity is None else sensitivity + term
-    sensitivity = sensitivity.astype(jnp.bfloat16)
+    sensitivity = sum(
+        jnp.dot(jnp.transpose(value), tile_ref[part], preferred_element_type=jnp.float32)
+        for part, value in enumerate((source, turned(source, -1)))
+    ).astype(jnp.bfloat16)
     half = own_ref.shape[0]
     modal = jnp.dot(sensitivity[:, :half], own_ref[...], preferred_element_type=jnp.float32)
     modal = modal + jnp.dot(sensitivity[:, half:], other_ref[...], preferred_element_type=jnp.float32)
@@ -401,7 +377,12 @@
     low, high = modal[:modes_each, :], modal[modes_each:, :]
     kept_ref[...] = jnp.where(col % 2 == 0, low, high)
     sent_ref[...] = jnp.where(col % 2 == 0, high, low)
-    copy.wait()
+
+
+def own_rows_kernel(value_ref, out_ref):
+    each = out_ref.shape[0]
+    block = (lax.axis_index("row") * lax.axis_size("col") + lax.axis_index("col")) // 2
+    out_ref[...] = value_ref[pl.ds(pl.multiple_of(block * each, each), each), :]
 
 
 def swap(value, axis, mask):
@@ -413,7 +394,7 @@
     norm_const = math.sqrt(4.0 * math.pi * panels)
     own_rows, load_columns = mode_shapes.shape[0], modal_velocity.shape[1]
     half = 4 * own_rows
-    part_rows = 256 * half // 768
+    part_rows = half // 2
     wide = (panels // lanes, lanes)
     modes, order, coords, areas, weights, terms, sent = load(
         modal_velocity,
@@ -423,44 +404,39 @@
         areas.reshape(wide),
         weights.reshape(wide),
     )
-    received = [swap(sent, "row", mask) for mask in (3, 2, 1)]
+    received = [swap(sent, "row", mask) for mask in (1, 2, 3)]
     tiles = first_tile(order, coords, areas, weights, norm_const, part_rows)
     received, tiles = lax.optimization_barrier((received, tiles))
     tile, columns, down = tiles
     joined = call(
         join_kernel, (((2 * own_rows, load_columns), jnp.bfloat16),) * 4, (), terms, *received, modes
     )
-    received = [swap(value, "col", 2 * mask) for mask, value in zip((1, 2, 3), joined[1:])]
-    last_tile = next_tile(columns, down, part_rows, half - part_rows)
-    received, last_tile = lax.optimization_barrier((received, last_tile))
-    joined = [joined[0], *received]
+    received = [swap(value, "col", 2 * mask) for mask, value in zip((3, 2, 1), joined[:0:-1])]
+    tile = next_tile(columns, down, tile, part_rows)
+    received, tile = lax.optimization_barrier((received, tile))
+    joined = [joined[0], *received[::-1]]
     own = jnp.concatenate([value[:own_rows] for value in joined], 0)
+    modes = jnp.concatenate([value[own_rows:] for value in joined], 0)
     other = swap(own, "col", 1)
+    other_modes = swap(modes, "col", 1)
     out = ((half, load_columns), jnp.float32)
     term, weight = call(
-        own_pressure_kernel, (out, ((half, lanes), jnp.float32)), (), tile, last_tile, own, down
-    )
-    modes = jnp.concatenate([value[own_rows:] for value in joined], 0)
-    modes, term = lax.optimization_barrier((modes, term))
-    other_modes = swap(modes, "col", 1)
-    pressure = call(other_pressure_kernel, (out,), (), tile, last_tile, other, term)[0]
+        own_pressure_kernel, (out, ((half, lanes), jnp.float32)), (), tile, own, down
+    )
+    pressure = call(other_pressure_kernel, (out,), (), tile, other, term)[0]
     modes_each = mode_shapes.shape[1] // 8
-    kept, sent, own_pressure = call(
+    kept, sent = call(
         modal_kernel,
-        (
-            ((modes_each, load_columns), jnp.float32),
-            ((modes_each, load_columns), jnp.float32),
-            ((own_rows // lax.axis_size("row"), load_columns), jnp.float32),
-        ),
-        (pltpu.SemaphoreType.DMA,),
+        (((modes_each, load_columns), jnp.float32),) * 2,
+        (),
         tile,
-        last_tile,
         pressure,
         weight,
         modes,
         other_modes,
-        outs=(whole, whole, remote),
-    )
+    )
+    each = own_rows // lax.axis_size("row")
+    own_pressure = call(own_rows_kernel, (((each, load_columns), jnp.float32),), (), pressure)[0]
     return (own_pressure, kept + swap(sent, "col", 1))
 
 

time: 26.9 us -> 25.4 us (0.944)
  waiting for transfers between devices: 3.95 us -> 2.43 us
  Pallas kernels: 11 us -> 11.3 us
  starting transfers between devices: 10.4 us -> 10.1 us
    ppermute x9, waiting for transfers between devices: 3.95 us -> 2.43 us  [swap(): lax.ppermute(value, axis, [(i, i ^ mask) for i in range(lax.axis_size(axi...]
    pallas_call x7 -> x8, Pallas kernels: 11 us -> 11.3 us  [call(): pl.pallas_call(kernel, out_shape=shapes, in_specs=specs or [whole] * len(...]
  transfers between devices with their start and end apart: 9 -> 9, of which waited for: 4 -> 4; matrix products, arithmetic and copies ran while one was open for 0% -> 0% of each run, Pallas kernels for 31% -> 35%
where the time goes in v5:
time: 25.4 us; the launch traced here: 25.3 us
  Pallas kernels  11.3 us (44%)
  starting transfers between devices  10.1 us (40%)
  waiting for transfers between devices  2.43 us (10%)
  between operations  0.74 us (3%)
  other arithmetic  0.65 us (3%)
    pallas_call x8, Pallas kernels, call(): pl.pallas_call(kernel, out_shape=shapes, in_specs=specs or [whole] * len(...  11.3 us
    ppermute x9, starting transfers between devices, swap(): lax.ppermute(value, axis, [(i, i ^ mask) for i in range(lax.axis_size(axi...  10.1 us
    ppermute x9, waiting for transfers between devices, swap(): lax.ppermute(value, axis, [(i, i ^ mask) for i in range(lax.axis_size(axi...  2.43 us
    add x1, other arithmetic, local(): return (own_pressure, kept + swap(sent, 'col', 1))  0.62 us
  transfers between devices with their start and end apart: 9, of which 4 were waited for; matrix products, arithmetic and copies ran while one was open for 0% of the time, Pallas kernels for 35%

profile of v5, /device:TPU:0, one launch (start us, length us, event | category | flops | bytes accessed | tf_op | source)
XLA Modules:
  0.0 25.3 jit_solution(17717285482217217183)
XLA Ops:
  0.6 1.2 %shard_map.77 = (bf16[192,512]{1,0:T(8,128)(2,1)S(1)}, s32[12,128]{1,0:T(8,128)S(1)}, f32[3,1536]{1,0:T(4,128)S(1)}, f32[12,128]{1,0:T(8,128)S(1)}, f32[12,128]{...) custom-call(bf16[512,128]{1,0:T(8,128)(2,1)} %refs_0_.1, bf16[192,512]{1,0:T(8,128)(2,1)} %refs_1_.1, ...), custom_call_target="tpu_custom_call" | custom-call | tf_op jit(solution)/shard_map/pallas_call | solution.py:115
  1.9 5.1 %collective-permute-start.2 = (bf16[192,128]{1,0:T(8,128)(2,1)S(1)}, bf16[192,128]{1,0:T(8,128)(2,1)S(1)}, u32[]{:S(2)}, u32[]{:S(2)}) collective-permute-start(bf16[192,128]{1,0:T(8,128)(2,1)S(1)} %get-tuple-element.31), channel_id=1, source_target_pairs={{0,24},{8,16},{16,8},{24,0},{1,25},{9,17},{17,9},{25,1},{2,26},{10... | collective-permute-start | bytes 147464 | tf_op jit(solution)/shard_map/ppermute | solution.py:389
  7.0 0.0 collective-permute-start.1
  7.0 0.6 %collective-permute-start = (bf16[192,128]{1,0:T(8,128)(2,1)S(1)}, bf16[192,128]{1,0:T(8,128)(2,1)S(1)}, u32[]{:S(2)}, u32[]{:S(2)}) collective-permute-start(bf16[192,128]{1,0:T(8,128)(2,1)S(1)} %get-tuple-element.31), channel_id=1, source_target_pairs={{0,8},{8,0},{16,24},{24,16},{1,9},{9,1},{17,25},{25,17},{2,10},{10... | collective-permute-start | bytes 147464 | tf_op jit(solution)/shard_map/ppermute | solution.py:389
  7.6 3.6 %shard_map.78 = (bf16[2,768,1536]{2,1,0:T(8,128)(2,1)S(1)}, f32[4,8,1536]{2,1,0:T(8,128)S(1)}, f32[4,128,8]{2,1,0:T(8,128)S(1)}) custom-call(s32[12,128]{1,0:T(8,128)S(1)} %get-tuple-element.32.order_ref, f32[3,1536]{1,0:T(4,128)S(1)} %get-tuple-element.33.coords_ref, f32[12,128]{1,0:T(8,128)S(1)} %get-tuple-element.34.areas_ref, ...), custom_call_target="tpu_custom_call" | custom-call | flops 23592960 | bytes 2359296 | tf_op jit(solution)/shard_map/pallas_call | solution.py:115
  11.2 0.0 collective-permute-done.2.third_ref
  11.2 0.8 %collective-permute-done.1.second_ref = bf16[192,128]{1,0:T(8,128)(2,1)S(1)} collective-permute-done((bf16[192,128]{1,0:T(8,128)(2,1)S(1)}, bf16[192,128]{1,0:T(8,128)(2,1)S(1)}, u32[]{:S(2)}, u32[]{:S(2)}) %collective-permute-start.1) | collective-permute-done | bytes 49184 | tf_op jit(solution)/shard_map/ppermute | solution.py:389
  12.0 0.0 collective-permute-done.first_ref
  12.0 0.1 shard_map.79
  12.1 2.5 %collective-permute-start.3 = (bf16[384,128]{1,0:T(8,128)(2,1)S(1)}, bf16[384,128]{1,0:T(8,128)(2,1)S(1)}, u32[]{:S(2)}, u32[]{:S(2)}) collective-permute-start(bf16[384,128]{1,0:T(8,128)(2,1)S(1)} %get-tuple-element.43), channel_id=1, source_target_pairs={{0,6},{1,7},{2,4},{3,5},{4,2},{5,3},{6,0},{7,1},{8,14},{9,15},{10,... | collective-permute-start | bytes 294920 | tf_op jit(solution)/shard_map/ppermute | solution.py:389
  14.6 0.5 %collective-permute-start.4 = (bf16[384,128]{1,0:T(8,128)(2,1)S(1)}, bf16[384,128]{1,0:T(8,128)(2,1)S(1)}, u32[]{:S(2)}, u32[]{:S(2)}) collective-permute-start(bf16[384,128]{1,0:T(8,128)(2,1)S(1)} %get-tuple-element.44), channel_id=1, source_target_pairs={{0,4},{1,5},{2,6},{3,7},{4,0},{5,1},{6,2},{7,3},{8,12},{9,13},{10,... | collective-permute-start | bytes 294920 | tf_op jit(solution)/shard_map/ppermute | solution.py:389
  15.1 0.5 %collective-permute-start.5 = (bf16[384,128]{1,0:T(8,128)(2,1)S(1)}, bf16[384,128]{1,0:T(8,128)(2,1)S(1)}, u32[]{:S(2)}, u32[]{:S(2)}) collective-permute-start(bf16[384,128]{1,0:T(8,128)(2,1)S(1)} %get-tuple-element.45), channel_id=1, source_target_pairs={{0,2},{1,3},{2,0},{3,1},{4,6},{5,7},{6,4},{7,5},{8,10},{9,11},{10,... | collective-permute-start | bytes 294920 | tf_op jit(solution)/shard_map/ppermute | solution.py:389
  15.6 2.9 %shard_map.80.tile_ref = bf16[2,768,1536]{2,1,0:T(8,128)(2,1)S(1)} custom-call(f32[4,8,1536]{2,1,0:T(8,128)S(1)} %get-tuple-element.46.columns_ref, f32[4,128,8]{2,1,0:T(8,128)S(1)} %get-tuple-element.47.down_ref, bf16[2,768,1536]{2,1,0:T(8,128)(2,1)S(1)} %get-tuple-element.48.filled_ref), custom_call_target="tpu_custom_call", output_to_operand_aliasing={{}: (2, {})} | custom-call | flops 23592960 | bytes 2359296 | tf_op jit(solution)/shard_map/pallas_call | solution.py:115
  18.5 0.0 collective-permute-done.3
  18.5 0.8 %collective-permute-done.4 = bf16[384,128]{1,0:T(8,128)(2,1)S(1)} collective-permute-done((bf16[384,128]{1,0:T(8,128)(2,1)S(1)}, bf16[384,128]{1,0:T(8,128)(2,1)S(1)}, u32[]{:S(2)}, u32[]{:S(2)}) %collective-permute-start.4) | collective-permute-done | bytes 98336 | tf_op jit(solution)/shard_map/ppermute | solution.py:389
  19.3 0.4 %collective-permute-done.5 = bf16[384,128]{1,0:T(8,128)(2,1)S(1)} collective-permute-done((bf16[384,128]{1,0:T(8,128)(2,1)S(1)}, bf16[384,128]{1,0:T(8,128)(2,1)S(1)}, u32[]{:S(2)}, u32[]{:S(2)}) %collective-permute-start.5) | collective-permute-done | bytes 98336 | tf_op jit(solution)/shard_map/ppermute | solution.py:389
  19.7 0.1 collective-permute-start.6
  19.9 0.6 %collective-permute-start.7 = (bf16[768,128]{1,0:T(8,128)(2,1)S(1)}, bf16[768,128]{1,0:T(8,128)(2,1)S(1)}, u32[]{:S(2)}, u32[]{:S(2)}) collective-permute-start(bf16[768,128]{1,0:T(8,128)(2,1)S(1)} %pad_maximum_fusion.1.own_ref), channel_id=1, source_target_pairs={{0,1},{1,0},{2,3},{3,2},{4,5},{5,4},{6,7},{7,6},{8,9},{9,8},{10,11... | collective-permute-start | bytes 589832 | tf_op jit(solution)/shard_map/ppermute | solution.py:389
  20.4 0.8 %shard_map.81 = (f32[768,128]{1,0:T(8,128)S(1)}, f32[768,128]{1,0:T(8,128)S(1)}) custom-call(bf16[2,768,1536]{2,1,0:T(8,128)(2,1)S(1)} %shard_map.80.tile_ref, bf16[768,128]{1,0:T(8,128)(2,1)S(1)} %pad_maximum_fusion.value_ref, f32[4,128,8]{2,1,0:T(8,128)S(1)} %get-tuple-element.47.down_ref), custom_call_target="tpu_custom_call" | custom-call | tf_op jit(solution)/shard_map/pallas_call | solution.py:115
  21.2 0.0 collective-permute-done.6.value_ref
  21.3 0.9 %shard_map.82.value_ref = f32[768,128]{1,0:T(8,128)S(1)} custom-call(bf16[2,768,1536]{2,1,0:T(8,128)(2,1)S(1)} %shard_map.80.tile_ref, bf16[768,128]{1,0:T(8,128)(2,1)S(1)} %collective-permute-done.6.value_ref, f32[768,128]{1,0:T(8,128)S(1)} %get-tuple-element.54.term_ref), custom_call_target="tpu_custom_call" | custom-call | tf_op jit(solution)/shard_map/pallas_call | solution.py:115
  22.1 0.0 collective-permute-done.7.other_ref
  22.2 1.2 %shard_map.84 = (f32[64,128]{1,0:T(8,128)S(1)}, f32[64,128]{1,0:T(8,128)S(1)}) custom-call(bf16[2,768,1536]{2,1,0:T(8,128)(2,1)S(1)} %shard_map.80.tile_ref, f32[768,128]{1,0:T(8,128)S(1)} %shard_map.82.value_ref, f32[768,128]{1,0:T(8,128)S(1)} %get-tuple-element.55.weight_ref, bf16[768,128]{1,0:T(8,128)(2,1)S(1)} %pad_maximum_fusion.1.own_ref, ...), custom_call_target="tpu_custom_call" | custom-call | tf_op jit(solution)/shard_map/pallas_call | solution.py:115
  23.4 0.2 collective-permute-start.8
  23.6 0.6 %shard_map.83 = f32[48,128]{1,0:T(8,128)} custom-call(f32[768,128]{1,0:T(8,128)S(1)} %shard_map.82.value_ref), custom_call_target="tpu_custom_call" | custom-call | tf_op jit(solution)/shard_map/pallas_call | solution.py:115
  24.2 0.5 %collective-permute-done.8 = f32[64,128]{1,0:T(8,128)S(1)} collective-permute-done((f32[64,128]{1,0:T(8,128)S(1)}, f32[64,128]{1,0:T(8,128)S(1)}, u32[]{:S(2)}, u32[]{:S(2)}) %collective-permute-start.8) | collective-permute-done | bytes 32800 | tf_op jit(solution)/shard_map/ppermute | solution.py:389
  24.7 0.6 %add.3 = f32[64,128]{1,0:T(8,128)} add(f32[64,128]{1,0:T(8,128)S(1)} %get-tuple-element.56, f32[64,128]{1,0:T(8,128)S(1)} %collective-permute-done.8) | non-fusion elementwise | flops 8192 | bytes 98304 | tf_op jit(solution)/shard_map/add | solution.py:440
  (5 shorter events, 0.1 us)
Async XLA Ops:
  1.9 9.3 %collective-permute-start.2 = (bf16[192,128]{1,0:T(8,128)(2,1)S(1)}, bf16[192,128]{1,0:T(8,128)(2,1)S(1)}, u32[]{:S(2)}, u32[]{:S(2)}) collective-permute-start(bf16[192,128]{1,0:T(8,128)(2,1)S(1)} %get-tuple-element.31), channel_id=1, source_target_pairs={{0,24},{8,16},{16,8},{24,0},{1,25},{9,17},{17,9},{25,1},{2,26},{10... | collective-permute-start | bytes 147464 | tf_op jit(solution)/shard_map/ppermute | solution.py:389
  7.0 5.0 %collective-permute-start.1 = (bf16[192,128]{1,0:T(8,128)(2,1)S(1)}, bf16[192,128]{1,0:T(8,128)(2,1)S(1)}, u32[]{:S(2)}, u32[]{:S(2)}) collective-permute-start(bf16[192,128]{1,0:T(8,128)(2,1)S(1)} %get-tuple-element.31), channel_id=1, source_target_pairs={{0,16},{8,24},{16,0},{24,8},{1,17},{9,25},{17,1},{25,9},{2,18},{10... | collective-permute-start | bytes 147464 | tf_op jit(solution)/shard_map/ppermute | solution.py:389
  7.0 5.0 %collective-permute-start = (bf16[192,128]{1,0:T(8,128)(2,1)S(1)}, bf16[192,128]{1,0:T(8,128)(2,1)S(1)}, u32[]{:S(2)}, u32[]{:S(2)}) collective-permute-start(bf16[192,128]{1,0:T(8,128)(2,1)S(1)} %get-tuple-element.31), channel_id=1, source_target_pairs={{0,8},{8,0},{16,24},{24,16},{1,9},{9,1},{17,25},{25,17},{2,10},{10... | collective-permute-start | bytes 147464 | tf_op jit(solution)/shard_map/ppermute | solution.py:389
  12.1 6.5 %collective-permute-start.3 = (bf16[384,128]{1,0:T(8,128)(2,1)S(1)}, bf16[384,128]{1,0:T(8,128)(2,1)S(1)}, u32[]{:S(2)}, u32[]{:S(2)}) collective-permute-start(bf16[384,128]{1,0:T(8,128)(2,1)S(1)} %get-tuple-element.43), channel_id=1, source_target_pairs={{0,6},{1,7},{2,4},{3,5},{4,2},{5,3},{6,0},{7,1},{8,14},{9,15},{10,... | collective-permute-start | bytes 294920 | tf_op jit(solution)/shard_map/ppermute | solution.py:389
  14.6 4.7 %collective-permute-start.4 = (bf16[384,128]{1,0:T(8,128)(2,1)S(1)}, bf16[384,128]{1,0:T(8,128)(2,1)S(1)}, u32[]{:S(2)}, u32[]{:S(2)}) collective-permute-start(bf16[384,128]{1,0:T(8,128)(2,1)S(1)} %get-tuple-element.44), channel_id=1, source_target_pairs={{0,4},{1,5},{2,6},{3,7},{4,0},{5,1},{6,2},{7,3},{8,12},{9,13},{10,... | collective-permute-start | bytes 294920 | tf_op jit(solution)/shard_map/ppermute | solution.py:389
  15.1 4.6 %collective-permute-start.5 = (bf16[384,128]{1,0:T(8,128)(2,1)S(1)}, bf16[384,128]{1,0:T(8,128)(2,1)S(1)}, u32[]{:S(2)}, u32[]{:S(2)}) collective-permute-start(bf16[384,128]{1,0:T(8,128)(2,1)S(1)} %get-tuple-element.45), channel_id=1, source_target_pairs={{0,2},{1,3},{2,0},{3,1},{4,6},{5,7},{6,4},{7,5},{8,10},{9,11},{10,... | collective-permute-start | bytes 294920 | tf_op jit(solution)/shard_map/ppermute | solution.py:389
  19.7 1.5 %collective-permute-start.6 = (bf16[768,128]{1,0:T(8,128)(2,1)S(1)}, bf16[768,128]{1,0:T(8,128)(2,1)S(1)}, u32[]{:S(2)}, u32[]{:S(2)}) collective-permute-start(bf16[768,128]{1,0:T(8,128)(2,1)S(1)} %pad_maximum_fusion.value_ref), channel_id=1, source_target_pairs={{0,1},{1,0},{2,3},{3,2},{4,5},{5,4},{6,7},{7,6},{8,9},{9,8},{10,11... | collective-permute-start | bytes 589832 | tf_op jit(solution)/shard_map/ppermute | solution.py:389
  19.9 2.3 %collective-permute-start.7 = (bf16[768,128]{1,0:T(8,128)(2,1)S(1)}, bf16[768,128]{1,0:T(8,128)(2,1)S(1)}, u32[]{:S(2)}, u32[]{:S(2)}) collective-permute-start(bf16[768,128]{1,0:T(8,128)(2,1)S(1)} %pad_maximum_fusion.1.own_ref), channel_id=1, source_target_pairs={{0,1},{1,0},{2,3},{3,2},{4,5},{5,4},{6,7},{7,6},{8,9},{9,8},{10,11... | collective-permute-start | bytes 589832 | tf_op jit(solution)/shard_map/ppermute | solution.py:389
  23.4 1.3 %collective-permute-start.8 = (f32[64,128]{1,0:T(8,128)S(1)}, f32[64,128]{1,0:T(8,128)S(1)}, u32[]{:S(2)}, u32[]{:S(2)}) collective-permute-start(f32[64,128]{1,0:T(8,128)S(1)} %get-tuple-element.57), channel_id=1, source_target_pairs={{0,1},{1,0},{2,3},{3,2},{4,5},{5,4},{6,7},{7,6},{8,9},{9,8},{10,11... | collective-permute-start | bytes 98312 | tf_op jit(solution)/shard_map/ppermute | solution.py:389

commit v6 on v5

--- a/solution.py
+++ b/solution.py
@@ -404,17 +404,17 @@
         areas.reshape(wide),
         weights.reshape(wide),
     )
-    received = [swap(sent, "row", mask) for mask in (1, 2, 3)]
+    received = [swap(sent, "row", mask) for mask in (1, 3, 2)]
     tiles = first_tile(order, coords, areas, weights, norm_const, part_rows)
     received, tiles = lax.optimization_barrier((received, tiles))
     tile, columns, down = tiles
     joined = call(
         join_kernel, (((2 * own_rows, load_columns), jnp.bfloat16),) * 4, (), terms, *received, modes
     )
-    received = [swap(value, "col", 2 * mask) for mask, value in zip((3, 2, 1), joined[:0:-1])]
+    received = [swap(value, "col", 2 * mask) for mask, value in zip((3, 1, 2), (joined[3], joined[1], joined[2]))]
     tile = next_tile(columns, down, tile, part_rows)
     received, tile = lax.optimization_barrier((received, tile))
-    joined = [joined[0], *received[::-1]]
+    joined = [joined[0], received[1], received[2], received[0]]
     own = jnp.concatenate([value[:own_rows] for value in joined], 0)
     modes = jnp.concatenate([value[own_rows:] for value in joined], 0)
     other = swap(own, "col", 1)

time: 25.4 us -> 25.4 us (level)
  no operation moved by 1% of the time
where the time goes in v6:
time: 25.4 us; the launch traced here: 25.3 us
  Pallas kernels  11.3 us (44%)
  starting transfers between devices  10.1 us (40%)
  waiting for transfers between devices  2.49 us (10%)
  between operations  0.74 us (3%)
  other arithmetic  0.65 us (3%)
    pallas_call x8, Pallas kernels, call(): pl.pallas_call(kernel, out_shape=shapes, in_specs=specs or [whole] * len(...  11.3 us
    ppermute x9, starting transfers between devices, swap(): lax.ppermute(value, axis, [(i, i ^ mask) for i in range(lax.axis_size(axi...  10.1 us
    ppermute x9, waiting for transfers between devices, swap(): lax.ppermute(value, axis, [(i, i ^ mask) for i in range(lax.axis_size(axi...  2.49 us
    add x1, other arithmetic, local(): return (own_pressure, kept + swap(sent, 'col', 1))  0.62 us
  transfers between devices with their start and end apart: 9, of which 4 were waited for; matrix products, arithmetic and copies ran while one was open for 0% of the time, Pallas kernels for 35%

profile of v6, /device:TPU:0, one launch (start us, length us, event | category | flops | bytes accessed | tf_op | source)
XLA Modules:
  0.0 25.3 jit_solution(13413130431134442091)
XLA Ops:
  0.6 1.2 %shard_map.77 = (bf16[192,512]{1,0:T(8,128)(2,1)S(1)}, s32[12,128]{1,0:T(8,128)S(1)}, f32[3,1536]{1,0:T(4,128)S(1)}, f32[12,128]{1,0:T(8,128)S(1)}, f32[12,128]{...) custom-call(bf16[512,128]{1,0:T(8,128)(2,1)} %refs_0_.1, bf16[192,512]{1,0:T(8,128)(2,1)} %refs_1_.1, ...), custom_call_target="tpu_custom_call" | custom-call | tf_op jit(solution)/shard_map/pallas_call | solution.py:115
  1.9 4.1 %collective-permute-start.2 = (bf16[192,128]{1,0:T(8,128)(2,1)S(1)}, bf16[192,128]{1,0:T(8,128)(2,1)S(1)}, u32[]{:S(2)}, u32[]{:S(2)}) collective-permute-start(bf16[192,128]{1,0:T(8,128)(2,1)S(1)} %get-tuple-element.31), channel_id=1, source_target_pairs={{0,16},{8,24},{16,0},{24,8},{1,17},{9,25},{17,1},{25,9},{2,18},{10... | collective-permute-start | bytes 147464 | tf_op jit(solution)/shard_map/ppermute | solution.py:389
  6.0 1.3 %collective-permute-start.1 = (bf16[192,128]{1,0:T(8,128)(2,1)S(1)}, bf16[192,128]{1,0:T(8,128)(2,1)S(1)}, u32[]{:S(2)}, u32[]{:S(2)}) collective-permute-start(bf16[192,128]{1,0:T(8,128)(2,1)S(1)} %get-tuple-element.31), channel_id=1, source_target_pairs={{0,24},{8,16},{16,8},{24,0},{1,25},{9,17},{17,9},{25,1},{2,26},{10... | collective-permute-start | bytes 147464 | tf_op jit(solution)/shard_map/ppermute | solution.py:389
  7.3 0.2 collective-permute-start
  7.6 3.6 %shard_map.78 = (bf16[2,768,1536]{2,1,0:T(8,128)(2,1)S(1)}, f32[4,8,1536]{2,1,0:T(8,128)S(1)}, f32[4,128,8]{2,1,0:T(8,128)S(1)}) custom-call(s32[12,128]{1,0:T(8,128)S(1)} %get-tuple-element.32.order_ref, f32[3,1536]{1,0:T(4,128)S(1)} %get-tuple-element.33.coords_ref, f32[12,128]{1,0:T(8,128)S(1)} %get-tuple-element.34.areas_ref, ...), custom_call_target="tpu_custom_call" | custom-call | flops 23592960 | bytes 2359296 | tf_op jit(solution)/shard_map/pallas_call | solution.py:115
  11.1 0.0 collective-permute-done.2.third_ref
  11.1 0.8 %collective-permute-done.1.second_ref = bf16[192,128]{1,0:T(8,128)(2,1)S(1)} collective-permute-done((bf16[192,128]{1,0:T(8,128)(2,1)S(1)}, bf16[192,128]{1,0:T(8,128)(2,1)S(1)}, u32[]{:S(2)}, u32[]{:S(2)}) %collective-permute-start.1) | collective-permute-done | bytes 49184 | tf_op jit(solution)/shard_map/ppermute | solution.py:389
  12.0 0.0 collective-permute-done.first_ref
  12.0 0.1 shard_map.79
  12.0 2.5 %collective-permute-start.3 = (bf16[384,128]{1,0:T(8,128)(2,1)S(1)}, bf16[384,128]{1,0:T(8,128)(2,1)S(1)}, u32[]{:S(2)}, u32[]{:S(2)}) collective-permute-start(bf16[384,128]{1,0:T(8,128)(2,1)S(1)} %get-tuple-element.43), channel_id=1, source_target_pairs={{0,6},{1,7},{2,4},{3,5},{4,2},{5,3},{6,0},{7,1},{8,14},{9,15},{10,... | collective-permute-start | bytes 294920 | tf_op jit(solution)/shard_map/ppermute | solution.py:389
  14.5 0.5 %collective-permute-start.4 = (bf16[384,128]{1,0:T(8,128)(2,1)S(1)}, bf16[384,128]{1,0:T(8,128)(2,1)S(1)}, u32[]{:S(2)}, u32[]{:S(2)}) collective-permute-start(bf16[384,128]{1,0:T(8,128)(2,1)S(1)} %get-tuple-element.44), channel_id=1, source_target_pairs={{0,2},{1,3},{2,0},{3,1},{4,6},{5,7},{6,4},{7,5},{8,10},{9,11},{10,... | collective-permute-start | bytes 294920 | tf_op jit(solution)/shard_map/ppermute | solution.py:389
  15.1 0.5 %collective-permute-start.5 = (bf16[384,128]{1,0:T(8,128)(2,1)S(1)}, bf16[384,128]{1,0:T(8,128)(2,1)S(1)}, u32[]{:S(2)}, u32[]{:S(2)}) collective-permute-start(bf16[384,128]{1,0:T(8,128)(2,1)S(1)} %get-tuple-element.45), channel_id=1, source_target_pairs={{0,4},{1,5},{2,6},{3,7},{4,0},{5,1},{6,2},{7,3},{8,12},{9,13},{10,... | collective-permute-start | bytes 294920 | tf_op jit(solution)/shard_map/ppermute | solution.py:389
  15.6 2.9 %shard_map.80.tile_ref = bf16[2,768,1536]{2,1,0:T(8,128)(2,1)S(1)} custom-call(f32[4,8,1536]{2,1,0:T(8,128)S(1)} %get-tuple-element.46.columns_ref, f32[4,128,8]{2,1,0:T(8,128)S(1)} %get-tuple-element.47.down_ref, bf16[2,768,1536]{2,1,0:T(8,128)(2,1)S(1)} %get-tuple-element.48.filled_ref), custom_call_target="tpu_custom_call", output_to_operand_aliasing={{}: (2, {})} | custom-call | flops 23592960 | bytes 2359296 | tf_op jit(solution)/shard_map/pallas_call | solution.py:115
  18.5 0.0 collective-permute-done.3
  18.5 0.7 %collective-permute-done.4 = bf16[384,128]{1,0:T(8,128)(2,1)S(1)} collective-permute-done((bf16[384,128]{1,0:T(8,128)(2,1)S(1)}, bf16[384,128]{1,0:T(8,128)(2,1)S(1)}, u32[]{:S(2)}, u32[]{:S(2)}) %collective-permute-start.4) | collective-permute-done | bytes 98336 | tf_op jit(solution)/shard_map/ppermute | solution.py:389
  19.1 0.5 %collective-permute-done.5 = bf16[384,128]{1,0:T(8,128)(2,1)S(1)} collective-permute-done((bf16[384,128]{1,0:T(8,128)(2,1)S(1)}, bf16[384,128]{1,0:T(8,128)(2,1)S(1)}, u32[]{:S(2)}, u32[]{:S(2)}) %collective-permute-start.5) | collective-permute-done | bytes 98336 | tf_op jit(solution)/shard_map/ppermute | solution.py:389
  19.7 0.1 collective-permute-start.6
  19.8 0.6 %collective-permute-start.7 = (bf16[768,128]{1,0:T(8,128)(2,1)S(1)}, bf16[768,128]{1,0:T(8,128)(2,1)S(1)}, u32[]{:S(2)}, u32[]{:S(2)}) collective-permute-start(bf16[768,128]{1,0:T(8,128)(2,1)S(1)} %pad_maximum_fusion.1.own_ref), channel_id=1, source_target_pairs={{0,1},{1,0},{2,3},{3,2},{4,5},{5,4},{6,7},{7,6},{8,9},{9,8},{10,11... | collective-permute-start | bytes 589832 | tf_op jit(solution)/shard_map/ppermute | solution.py:389
  20.4 0.8 %shard_map.81 = (f32[768,128]{1,0:T(8,128)S(1)}, f32[768,128]{1,0:T(8,128)S(1)}) custom-call(bf16[2,768,1536]{2,1,0:T(8,128)(2,1)S(1)} %shard_map.80.tile_ref, bf16[768,128]{1,0:T(8,128)(2,1)S(1)} %pad_maximum_fusion.value_ref, f32[4,128,8]{2,1,0:T(8,128)S(1)} %get-tuple-element.47.down_ref), custom_call_target="tpu_custom_call" | custom-call | tf_op jit(solution)/shard_map/pallas_call | solution.py:115
  21.2 0.0 collective-permute-done.6.value_ref
  21.2 0.9 %shard_map.82.value_ref = f32[768,128]{1,0:T(8,128)S(1)} custom-call(bf16[2,768,1536]{2,1,0:T(8,128)(2,1)S(1)} %shard_map.80.tile_ref, bf16[768,128]{1,0:T(8,128)(2,1)S(1)} %collective-permute-done.6.value_ref, f32[768,128]{1,0:T(8,128)S(1)} %get-tuple-element.54.term_ref), custom_call_target="tpu_custom_call" | custom-call | tf_op jit(solution)/shard_map/pallas_call | solution.py:115
  22.1 0.0 collective-permute-done.7.other_ref
  22.1 1.2 %shard_map.84 = (f32[64,128]{1,0:T(8,128)S(1)}, f32[64,128]{1,0:T(8,128)S(1)}) custom-call(bf16[2,768,1536]{2,1,0:T(8,128)(2,1)S(1)} %shard_map.80.tile_ref, f32[768,128]{1,0:T(8,128)S(1)} %shard_map.82.value_ref, f32[768,128]{1,0:T(8,128)S(1)} %get-tuple-element.55.weight_ref, bf16[768,128]{1,0:T(8,128)(2,1)S(1)} %pad_maximum_fusion.1.own_ref, ...), custom_call_target="tpu_custom_call" | custom-call | tf_op jit(solution)/shard_map/pallas_call | solution.py:115
  23.4 0.2 collective-permute-start.8
  23.6 0.6 %shard_map.83 = f32[48,128]{1,0:T(8,128)} custom-call(f32[768,128]{1,0:T(8,128)S(1)} %shard_map.82.value_ref), custom_call_target="tpu_custom_call" | custom-call | tf_op jit(solution)/shard_map/pallas_call | solution.py:115
  24.2 0.5 %collective-permute-done.8 = f32[64,128]{1,0:T(8,128)S(1)} collective-permute-done((f32[64,128]{1,0:T(8,128)S(1)}, f32[64,128]{1,0:T(8,128)S(1)}, u32[]{:S(2)}, u32[]{:S(2)}) %collective-permute-start.8) | collective-permute-done | bytes 32800 | tf_op jit(solution)/shard_map/ppermute | solution.py:389
  24.7 0.6 %add.3 = f32[64,128]{1,0:T(8,128)} add(f32[64,128]{1,0:T(8,128)S(1)} %get-tuple-element.56, f32[64,128]{1,0:T(8,128)S(1)} %collective-permute-done.8) | non-fusion elementwise | flops 8192 | bytes 98304 | tf_op jit(solution)/shard_map/add | solution.py:440
  (5 shorter events, 0.1 us)
Async XLA Ops:
  1.9 9.3 %collective-permute-start.2 = (bf16[192,128]{1,0:T(8,128)(2,1)S(1)}, bf16[192,128]{1,0:T(8,128)(2,1)S(1)}, u32[]{:S(2)}, u32[]{:S(2)}) collective-permute-start(bf16[192,128]{1,0:T(8,128)(2,1)S(1)} %get-tuple-element.31), channel_id=1, source_target_pairs={{0,16},{8,24},{16,0},{24,8},{1,17},{9,25},{17,1},{25,9},{2,18},{10... | collective-permute-start | bytes 147464 | tf_op jit(solution)/shard_map/ppermute | solution.py:389
  6.0 6.0 %collective-permute-start.1 = (bf16[192,128]{1,0:T(8,128)(2,1)S(1)}, bf16[192,128]{1,0:T(8,128)(2,1)S(1)}, u32[]{:S(2)}, u32[]{:S(2)}) collective-permute-start(bf16[192,128]{1,0:T(8,128)(2,1)S(1)} %get-tuple-element.31), channel_id=1, source_target_pairs={{0,24},{8,16},{16,8},{24,0},{1,25},{9,17},{17,9},{25,1},{2,26},{10... | collective-permute-start | bytes 147464 | tf_op jit(solution)/shard_map/ppermute | solution.py:389
  7.3 4.6 %collective-permute-start = (bf16[192,128]{1,0:T(8,128)(2,1)S(1)}, bf16[192,128]{1,0:T(8,128)(2,1)S(1)}, u32[]{:S(2)}, u32[]{:S(2)}) collective-permute-start(bf16[192,128]{1,0:T(8,128)(2,1)S(1)} %get-tuple-element.31), channel_id=1, source_target_pairs={{0,8},{8,0},{16,24},{24,16},{1,9},{9,1},{17,25},{25,17},{2,10},{10... | collective-permute-start | bytes 147464 | tf_op jit(solution)/shard_map/ppermute | solution.py:389
  12.0 6.5 %collective-permute-start.3 = (bf16[384,128]{1,0:T(8,128)(2,1)S(1)}, bf16[384,128]{1,0:T(8,128)(2,1)S(1)}, u32[]{:S(2)}, u32[]{:S(2)}) collective-permute-start(bf16[384,128]{1,0:T(8,128)(2,1)S(1)} %get-tuple-element.43), channel_id=1, source_target_pairs={{0,6},{1,7},{2,4},{3,5},{4,2},{5,3},{6,0},{7,1},{8,14},{9,15},{10,... | collective-permute-start | bytes 294920 | tf_op jit(solution)/shard_map/ppermute | solution.py:389
  14.5 4.6 %collective-permute-start.4 = (bf16[384,128]{1,0:T(8,128)(2,1)S(1)}, bf16[384,128]{1,0:T(8,128)(2,1)S(1)}, u32[]{:S(2)}, u32[]{:S(2)}) collective-permute-start(bf16[384,128]{1,0:T(8,128)(2,1)S(1)} %get-tuple-element.44), channel_id=1, source_target_pairs={{0,2},{1,3},{2,0},{3,1},{4,6},{5,7},{6,4},{7,5},{8,10},{9,11},{10,... | collective-permute-start | bytes 294920 | tf_op jit(solution)/shard_map/ppermute | solution.py:389
  15.1 4.6 %collective-permute-start.5 = (bf16[384,128]{1,0:T(8,128)(2,1)S(1)}, bf16[384,128]{1,0:T(8,128)(2,1)S(1)}, u32[]{:S(2)}, u32[]{:S(2)}) collective-permute-start(bf16[384,128]{1,0:T(8,128)(2,1)S(1)} %get-tuple-element.45), channel_id=1, source_target_pairs={{0,4},{1,5},{2,6},{3,7},{4,0},{5,1},{6,2},{7,3},{8,12},{9,13},{10,... | collective-permute-start | bytes 294920 | tf_op jit(solution)/shard_map/ppermute | solution.py:389
  19.7 1.5 %collective-permute-start.6 = (bf16[768,128]{1,0:T(8,128)(2,1)S(1)}, bf16[768,128]{1,0:T(8,128)(2,1)S(1)}, u32[]{:S(2)}, u32[]{:S(2)}) collective-permute-start(bf16[768,128]{1,0:T(8,128)(2,1)S(1)} %pad_maximum_fusion.value_ref), channel_id=1, source_target_pairs={{0,1},{1,0},{2,3},{3,2},{4,5},{5,4},{6,7},{7,6},{8,9},{9,8},{10,11... | collective-permute-start | bytes 589832 | tf_op jit(solution)/shard_map/ppermute | solution.py:389
  19.8 2.3 %collective-permute-start.7 = (bf16[768,128]{1,0:T(8,128)(2,1)S(1)}, bf16[768,128]{1,0:T(8,128)(2,1)S(1)}, u32[]{:S(2)}, u32[]{:S(2)}) collective-permute-start(bf16[768,128]{1,0:T(8,128)(2,1)S(1)} %pad_maximum_fusion.1.own_ref), channel_id=1, source_target_pairs={{0,1},{1,0},{2,3},{3,2},{4,5},{5,4},{6,7},{7,6},{8,9},{9,8},{10,11... | collective-permute-start | bytes 589832 | tf_op jit(solution)/shard_map/ppermute | solution.py:389
  23.4 1.3 %collective-permute-start.8 = (f32[64,128]{1,0:T(8,128)S(1)}, f32[64,128]{1,0:T(8,128)S(1)}, u32[]{:S(2)}, u32[]{:S(2)}) collective-permute-start(f32[64,128]{1,0:T(8,128)S(1)} %get-tuple-element.57), channel_id=1, source_target_pairs={{0,1},{1,0},{2,3},{3,2},{4,5},{5,4},{6,7},{7,6},{8,9},{9,8},{10,11... | collective-permute-start | bytes 98312 | tf_op jit(solution)/shard_map/ppermute | solution.py:389
